TPU v7x, 32 devices: a whole 2x2x4 slice. The times are simulated.
32 devices in a mesh: expert: 4 (over y, x), shard: 8 (over z, core).
Axes of the slice: x: 2, y: 2, z: 4, core: 2. Of those that a mesh axis runs over, the one named last changes fastest.
Arguments:
- tokens_in: bfloat16 [32768, 768], P(('expert', 'shard')), may hold values from -6 to 6
- cotangent: bfloat16 [32768, 768], P(('expert', 'shard'))
- routes: int32 [32768, 2], P(('expert', 'shard')), may hold values from 0 to 3, all different within a row
- prefix: int32 [32], P(('expert', 'shard')), may hold values from 102 to 512
- owners: int32 [48], replicated, may hold values from 0 to 3, as said below
- attn_master: float32 [96, 384, 128], P('expert', 'shard')
- attn_first: float32 [96, 384, 128], P('expert', 'shard')
- attn_second: float32 [96, 384, 128], P('expert', 'shard')
- expert_master: float32 [4, 3, 12288, 128], P('expert', None, 'shard')
- expert_first: float32 [4, 3, 12288, 128], P('expert', None, 'shard')
- expert_second: float32 [4, 3, 12288, 128], P('expert', None, 'shard')
- shared_master: float32 [3, 12288, 128], P(None, ('expert', 'shard'))
- shared_first: float32 [3, 12288, 128], P(None, ('expert', 'shard'))
- shared_second: float32 [3, 12288, 128], P(None, ('expert', 'shard'))
- norm_gains: float32 [2, 768], replicated, may hold values from 0.5 to 1.5
- gains_first: float32 [2, 768], replicated
- gains_second: float32 [2, 768], replicated
- router: float32 [768, 4], replicated, may hold values from -0.15625 to 0.15625
- router_first: float32 [768, 4], replicated
- router_second: float32 [768, 4], replicated
Outputs:
- block_out: bfloat16 [32768, 768], P(('expert', 'shard'))
- tokens_grad: float32 [32768, 768], P(('expert', 'shard'))
- attn_new: float32 [96, 384, 128], P('expert', 'shard')
- attn_first_new: float32 [96, 384, 128], P('expert', 'shard')
- attn_second_new: float32 [96, 384, 128], P('expert', 'shard')
- attn_copy: bfloat16 [48, 384, 128], P(None, 'shard')
- expert_new: float32 [4, 3, 12288, 128], P('expert', None, 'shard')
- expert_first_new: float32 [4, 3, 12288, 128], P('expert', None, 'shard')
- expert_second_new: float32 [4, 3, 12288, 128], P('expert', None, 'shard')
- shared_new: float32 [3, 12288, 128], P(None, ('expert', 'shard'))
- shared_first_new: float32 [3, 12288, 128], P(None, ('expert', 'shard'))
- shared_second_new: float32 [3, 12288, 128], P(None, ('expert', 'shard'))
- gains_new: float32 [2, 768], replicated
- gains_first_new: float32 [2, 768], replicated
- gains_second_new: float32 [2, 768], replicated
- router_new: float32 [768, 4], replicated
- router_first_new: float32 [768, 4], replicated
- router_second_new: float32 [768, 4], replicated
Inputs may be any that keep to these rules, and one draw needn't show every extreme that they name: `owners`: no owner holds more than 24 attention matrices, and one holds exactly 24. `routes`: the 2 experts of a token differ.
All inputs are finite; a program needn't handle non-finite values.
Results may differ from a plain program's by a relative error of at most 0.018.
Values may be sent and summed in bfloat16 or wider, within the bound.
No kernel may reach another device: no remote copies, remote signals or barrier semaphores. Data moves between devices by JAX's collectives and lax.ppermute only.
A program may use at most 384 MiB of HBM per device.

v0:
```python
import jax
import jax.numpy as jnp
from jax import lax
from jax.sharding import PartitionSpec as P

HEADS = 12
HEAD_DIM = 64
FF = 2048
FFS = 2048
SEQ_LEN = 1024
STEP = 5


NORM_EPSILON = 1e-06
ADAM_EPSILON = 1e-08
FIRST_BETA = 0.5
SECOND_BETA = 0.5
WEIGHT_DECAY = 0.1
RATE_ATTENTION = 0.06
RATE_MATRIX = 0.03
RATE_ROUTER = 0.02
RATE_GAIN = 0.3
ROPE_BASE = 10000.0


def slot_place(owners, own_count, owner_count):
    onehot = (owners[:, None] == jnp.arange(owner_count, dtype=jnp.int32)[None, :]).astype(
        jnp.int32
    )
    prior_count = jnp.sum((jnp.cumsum(onehot, 0) - onehot) * onehot, 1)
    return owners * own_count + prior_count


def rope_tables(length, head_dim):
    half_dim = head_dim // 2
    inv_freq = ROPE_BASE ** (-(jnp.arange(half_dim, dtype=jnp.float32) * 2.0 / head_dim))
    phase_angle = jnp.arange(length, dtype=jnp.float32)[:, None] * inv_freq[None, :]
    return (jnp.cos(phase_angle), jnp.sin(phase_angle))


def rotate(values, cos_part, sin_part):
    half_dim = values.shape[-1] // 2
    lead_half = values[..., :half_dim]
    tail_half = values[..., half_dim:]
    cos_wide = cos_part[:, None, :]
    sin_wide = sin_part[:, None, :]
    return jnp.concatenate(
        [lead_half * cos_wide - tail_half * sin_wide, tail_half * cos_wide + lead_half * sin_wide],
        -1,
    )


def unrotate(gradient, cos_part, sin_part):
    half_dim = gradient.shape[-1] // 2
    lead_half = gradient[..., :half_dim]
    tail_half = gradient[..., half_dim:]
    cos_wide = cos_part[:, None, :]
    sin_wide = sin_part[:, None, :]
    return jnp.concatenate(
        [lead_half * cos_wide + tail_half * sin_wide, tail_half * cos_wide - lead_half * sin_wide],
        -1,
    )


def visible(row_start, row_count, length, prefix_len):
    query_pos = row_start + jnp.arange(row_count, dtype=jnp.int32)
    key_pos = jnp.arange(length, dtype=jnp.int32)
    return (key_pos[None, :] <= query_pos[:, None]) | (key_pos[None, :] < prefix_len)


def rms_scale(values):
    return lax.rsqrt(jnp.mean(values * values, -1, keepdims=True) + NORM_EPSILON)


def norm_back(grad_normed, hat_values, rms_values, gain):
    grad_hat = grad_normed * gain
    return rms_values * (grad_hat - hat_values * jnp.mean(grad_hat * hat_values, -1, keepdims=True))


def adam_update(weight, first_state, second_state, gradient, step_rate, decay_rate):
    first_new = FIRST_BETA * first_state + (1.0 - FIRST_BETA) * gradient
    second_new = SECOND_BETA * second_state + (1.0 - SECOND_BETA) * gradient * gradient
    first_hat = first_new / (1.0 - FIRST_BETA**STEP)
    second_hat = second_new / (1.0 - SECOND_BETA**STEP)
    weight_new = weight - step_rate * (
        first_hat / (jnp.sqrt(second_hat) + ADAM_EPSILON) + decay_rate * weight
    )
    return (weight_new, first_new, second_new)


def masked_scores(query_block, key_rot, row_start, prefix_len, score_scale):
    length = key_rot.shape[0]
    scores = (
        jnp.einsum("qhd,khd->hqk", query_block, key_rot, preferred_element_type=jnp.float32)
        * score_scale
    )
    allowed = visible(row_start, query_block.shape[0], length, prefix_len)
    return jnp.where(allowed[None], scores, -1e30)


def attend_forward(query_rot, key_rot, value_rows, prefix_len, block_rows, score_scale):
    length = key_rot.shape[0]
    outputs = []
    totals = []
    for row_start in range(0, length, block_rows):
        query_block = query_rot[row_start : row_start + block_rows]
        scores = masked_scores(query_block, key_rot, row_start, prefix_len, score_scale)
        row_peak = jnp.max(scores, -1, keepdims=True)
        exp_scores = jnp.exp(scores - row_peak)
        row_total = jnp.sum(exp_scores, -1, keepdims=True)
        prob_block = (exp_scores / row_total).astype(jnp.bfloat16)
        outputs.append(
            jnp.einsum(
                "hqk,khd->qhd", prob_block, value_rows, preferred_element_type=jnp.float32
            ).astype(jnp.bfloat16)
        )
        totals.append((row_peak + jnp.log(row_total))[..., 0])
    return (jnp.concatenate(outputs, 0), jnp.concatenate(totals, 1))


def attend_backward(
    query_rot, key_rot, value_rows, grad_heads, log_totals, prefix_len, block_rows, score_scale
):
    length = key_rot.shape[0]
    grad_query = []
    grad_key = jnp.zeros(key_rot.shape, jnp.float32)
    grad_value = jnp.zeros(value_rows.shape, jnp.float32)
    for row_start in range(0, length, block_rows):
        query_block = query_rot[row_start : row_start + block_rows]
        grad_block = grad_heads[row_start : row_start + block_rows]
        scores = masked_scores(query_block, key_rot, row_start, prefix_len, score_scale)
        prob_block = jnp.exp(scores - log_totals[:, row_start : row_start + block_rows, None])
        grad_probs = jnp.einsum(
            "qhd,khd->hqk", grad_block, value_rows, preferred_element_type=jnp.float32
        )
        center = jnp.sum(prob_block * grad_probs, -1, keepdims=True)
        grad_scores = (prob_block * (grad_probs - center)).astype(jnp.bfloat16)
        grad_query.append(
            jnp.einsum("hqk,khd->qhd", grad_scores, key_rot, preferred_element_type=jnp.float32)
            * score_scale
        )
        grad_key = (
            grad_key
            + jnp.einsum(
                "hqk,qhd->khd", grad_scores, query_block, preferred_element_type=jnp.float32
            )
            * score_scale
        )
        grad_value = grad_value + jnp.einsum(
            "hqk,qhd->khd",
            prob_block.astype(jnp.bfloat16),
            grad_block,
            preferred_element_type=jnp.float32,
        )
    return (jnp.concatenate(grad_query, 0), grad_key, grad_value)


def per_head(columns, head_count, head_dim):
    return columns.reshape(columns.shape[0], head_count, head_dim).transpose(1, 0, 2)


def body(
    tokens_in,
    cotangent,
    routes,
    prefix,
    owners,
    attn_master,
    attn_first,
    attn_second,
    expert_master,
    expert_first,
    expert_second,
    shared_master,
    shared_first,
    shared_second,
    norm_gains,
    gains_first,
    gains_second,
    router,
    router_first,
    router_second,
):
    tok_count, model_width = tokens_in.shape
    owner_count = lax.axis_size("expert")
    own_count = attn_master.shape[0]
    experts_all = router.shape[1]
    top_count = routes.shape[1]
    capacity = tok_count * top_count // experts_all
    head_count = HEADS
    head_dim = HEAD_DIM
    seq_len = SEQ_LEN
    seq_count = tok_count // seq_len
    block_rows = min(512, seq_len)
    score_scale = head_dim ** (-0.5)
    hidden_e = FF
    hidden_s = FFS
    rows_a = model_width * head_dim // 128
    slot_of = slot_place(owners, own_count, owner_count)
    every_slot = lax.all_gather(attn_master.astype(jnp.bfloat16), "expert", axis=0, tiled=True)
    attn_part = jnp.take(every_slot, slot_of, axis=0)
    attn_full, expert_full = (
        lax.all_gather(attn_part, "shard", axis=1, tiled=True),
        lax.all_gather(expert_master.astype(jnp.bfloat16), "shard", axis=2, tiled=True),
    )
    shared_full = lax.all_gather(
        shared_master.astype(jnp.bfloat16), ("expert", "shard"), axis=1, tiled=True
    )
    matrices = attn_full.reshape(4, head_count, model_width, head_dim)
    w_qkv = jnp.concatenate(
        [
            matrices[member].transpose(1, 0, 2).reshape(model_width, head_count * head_dim)
            for member in range(3)
        ],
        1,
    )
    w_out = matrices[3].transpose(0, 2, 1).reshape(head_count * head_dim, model_width)
    w_egu = jnp.concatenate(
        [
            expert_full[0, 0].reshape(model_width, hidden_e),
            expert_full[0, 1].reshape(model_width, hidden_e),
        ],
        1,
    )
    w_ed = expert_full[0, 2].reshape(hidden_e, model_width)
    w_sgu = jnp.concatenate(
        [
            shared_full[0].reshape(model_width, hidden_s),
            shared_full[1].reshape(model_width, hidden_s),
        ],
        1,
    )
    w_sd = shared_full[2].reshape(hidden_s, model_width)
    router_low = router.astype(jnp.bfloat16)
    hidden_in = tokens_in.astype(jnp.float32)
    first_rms = rms_scale(hidden_in)
    first_hat = hidden_in * first_rms
    normed = (first_hat * norm_gains[0]).astype(jnp.bfloat16)
    qkv = jnp.dot(normed, w_qkv, preferred_element_type=jnp.float32)
    cos_table, sin_table = rope_tables(seq_len, head_dim)
    cos_tok = jnp.tile(cos_table, (seq_count, 1))
    sin_tok = jnp.tile(sin_table, (seq_count, 1))
    query_rot = rotate(
        qkv[:, :model_width].reshape(tok_count, head_count, head_dim), cos_tok, sin_tok
    ).astype(jnp.bfloat16)
    key_rot = rotate(
        qkv[:, model_width : 2 * model_width].reshape(tok_count, head_count, head_dim),
        cos_tok,
        sin_tok,
    ).astype(jnp.bfloat16)
    value_rows = (
        qkv[:, 2 * model_width :].astype(jnp.bfloat16).reshape(tok_count, head_count, head_dim)
    )
    member = 0
    seq_heads, seq_totals = attend_forward(
        query_rot, key_rot, value_rows, prefix[member], block_rows, score_scale
    )
    total_parts = [seq_totals]
    heads_flat = seq_heads.reshape(tok_count, model_width)
    middle = hidden_in + jnp.dot(heads_flat, w_out, preferred_element_type=jnp.float32)
    second_rms = rms_scale(middle)
    second_hat = middle * second_rms
    branch_in = (second_hat * norm_gains[1]).astype(jnp.bfloat16)
    logits = jnp.dot(branch_in, router_low, preferred_element_type=jnp.float32)
    choose = routes[:, :, None] == jnp.arange(experts_all, dtype=jnp.int32)[None, None, :]
    chosen = jnp.sum(jnp.where(choose, logits[:, None, :], 0.0), -1)
    exp_chosen = jnp.exp(chosen - jnp.max(chosen, -1, keepdims=True))
    gate_w = exp_chosen / jnp.sum(exp_chosen, -1, keepdims=True)
    shared_gu = jnp.dot(branch_in, w_sgu, preferred_element_type=jnp.float32)
    shared_gate = shared_gu[:, :hidden_s]
    shared_up = shared_gu[:, hidden_s:]
    shared_sig = jax.nn.sigmoid(shared_gate)
    shared_act = shared_gate * shared_sig
    shared_hidden = (shared_act * shared_up).astype(jnp.bfloat16)
    shared_out = jnp.dot(shared_hidden, w_sd, preferred_element_type=jnp.float32)
    flat_ids = routes.reshape(-1)
    onehot = (flat_ids[:, None] == jnp.arange(experts_all, dtype=jnp.int32)[None, :]).astype(
        jnp.int32
    )
    slot_rank = jnp.sum((jnp.cumsum(onehot, 0) - onehot) * onehot, 1)
    target_row = jnp.where(
        slot_rank < capacity, flat_ids * capacity + slot_rank, experts_all * capacity
    )
    token_of = jnp.arange(tok_count * top_count, dtype=jnp.int32) // top_count
    source = (
        jnp.full((experts_all * capacity,), tok_count, jnp.int32)
        .at[target_row]
        .set(token_of, mode="drop")
    )
    padded_in = jnp.concatenate([branch_in, jnp.zeros((1, model_width), jnp.bfloat16)], 0)
    outgoing = jnp.take(padded_in, source, axis=0).reshape(owner_count, 1, capacity, model_width)
    arrived = lax.all_to_all(outgoing, "expert", split_axis=0, concat_axis=1, tiled=True)
    count_rows = arrived.shape[2]
    gate_up = jnp.dot(arrived.reshape(-1, model_width), w_egu, preferred_element_type=jnp.float32)
    gate_part = gate_up[:, :hidden_e]
    expert_hidden = (gate_part * jax.nn.sigmoid(gate_part) * gate_up[:, hidden_e:]).astype(
        jnp.bfloat16
    )
    expert_out = jnp.dot(expert_hidden, w_ed, preferred_element_type=jnp.float32).astype(
        jnp.bfloat16
    )
    returned_rows = lax.all_to_all(
        expert_out.reshape(1, owner_count, count_rows, model_width),
        "expert",
        split_axis=1,
        concat_axis=0,
        tiled=True,
    )
    kept_gate_up = gate_up.reshape(1, owner_count, count_rows, 2 * hidden_e)
    returned_flat = jnp.concatenate(
        [
            returned_rows.reshape(experts_all * capacity, model_width),
            jnp.zeros((1, model_width), jnp.bfloat16),
        ],
        0,
    )
    picked = (
        jnp.take(returned_flat, target_row, axis=0)
        .reshape(tok_count, top_count, model_width)
        .astype(jnp.float32)
    )
    expert_sum = jnp.einsum("tk,tkd->td", gate_w, picked)
    block_out = (middle + shared_out + expert_sum).astype(jnp.bfloat16)
    grad_out = cotangent.astype(jnp.float32)
    grad_gate = jnp.einsum("td,tkd->tk", grad_out, picked)
    grad_chosen = gate_w * (grad_gate - jnp.sum(gate_w * grad_gate, -1, keepdims=True))
    grad_logits = jnp.sum(jnp.where(choose, grad_chosen[:, :, None], 0.0), 1).astype(jnp.bfloat16)
    grad_pairs = (
        (gate_w[:, :, None] * grad_out[:, None, :]).astype(jnp.bfloat16).reshape(-1, model_width)
    )
    grad_send = (
        jnp.zeros((experts_all * capacity, model_width), jnp.bfloat16)
        .at[target_row]
        .set(grad_pairs, mode="drop")
        .reshape(owner_count, 1, capacity, model_width)
    )
    grad_arrived = lax.all_to_all(
        grad_send, "expert", split_axis=0, concat_axis=1, tiled=True
    ).reshape(-1, model_width)
    gate_up_kept = kept_gate_up.reshape(-1, 2 * hidden_e)
    gate_part = gate_up_kept[:, :hidden_e]
    up_part = gate_up_kept[:, hidden_e:]
    gate_sig = jax.nn.sigmoid(gate_part)
    gate_act = gate_part * gate_sig
    expert_hidden = (gate_act * up_part).astype(jnp.bfloat16)
    grad_down = jnp.einsum(
        "rf,rd->fd", expert_hidden, grad_arrived, preferred_element_type=jnp.float32
    )
    grad_hidden = jnp.einsum("rd,fd->rf", grad_arrived, w_ed, preferred_element_type=jnp.float32)
    grad_gate_up = jnp.concatenate(
        [
            grad_hidden * up_part * gate_sig * (1.0 + gate_part * (1.0 - gate_sig)),
            grad_hidden * gate_act,
        ],
        1,
    ).astype(jnp.bfloat16)
    flat_arrived = arrived.reshape(-1, model_width)
    grad_expert_in = jnp.einsum(
        "rd,rf->df", flat_arrived, grad_gate_up, preferred_element_type=jnp.float32
    )
    grad_expert_rows = jnp.einsum(
        "rf,df->rd", grad_gate_up, w_egu, preferred_element_type=jnp.float32
    ).astype(jnp.bfloat16)
    back_rows = lax.all_to_all(
        grad_expert_rows.reshape(1, owner_count, capacity, model_width),
        "expert",
        split_axis=1,
        concat_axis=0,
        tiled=True,
    )
    back_flat = jnp.concatenate(
        [
            back_rows.reshape(experts_all * capacity, model_width),
            jnp.zeros((1, model_width), jnp.bfloat16),
        ],
        0,
    )
    grad_from_experts = jnp.sum(
        jnp.take(back_flat, target_row, axis=0)
        .reshape(tok_count, top_count, model_width)
        .astype(jnp.float32),
        1,
    )
    grad_low_out = grad_out.astype(jnp.bfloat16)
    grad_shared_down = jnp.einsum(
        "tf,td->fd", shared_hidden, grad_low_out, preferred_element_type=jnp.float32
    )
    grad_shared_hidden = jnp.einsum(
        "td,fd->tf", grad_low_out, w_sd, preferred_element_type=jnp.float32
    )
    grad_shared_gu = jnp.concatenate(
        [
            grad_shared_hidden * shared_up * shared_sig * (1.0 + shared_gate * (1.0 - shared_sig)),
            grad_shared_hidden * shared_act,
        ],
        1,
    ).astype(jnp.bfloat16)
    grad_shared_in = jnp.einsum(
        "td,tf->df", branch_in, grad_shared_gu, preferred_element_type=jnp.float32
    )
    grad_router = jnp.einsum(
        "td,te->de", branch_in, grad_logits, preferred_element_type=jnp.float32
    )
    grad_branch = (
        jnp.einsum("tf,df->td", grad_shared_gu, w_sgu, preferred_element_type=jnp.float32)
        + jnp.einsum("te,de->td", grad_logits, router_low, preferred_element_type=jnp.float32)
        + grad_from_experts
    )
    grad_second_gain = jnp.sum(grad_branch * second_hat, 0)
    grad_middle = grad_out + norm_back(grad_branch, second_hat, second_rms, norm_gains[1])
    grad_attn_low = grad_middle.astype(jnp.bfloat16)
    grad_w_out = jnp.einsum(
        "tk,td->kd", heads_flat, grad_attn_low, preferred_element_type=jnp.float32
    )
    grad_heads = (
        jnp.einsum("td,kd->tk", grad_attn_low, w_out, preferred_element_type=jnp.float32)
        .astype(jnp.bfloat16)
        .reshape(tok_count, head_count, head_dim)
    )
    member = 0
    grad_q_seq, grad_k_seq, grad_v_seq = attend_backward(
        query_rot,
        key_rot,
        value_rows,
        grad_heads,
        total_parts[member],
        prefix[member],
        block_rows,
        score_scale,
    )
    grad_query_pre = unrotate(grad_q_seq, cos_tok, sin_tok).reshape(tok_count, model_width)
    grad_key_pre = unrotate(grad_k_seq, cos_tok, sin_tok).reshape(tok_count, model_width)
    grad_value_pre = grad_v_seq.reshape(tok_count, model_width)
    grad_qkv = jnp.concatenate([grad_query_pre, grad_key_pre, grad_value_pre], 1).astype(
        jnp.bfloat16
    )
    grad_w_qkv = jnp.einsum("td,tk->dk", normed, grad_qkv, preferred_element_type=jnp.float32)
    grad_normed = jnp.einsum("tk,dk->td", grad_qkv, w_qkv, preferred_element_type=jnp.float32)
    grad_first_gain = jnp.sum(grad_normed * first_hat, 0)
    tokens_grad = grad_middle + norm_back(grad_normed, first_hat, first_rms, norm_gains[0])
    attn_grad = jnp.concatenate(
        [
            per_head(grad_w_qkv[:, :model_width], head_count, head_dim),
            per_head(grad_w_qkv[:, model_width : 2 * model_width], head_count, head_dim),
            per_head(grad_w_qkv[:, 2 * model_width :], head_count, head_dim),
            grad_w_out.reshape(head_count, head_dim, model_width).transpose(0, 2, 1),
        ],
        0,
    ).reshape(4 * head_count, rows_a, 128)
    expert_grad = jnp.stack(
        [
            grad_expert_in[:, :hidden_e].reshape(-1, 128),
            grad_expert_in[:, hidden_e:].reshape(-1, 128),
            grad_down.reshape(-1, 128),
        ]
    )[None]
    shared_grad = jnp.stack(
        [
            grad_shared_in[:, :hidden_s].reshape(-1, 128),
            grad_shared_in[:, hidden_s:].reshape(-1, 128),
            grad_shared_down.reshape(-1, 128),
        ]
    )
    attn_summed, expert_summed = (
        lax.psum_scatter(attn_grad, "shard", scatter_dimension=1, tiled=True),
        lax.psum_scatter(expert_grad, "shard", scatter_dimension=2, tiled=True),
    )
    shared_summed = lax.psum_scatter(
        shared_grad, ("expert", "shard"), scatter_dimension=1, tiled=True
    )
    slot_buffer = (
        jnp.zeros((owner_count * own_count,) + attn_summed.shape[1:], jnp.float32)
        .at[slot_of]
        .set(attn_summed)
    )
    owned_grad = lax.psum_scatter(slot_buffer, "expert", scatter_dimension=0, tiled=True)
    gain_grad, router_grad = lax.psum(
        (jnp.stack([grad_first_gain, grad_second_gain]), grad_router), ("expert", "shard")
    )
    my_index = lax.axis_index("expert")
    owned_count = jnp.sum((owners == my_index).astype(jnp.int32))
    slot_used = (jnp.arange(own_count, dtype=jnp.int32) < owned_count)[:, None, None]
    attn_w, attn_m, attn_n = adam_update(
        attn_master, attn_first, attn_second, owned_grad, RATE_ATTENTION, WEIGHT_DECAY
    )
    attn_new = jnp.where(slot_used, attn_w, 0.0)
    attn_first_new = jnp.where(slot_used, attn_m, 0.0)
    attn_second_new = jnp.where(slot_used, attn_n, 0.0)
    copies = lax.all_gather(attn_new.astype(jnp.bfloat16), "expert", axis=0, tiled=True)
    attn_copy = jnp.take(copies, slot_of, axis=0)
    expert_new, expert_first_new, expert_second_new = adam_update(
        expert_master, expert_first, expert_second, expert_summed, RATE_MATRIX, WEIGHT_DECAY
    )
    shared_new, shared_first_new, shared_second_new = adam_update(
        shared_master, shared_first, shared_second, shared_summed, RATE_MATRIX, WEIGHT_DECAY
    )
    gains_new, gains_first_new, gains_second_new = adam_update(
        norm_gains, gains_first, gains_second, gain_grad, RATE_GAIN, 0.0
    )
    router_new, router_first_new, router_second_new = adam_update(
        router, router_first, router_second, router_grad, RATE_ROUTER, WEIGHT_DECAY
    )
    return (
        block_out,
        tokens_grad,
        attn_new,
        attn_first_new,
        attn_second_new,
        attn_copy,
        expert_new,
        expert_first_new,
        expert_second_new,
        shared_new,
        shared_first_new,
        shared_second_new,
        gains_new,
        gains_first_new,
        gains_second_new,
        router_new,
        router_first_new,
        router_second_new,
    )


def solution(mesh):
    placed = (
        P(("expert", "shard"), None),
        P(("expert", "shard"), None),
        P(("expert", "shard"), None),
        P(("expert", "shard")),
        P(),
        P("expert", "shard", None),
        P("expert", "shard", None),
        P("expert", "shard", None),
        P("expert", None, "shard", None),
        P("expert", None, "shard", None),
        P("expert", None, "shard", None),
        P(None, ("expert", "shard"), None),
        P(None, ("expert", "shard"), None),
        P(None, ("expert", "shard"), None),
        P(),
        P(),
        P(),
        P(),
        P(),
        P(),
    )
    return jax.shard_map(
        body,
        mesh=mesh,
        in_specs=placed,
        out_specs=(
            P(("expert", "shard"), None),
            P(("expert", "shard"), None),
            P("expert", "shard", None),
            P("expert", "shard", None),
            P("expert", "shard", None),
            P(None, "shard", None),
            P("expert", None, "shard", None),
            P("expert", None, "shard", None),
            P("expert", None, "shard", None),
            P(None, ("expert", "shard"), None),
            P(None, ("expert", "shard"), None),
            P(None, ("expert", "shard"), None),
            P(),
            P(),
            P(),
            P(),
            P(),
            P(),
        ),
        check_vma=False,
    )
```

profile of v0, /device:TPU:9, one launch (start us, length us, event | category | flops | bytes accessed | tf_op | source)
XLA Modules:
  0.0 1397.7 jit_solution(1591649821215142952)
XLA Ops:
  11.6 27.7 %all-gather.6.cloned.1.call-done = bf16[96,48,128]{2,1,0:T(8,128)(2,1)} async-done(((bf16[24,48,128]{2,1,0:T(8,128)(2,1)}), bf16[96,48,128]{2,1,0:T(8,128)(2,1)}) %all-gather.6.cloned.1.call-update) | async-done | bytes 1179664 | tf_op jit(solution)/shard_map/all_gather | solution.py:200
  60.4 32.6 %all-gather.8.cloned.1.call-done = bf16[48,384,128]{2,1,0:T(8,128)(2,1)} async-done(((bf16[48,48,128]{2,1,0:T(8,128)(2,1)}), bf16[48,384,128]{2,1,0:T(8,128)(2,1)}) %all-gather.8.cloned.1.call-update) | async-done | bytes 4718608 | tf_op jit(solution)/shard_map/all_gather | solution.py:203
  137.9 11.5 fusion.16
  149.4 14.5 %fusion.15 = (f32[12,512]{1,0:T(8,128)}, f32[12,512,1024]{2,1,0:T(8,128)}) fusion(pred[512,1024]{1,0:T(8,128)(4,1)S(1)} %get-tuple-element.86, bf16[1024,12,32]{0,2,1:T(8,128)(2,1)} %copy-done.22, bf16[1024,12,32]{0,2,1:T(8,128)(2,1)} %copy-done.20, bf16[1024,12,32]{0,2,1:T(8,128)(2,1)} %copy-done.13, bf16[1024,12,32]{0,2,1:T(8,128)(2,1)} %copy-done.11), kind=kOutput, calls=%fused_computation.41 | convolution fusion | flops 828893184 | bytes 28860416 | tf_op jit(solution)/shard_map/qhd,khd->hqk/dot_general | solution.py:94
  164.0 12.8 fusion.1
  176.9 8.6 fusion.52
  185.4 13.7 fusion
  201.2 8.6 fusion.51
  220.3 9.4 gather_fusion
  268.9 20.5 %all-to-all-done = bf16[4,1,512,768]{3,2,1,0:T(8,128)(2,1)} async-done(((bf16[4,1,512,768]{3,2,1,0:T(8,128)(2,1)}), bf16[4,1,512,768]{3,2,1,0:T(8,128)(2,1)}, u32[]{:S(2)}, u32[]{:S(2)}) %all-to-all-start) | async-done | bytes 3145760 | tf_op jit(solution)/shard_map/all_to_all | solution.py:292
  289.4 22.0 %fusion.126 = f32[2048,4096]{1,0:T(8,128)} fusion(bf16[2048,768]{1,0:T(8,128)(2,1)} %bitcast.20, bf16[768,4096]{1,0:T(8,128)(2,1)} %constant_dynamic-update-slice_fusion.2), kind=kOutput, calls=%fused_computation.256 | convolution fusion | flops 12884901888 | bytes 42991616 | tf_op jit(solution)/shard_map/dot_general | solution.py:294
  311.5 12.2 multiply_convert_fusion.4
  341.4 8.6 mul.636
  351.9 20.7 %all-to-all-done.1 = bf16[1,4,512,768]{3,2,0,1:T(8,128)(2,1)} async-done(((bf16[1,4,512,768]{3,2,0,1:T(8,128)(2,1)}), bf16[1,4,512,768]{3,2,0,1:T(8,128)(2,1)}, u32[]{:S(2)}, u32[]{:S(2)}) %all-to-all-start.1) | async-done | bytes 3145760 | tf_op jit(solution)/shard_map/all_to_all | solution.py:302
  374.7 9.4 gather_fusion.2
  389.0 8.4 fusion.35
  398.2 13.3 scatter_custom_fusion.1
  443.8 9.8 fusion.125
  453.5 23.1 %multiply_convert_fusion.3 = (bf16[2048,2048]{1,0:T(8,128)(2,1)}, bf16[2048,2048]{1,0:T(8,128)(2,1)}) fusion(f32[2048,4096]{1,0:T(8,128)} %fusion.126, bf16[2048,768]{1,0:T(8,128)(2,1)} %bitcast.28, bf16[2048,768]{1,0:T(8,128)(2,1)S(1)} %copy-done.36), kind=kOutput, calls=%fused_computation.28 | convolution fusion | flops 6496976896 | bytes 56623104 | tf_op jit(solution)/shard_map/rd,fd->rf/dot_general | solution.py:349
  476.7 19.8 %fusion.24 = bf16[2048,768]{1,0:T(8,128)(2,1)} fusion(bf16[768,4096]{1,0:T(8,128)(2,1)} %constant_dynamic-update-slice_fusion.2, bf16[2048,2048]{1,0:T(8,128)(2,1)} %get-tuple-element.47, bf16[2048,2048]{1,0:T(8,128)(2,1)} %get-tuple-element.46), kind=kOutput, calls=%fused_computation.64 | convolution fusion | flops 12920029184 | bytes 26214400 | tf_op jit(solution)/shard_map/rf,df->rd/dot_general | solution.py:361
  500.2 13.8 multiply_convert_fusion.6
  514.0 14.1 %fusion.19 = f32[1024,768]{1,0:T(8,128)} fusion(bf16[768,4096]{1,0:T(8,128)(2,1)} %copy-done.40, bf16[1024,2048]{1,0:T(8,128)(2,1)S(1)} %get-tuple-element.49, bf16[1024,2048]{1,0:T(8,128)(2,1)S(1)} %get-tuple-element.48), kind=kOutput, calls=%fused_computation.51 | convolution fusion | flops 6459228160 | bytes 17825792 | tf_op jit(solution)/shard_map/tf,df->td/dot_general | solution.py:405
  539.5 9.4 gather_fusion.3
  553.2 8.6 reshape.452
  561.8 12.1 reduce_sum.175
  585.6 13.2 fusion.5
  598.8 17.7 %multiply_reduce_fusion = (f32[12,512]{1,0:T(8,128)S(1)}, f32[12,512,1024]{2,1,0:T(8,128)}) fusion(f32[12,512]{1,0:T(8,128)S(1)} %copy-done.58, f32[12,512,1024]{2,1,0:T(8,128)} %get-tuple-element.91, pred[512,1024]{1,0:T(8,128)(4,1)S(1)} %copy-done.10, bf16[512,12,64]{0,2,1:T(8,128)(2,1)} %bitcast.179, bf16[1024,12,64]{0,2,1:T(8,128)(2,1)S(1)} %bitcast.161), kind=kOutput, calls=%fused_computation.9 | convolution fusion | flops 836757504 | bytes 53264384 | tf_op jit(solution)/shard_map/qhd,khd->hqk/dot_general | solution.py:133
  616.5 21.4 %multiply_reduce_fusion.1 = (f32[12,512]{1,0:T(8,128)S(1)}, f32[12,512,1024]{2,1,0:T(8,128)}) fusion(f32[12,512]{1,0:T(8,128)S(1)} %copy-done.57, f32[12,512,1024]{2,1,0:T(8,128)} %get-tuple-element.93, pred[512,1024]{1,0:T(8,128)(4,1)S(1)} %copy-done.27, bf16[512,12,64]{0,2,1:T(8,128)(2,1)S(1)} %bitcast.176, bf16[1024,12,64]{0,2,1:T(8,128)(2,1)S(1)} %bitcast.162), kind=kOutput, calls=%fused_computation.12 | convolution fusion | flops 836757504 | bytes 53264384 | tf_op jit(solution)/shard_map/qhd,khd->hqk/dot_general | solution.py:133
  637.9 42.0 %multiply_convert_fusion = (bf16[12,512,1024]{2,1,0:T(8,128)(2,1)}, bf16[12,512,1024]{2,1,0:T(8,128)(2,1)}) fusion(f32[12,512,1024]{2,1,0:T(8,128)} %get-tuple-element.98, f32[12,512]{1,0:T(8,128)S(1)} %get-tuple-element.97, f32[12,512]{1,0:T(8,128)S(1)} %copy-done.58, f32[12,512,1024]{2,1,0:T(8,128)} %get-tuple-element.91, ...), kind=kLoop, calls=%fused_computation.8 | loop fusion | flops 75497472 | bytes 126976000 | tf_op jit(solution)/shard_map/convert_element_type | solution.py:137
  679.9 8.7 multiply_bitcast_fusion.2
  695.5 14.1 %add_convert_fusion = bf16[12,64,1024]{2,1,0:T(8,128)(2,1)} fusion(f32[12,64,1024]{2,1,0:T(8,128)} %fusion.5, bf16[512,12,64]{0,2,1:T(8,128)(2,1)S(1)} %bitcast.177, f32[12,512]{1,0:T(8,128)S(1)} %copy-done.57, f32[12,512,1024]{2,1,0:T(8,128)} %get-tuple-element.93, pred[512,1024]{1,0:T(8,128)(4,1)S(1)} %copy-done.27), kind=kOutput, calls=%fused_computation.80 | convolution fusion | flops 832045056 | bytes 31219712 | tf_op jit(solution)/shard_map/hqk,qhd->khd/dot_general | solution.py:149
  709.7 8.6 multiply_bitcast_fusion.1
  752.6 13.8 copy.111
  766.4 15.8 %reshape.451 = f32[48,384,128]{2,1,0:T(8,128)} reshape(f32[48,768,64]{2,1,0:T(8,128)} %copy.111) | data formatting | bytes 18874368 | tf_op jit(solution)/shard_map/reshape | solution.py:449
  782.2 99.3 %reduce-scatter.5.cloned.1.call-done = f32[48,48,128]{2,1,0:T(8,128)} async-done(((f32[48,384,128]{2,1,0:T(8,128)}), f32[48,48,128]{2,1,0:T(8,128)}) %reduce-scatter.5.cloned.1.call-update) | async-done | bytes 1179664 | tf_op jit(solution)/shard_map/reduce_scatter | solution.py:465
  889.7 13.1 fusion.18
  902.8 11.7 fusion.117
  929.0 8.3 fusion.129
  944.2 14.6 %pad_maximum_fusion = f32[3,12288,128]{2,1,0:T(8,128)} fusion(f32[1,12288,128]{2,1,0:T(8,128)} %stack_reshape.23, f32[1,12288,128]{2,1,0:T(8,128)} %stack_reshape.22, f32[1,12288,128]{2,1,0:T(8,128)} %stack_reshape.21), kind=kLoop, calls=%fused_computation.25 | loop fusion | flops 9437184 | bytes 37748736 | tf_op jit(solution)/shard_map/stack | solution.py:457
  960.8 12.1 fusion.128
  980.1 21.5 %fusion.13 = f32[768,4096]{1,0:T(8,128)} fusion(bf16[2048,768]{1,0:T(8,128)(2,1)} %bitcast.20, bf16[2048,2048]{1,0:T(8,128)(2,1)} %get-tuple-element.47, bf16[2048,2048]{1,0:T(8,128)(2,1)} %get-tuple-element.46), kind=kOutput, calls=%fused_computation.38 | convolution fusion | flops 12918456320 | bytes 32505856 | tf_op jit(solution)/shard_map/rd,rf->df/dot_general | solution.py:358
  1001.5 12.4 fusion.118
  1031.9 14.9 %maximum_bitcast_fusion = f32[1,3,12288,128]{3,2,1,0:T(8,128)} fusion(f32[1,12288,128]{2,1,0:T(8,128)} %stack_reshape.20, f32[1,12288,128]{2,1,0:T(8,128)} %stack_reshape.19, f32[1,12288,128]{2,1,0:T(8,128)} %stack_reshape.18), kind=kLoop, calls=%fused_computation.24 | loop fusion | flops 9437184 | bytes 37748736 | tf_op jit(solution)/shard_map/broadcast_in_dim | solution.py:450
  1056.4 8.9 fusion.33
  1071.5 41.5 %all-reduce.3 = (f32[2,768]{1,0:T(2,128)S(1)}, f32[768,4]{0,1:T(4,128)S(1)}) all-reduce(f32[2,768]{1,0:T(2,128)S(1)} %pad_maximum_fusion.26, f32[768,4]{0,1:T(4,128)S(1)} %fusion.130), channel_id=1, replica_groups=mesh['expert'=4,'shard'=8] {'expert','shard'}, use_global_device_ids=true, to_apply=%region_31.34 | all-reduce | flops 4608 | bytes 36864 | tf_op jit(solution)/shard_map/psum | solution.py:477
  1119.2 45.2 %reduce-scatter.11.cloned.1.call-done = f32[3,384,128]{2,1,0:T(8,128)} async-done(((f32[3,12288,128]{2,1,0:T(8,128)}), f32[3,384,128]{2,1,0:T(8,128)}) %reduce-scatter.11.cloned.1.call-update) | async-done | bytes 589840 | tf_op jit(solution)/shard_map/reduce_scatter | solution.py:468
  1167.5 27.4 %all-gather.14.cloned.1.call-done = bf16[96,48,128]{2,1,0:T(8,128)(2,1)} async-done(((bf16[24,48,128]{2,1,0:T(8,128)(2,1)}), bf16[96,48,128]{2,1,0:T(8,128)(2,1)}) %all-gather.14.cloned.1.call-update) | async-done | bytes 1179664 | tf_op jit(solution)/shard_map/all_gather | solution.py:489
  1197.8 185.8 %reduce-scatter.9.cloned.1.call-done = f32[1,3,1536,128]{3,2,1,0:T(8,128)} async-done(((f32[1,3,12288,128]{3,2,1,0:T(8,128)}), f32[1,3,1536,128]{3,2,1,0:T(8,128)}) %reduce-scatter.9.cloned.1.call-update) | async-done | bytes 2359312 | tf_op jit(solution)/shard_map/reduce_scatter | solution.py:466
  (407 shorter events, 344.1 us)
Async XLA Ops:
  7.2 35.2 %copy-start.24 = (f32[1,3,1536,128]{3,2,1,0:T(8,128)S(1)}, f32[1,3,1536,128]{3,2,1,0:T(8,128)}, u32[]{:S(2)}) copy-start(f32[1,3,1536,128]{3,2,1,0:T(8,128)} %param.32) | copy-start | bytes 7077892
  7.2 32.2 %all-gather.6.cloned.1.call-start = ((), (), s32[]{:S(2)}) async-start(), calls=%async_computation.8 | async-start | bytes 1474560 | tf_op jit(solution)/shard_map/all_gather | solution.py:200
  9.2 83.8 %all-gather.8.cloned.1.call-start = ((), (), s32[]{:S(2)}) async-start(), calls=%async_computation.9 | async-start | bytes 5308416 | tf_op jit(solution)/shard_map/all_gather | solution.py:203
  11.6 29.7 %copy-start.109 = (s32[48]{0:T(128)}, s32[48]{0:T(128)S(1)}, u32[]{:S(2)}) copy-start(s32[48]{0:T(128)S(1)} %get-tuple-element.45) | copy-start | bytes 580
  11.6 32.0 %copy-start.106 = (pred[48]{0:T(512)(128)(4,1)}, pred[48]{0:T(512)(128)(4,1)S(1)}, u32[]{:S(2)}) copy-start(pred[48]{0:T(512)(128)(4,1)S(1)} %get-tuple-element.44) | copy-start | bytes 148
  11.6 29.7 %copy-start.103 = (s32[1024]{0:T(1024)}, s32[1024]{0:T(1024)S(1)}, u32[]{:S(2)}) copy-start(s32[1024]{0:T(1024)S(1)} %pad_clamp_fusion) | copy-start | bytes 12292
  42.3 195.6 %all-gather.12.cloned.1.call-start = ((), (), s32[]{:S(2)}) async-start(), calls=%async_computation.11 | async-start | bytes 10616832 | tf_op jit(solution)/shard_map/all_gather | solution.py:204
  43.6 372.8 %all-gather.10.cloned.1.call-start = ((), (), s32[]{:S(2)}) async-start(), calls=%async_computation.10 | async-start | bytes 9732096 | tf_op jit(solution)/shard_map/all_gather | solution.py:206
  45.0 52.6 %copy-start.72 = (s32[2048]{0:T(1024)}, s32[2048]{0:T(1024)S(1)}, u32[]{:S(2)}) copy-start(s32[2048]{0:T(1024)S(1)} %eq.63) | copy-start | bytes 24580
  47.5 50.1 %copy-start.74 = (s32[2048]{0:T(1024)}, s32[2048]{0:T(1024)S(1)}, u32[]{:S(2)}) copy-start(s32[2048]{0:T(1024)S(1)} %fusion.66) | copy-start | bytes 24580
  47.6 50.0 %copy-start.102 = (s32[2048,1]{0,1:T(1,128)}, s32[2048,1]{0,1:T(1,128)S(1)}, u32[]{:S(2)}) copy-start(s32[2048,1]{0,1:T(1,128)S(1)} %compare_select_fusion) | copy-start | bytes 24580
  57.3 56.1 %copy-start.96 = (f32[1024]{0:T(1024)}, f32[1024]{0:T(1024)S(1)}, u32[]{:S(2)}) copy-start(f32[1024]{0:T(1024)S(1)} %add_rsqrt_fusion.1) | copy-start | bytes 12292
  58.0 55.5 %copy-start.92 = (f32[768]{0:T(1024)}, f32[768]{0:T(1024)S(1)}, u32[]{:S(2)}) copy-start(f32[768]{0:T(1024)S(1)} %get-tuple-element.25) | copy-start | bytes 9220
  60.4 116.4 %copy-start.9 = (pred[512,1024]{1,0:T(8,128)(4,1)}, pred[512,1024]{1,0:T(8,128)(4,1)S(1)}, u32[]{:S(2)}) copy-start(pred[512,1024]{1,0:T(8,128)(4,1)S(1)} %get-tuple-element.87) | copy-start | bytes 1572868
  60.4 138.8 %copy-start.26 = (pred[512,1024]{1,0:T(8,128)(4,1)}, pred[512,1024]{1,0:T(8,128)(4,1)S(1)}, u32[]{:S(2)}) copy-start(pred[512,1024]{1,0:T(8,128)(4,1)S(1)} %get-tuple-element.86) | copy-start | bytes 1572868
  129.7 69.5 %copy-start.7 = (bf16[1024,768]{0,1:T(8,128)(2,1)}, bf16[1024,768]{0,1:T(8,128)(2,1)S(1)}, u32[]{:S(2)}) copy-start(bf16[1024,768]{0,1:T(8,128)(2,1)S(1)} %copy.95) | copy-start | bytes 4718596
  149.4 27.4 %slice-start = ((s8[25165824]{0:T(1024)(128)(4,1)}), s8[4194304]{0:T(1024)(128)(4,1)S(1)}, s32[]{:S(2)}) async-start(s8[25165824]{0:T(1024)(128)(4,1)} %bitcast.157), calls=%async_computation.17 | async-start | bytes 8388608
  149.4 27.4 %slice-start.1 = ((s8[25165824]{0:T(1024)(128)(4,1)}), s8[4194304]{0:T(1024)(128)(4,1)S(1)}, s32[]{:S(2)}) async-start(s8[25165824]{0:T(1024)(128)(4,1)} %bitcast.157), calls=%async_computation.18 | async-start | bytes 8388608
  149.4 27.4 %slice-start.2 = ((s8[25165824]{0:T(1024)(128)(4,1)}), s8[4194304]{0:T(1024)(128)(4,1)S(1)}, s32[]{:S(2)}) async-start(s8[25165824]{0:T(1024)(128)(4,1)} %bitcast.157), calls=%async_computation.19 | async-start | bytes 8388608
  149.4 27.4 %slice-start.3 = ((s8[25165824]{0:T(1024)(128)(4,1)}), s8[4194304]{0:T(1024)(128)(4,1)S(1)}, s32[]{:S(2)}) async-start(s8[25165824]{0:T(1024)(128)(4,1)} %bitcast.157), calls=%async_computation.20 | async-start | bytes 8388608
  219.9 130.1 %copy-start.4 = (bf16[1024,768]{1,0:T(8,128)(2,1)}, bf16[1024,768]{1,0:T(8,128)(2,1)S(1)}, u32[]{:S(2)}) copy-start(bf16[1024,768]{1,0:T(8,128)(2,1)S(1)} %multiply_convert_fusion.10) | copy-start | bytes 4718596
  233.0 56.4 %all-to-all-start = ((bf16[4,1,512,768]{3,2,1,0:T(8,128)(2,1)}), bf16[4,1,512,768]{3,2,1,0:T(8,128)(2,1)}, u32[]{:S(2)}, u32[]{:S(2)}) async-start(bf16[4,1,512,768]{3,2,1,0:T(8,128)(2,1)} %broadcast_select_fusion.1), calls=%async_computation | async-start | bytes 6291456 | tf_op jit(solution)/shard_map/all_to_all | solution.py:292
  331.8 40.9 %all-to-all-start.1 = ((bf16[1,4,512,768]{3,2,0,1:T(8,128)(2,1)}), bf16[1,4,512,768]{3,2,0,1:T(8,128)(2,1)}, u32[]{:S(2)}, u32[]{:S(2)}) async-start(bf16[1,4,512,768]{3,2,0,1:T(8,128)(2,1)} %bitcast.174), calls=%async_computation.1 | async-start | bytes 6291456 | tf_op jit(solution)/shard_map/all_to_all | solution.py:302
  350.0 34.2 %copy-start.90 = (pred[2048]{0:T(1024)(128)(4,1)}, pred[2048]{0:T(1024)(128)(4,1)S(1)}, u32[]{:S(2)}) copy-start(pred[2048]{0:T(1024)(128)(4,1)S(1)} %compare_and_fusion) | copy-start | bytes 6148
  350.0 24.7 %copy-start.81 = (s32[2048]{0:T(1024)}, s32[2048]{0:T(1024)S(1)}, u32[]{:S(2)}) copy-start(s32[2048]{0:T(1024)S(1)} %broadcast_clamp_fusion) | copy-start | bytes 24580
  397.7 130.4 %copy-start.67 = (f32[1024,2]{0,1:T(2,128)}, f32[1024,2]{0,1:T(2,128)S(1)}, u32[]{:S(2)}) copy-start(f32[1024,2]{0,1:T(2,128)S(1)} %get-tuple-element.43) | copy-start | bytes 24580
  411.6 42.0 %all-to-all-start.2 = ((bf16[4,1,512,768]{3,2,1,0:T(8,128)(2,1)}), bf16[4,1,512,768]{3,2,1,0:T(8,128)(2,1)}, u32[]{:S(2)}, u32[]{:S(2)}) async-start(bf16[4,1,512,768]{3,2,1,0:T(8,128)(2,1)} %bitcast.27), calls=%async_computation.2 | async-start | bytes 6291456 | tf_op jit(solution)/shard_map/all_to_all | solution.py:337
  496.5 39.2 %all-to-all-start.3 = ((bf16[1,4,512,768]{3,2,0,1:T(8,128)(2,1)}), bf16[1,4,512,768]{3,2,0,1:T(8,128)(2,1)S(1)}, u32[]{:S(2)}, u32[]{:S(2)}) async-start(bf16[1,4,512,768]{3,2,0,1:T(8,128)(2,1)} %bitcast.175), calls=%async_computation.3 | async-start | bytes 6291456 | tf_op jit(solution)/shard_map/all_to_all | solution.py:364
  500.2 381.3 %reduce-scatter.5.cloned.1.call-start = ((), (), s32[]{:S(2)}) async-start(), calls=%async_computation.12 | async-start | bytes 10616832 | tf_op jit(solution)/shard_map/reduce_scatter | solution.py:465
  528.2 45.6 %copy-start.79 = (bf16[1024,4]{0,1:T(4,128)(2,1)}, bf16[1024,4]{0,1:T(4,128)(2,1)S(1)}, u32[]{:S(2)}) copy-start(bf16[1024,4]{0,1:T(4,128)(2,1)S(1)} %select_reduce_fusion) | copy-start | bytes 24580
  598.8 17.7 %copy-start.27 = (pred[512,1024]{1,0:T(8,128)(4,1)S(1)}, pred[512,1024]{1,0:T(8,128)(4,1)}, u32[]{:S(2)}) copy-start(pred[512,1024]{1,0:T(8,128)(4,1)} %copy-done.26) | copy-start | bytes 1572868
  598.8 17.7 %copy-start.57 = (f32[12,512]{1,0:T(8,128)S(1)}, f32[12,512]{1,0:T(8,128)}, u32[]{:S(2)}) copy-start(f32[12,512]{1,0:T(8,128)} %log_add_fusion.1) | copy-start | bytes 73732
  637.9 42.0 %copy-start.21 = (bf16[1024,12,32]{0,2,1:T(8,128)(2,1)S(1)}, bf16[1024,12,32]{0,2,1:T(8,128)(2,1)}, u32[]{:S(2)}) copy-start(bf16[1024,12,32]{0,2,1:T(8,128)(2,1)} %copy-done.20) | copy-start | bytes 2359300
  637.9 42.0 %copy-start.23 = (bf16[1024,12,32]{0,2,1:T(8,128)(2,1)S(1)}, bf16[1024,12,32]{0,2,1:T(8,128)(2,1)}, u32[]{:S(2)}) copy-start(bf16[1024,12,32]{0,2,1:T(8,128)(2,1)} %copy-done.22) | copy-start | bytes 2359300
  782.1 100.9 %copy-start.110 = (s32[48]{0:T(128)S(1)}, s32[48]{0:T(128)}, u32[]{:S(2)}) copy-start(s32[48]{0:T(128)} %copy-done.109) | copy-start | bytes 580
  782.2 246.6 %reduce-scatter.7.cloned.1.call-start = ((), (), s32[]{:S(2)}) async-start(), calls=%async_computation.13 | async-start | bytes 2949120 | tf_op jit(solution)/shard_map/reduce_scatter | solution.py:476
  889.6 274.7 %reduce-scatter.11.cloned.1.call-start = ((), (), s32[]{:S(2)}) async-start(), calls=%async_computation.16 | async-start | bytes 19464192 | tf_op jit(solution)/shard_map/reduce_scatter | solution.py:468
  958.9 236.0 %all-gather.14.cloned.1.call-start = ((), (), s32[]{:S(2)}) async-start(), calls=%async_computation.14 | async-start | bytes 1474560 | tf_op jit(solution)/shard_map/all_gather | solution.py:489
  1031.8 351.9 %reduce-scatter.9.cloned.1.call-start = ((), (), s32[]{:S(2)}) async-start(), calls=%async_computation.15 | async-start | bytes 21233664 | tf_op jit(solution)/shard_map/reduce_scatter | solution.py:466
  1065.4 47.6 %copy-start.89 = (f32[2,768]{1,0:T(2,128)S(1)}, f32[2,768]{1,0:T(2,128)}, u32[]{:S(2)}) copy-start(f32[2,768]{1,0:T(2,128)} %param.38) | copy-start | bytes 18436
  1065.4 47.6 %copy-start.104 = (f32[2,768]{1,0:T(2,128)S(1)}, f32[2,768]{1,0:T(2,128)}, u32[]{:S(2)}) copy-start(f32[2,768]{1,0:T(2,128)} %param.39) | copy-start | bytes 18436
  1065.4 47.6 %copy-start.105 = (f32[2,768]{1,0:T(2,128)S(1)}, f32[2,768]{1,0:T(2,128)}, u32[]{:S(2)}) copy-start(f32[2,768]{1,0:T(2,128)} %param.40) | copy-start | bytes 18436
  1065.5 48.2 %copy-start.78 = (f32[768,4]{0,1:T(4,128)S(1)}, f32[768,4]{0,1:T(4,128)}, u32[]{:S(2)}) copy-start(f32[768,4]{0,1:T(4,128)} %param.41) | copy-start | bytes 36868
  1065.5 48.2 %copy-start.99 = (f32[768,4]{0,1:T(4,128)S(1)}, f32[768,4]{0,1:T(4,128)}, u32[]{:S(2)}) copy-start(f32[768,4]{0,1:T(4,128)} %param.42) | copy-start | bytes 36868
  1065.5 48.2 %copy-start.100 = (f32[768,4]{0,1:T(4,128)S(1)}, f32[768,4]{0,1:T(4,128)}, u32[]{:S(2)}) copy-start(f32[768,4]{0,1:T(4,128)} %param.43) | copy-start | bytes 36868
  1065.5 48.8 %copy-start.19 = (f32[1024,768]{1,0:T(8,128)S(1)}, f32[1024,768]{1,0:T(8,128)}, u32[]{:S(2)}) copy-start(f32[1024,768]{1,0:T(8,128)} %copy-done.18) | copy-start | bytes 9437188
  1119.2 77.7 %copy-start.107 = (pred[48]{0:T(512)(128)(4,1)S(1)}, pred[48]{0:T(512)(128)(4,1)}, u32[]{:S(2)}) copy-start(pred[48]{0:T(512)(128)(4,1)} %copy-done.106) | copy-start | bytes 148
  1119.2 264.5 %copy-start.25 = (f32[1,3,1536,128]{3,2,1,0:T(8,128)S(1)}, f32[1,3,1536,128]{3,2,1,0:T(8,128)}, u32[]{:S(2)}) copy-start(f32[1,3,1536,128]{3,2,1,0:T(8,128)} %param.32) | copy-start | bytes 7077892
  (88 other events, 646.6 us)
Sparse Core Ops, SparseCore 0:
  10.4 28.8 all-gather.5
  42.4 50.5 all-gather.7
  94.6 88.3 all-gather.11
  186.5 115.9 all-gather.9
  782.3 99.1 reduce-scatter.4
  889.8 37.2 reduce-scatter.6
  959.0 205.3 reduce-scatter.10
  1166.8 27.9 all-gather.13
  1197.2 186.4 reduce-scatter.8
where the time goes:
time: 1410 us; the launch traced here: 1400 us
  waiting for transfers between devices  467 us (33%)
  matrix products  362 us (26%)
  local copies, waits for them, and re-layouts  298 us (21%)
  other arithmetic  194 us (14%)
  blocking collectives  41.5 us (3%)
  starting transfers between devices  19 us (1%)
  between operations  16.3 us (1%)
    reduce_scatter x1, waiting for transfers between devices, body(): lax.psum_scatter(expert_grad, 'shard', scatter_dimension=2, tiled=True)  186 us
    reduce_scatter x1, waiting for transfers between devices, body(): lax.psum_scatter(attn_grad, 'shard', scatter_dimension=1, tiled=True)  99.3 us
    reduce_scatter x1, waiting for transfers between devices, body(): lax.psum_scatter(shared_grad, ('expert', 'shard'), scatter_dimension=1, t...  45.2 us
    convert_element_type x1, other arithmetic, attend_backward(): grad_scores = (prob_block * (grad_probs - center)).astype(jnp.bfloat16)  42 us
    psum x1, blocking collectives, body(): lax.psum((jnp.stack([grad_first_gain, grad_second_gain]), grad_router), (...  41.5 us
    dot_general x2, matrix products, attend_backward(): jnp.einsum('qhd,khd->hqk', grad_block, value_rows, preferred_element_type...  39.1 us
    all_gather x1, waiting for transfers between devices, body(): lax.all_gather(attn_part, 'shard', axis=1, tiled=True)  32.6 us
  transfers between devices with their start and end apart: 13, of which 9 were waited for; matrix products, arithmetic and copies ran while one was open for 38% of the time, Pallas kernels for 0%

commit v1 on v0

v1 whole, which is shorter than its diff:
```python
import functools
import jax
import jax.numpy as jnp
from jax import lax
from jax.experimental import pallas as pl
from jax.experimental.pallas import tpu as pltpu
from jax.sharding import Mesh, PartitionSpec as P

HEADS = 12
HEAD_DIM = 64
FF = 2048
FFS = 2048
SEQ_LEN = 1024
STEP = 5

NORM_EPSILON = 1e-06
ADAM_EPSILON = 1e-08
FIRST_BETA = 0.5
SECOND_BETA = 0.5
WEIGHT_DECAY = 0.1
RATE_ATTENTION = 0.06
RATE_MATRIX = 0.03
RATE_ROUTER = 0.02
RATE_GAIN = 0.3
ROPE_BASE = 10000.0

PACK = 4
HALF = HEAD_DIM // 2
GROUP = PACK * HEAD_DIM
GROUPS = HEADS // PACK
BLOCK = 256
LONGEST_PREFIX = SEQ_LEN // 2
VMEM_BYTES = 60 * 1024 * 1024
AT_ONCE = pl.CostEstimate(flops=0, bytes_accessed=0, transcendentals=0)
LOW = jnp.bfloat16
WIDE = jnp.float32


def dot_nn(left, right):
    return jnp.dot(left, right, preferred_element_type=WIDE)


def dot_nt(left, right):
    return lax.dot_general(left, right, (((1,), (1,)), ((), ())), preferred_element_type=WIDE)


ANYWHERE = pl.BlockSpec(memory_space=pl.ANY)


def ignoring(kernel, first, count):
    return lambda *refs: kernel(*refs[:first], *refs[first + count :])


def side_by_side(ref):
    return jnp.concatenate([ref[piece] for piece in range(ref.shape[0])], 1)


def whole(shape):
    return pl.BlockSpec(shape, lambda *_: (0,) * len(shape))


def once(shape):
    return pl.BlockSpec(shape, lambda *_: (0,) * len(shape), pipeline_mode=pl.Buffered(1))


def params():
    return pltpu.CompilerParams(vmem_limit_bytes=VMEM_BYTES)


def chunk_of(shape):
    return (lax.broadcasted_iota(jnp.int32, shape, 1) & 127) >> 5


def gather_columns_kernel(slot_ref, slots_ref, out_ref, wide_ref):
    pairs = slots_ref.shape[1]
    chunk = chunk_of((pairs, 128))
    for group in range(GROUPS):
        for kind in range(4):
            parts = [
                slots_ref[slot_ref[kind * HEADS + group * PACK + head]].astype(WIDE)
                for head in range(PACK)
            ]
            for parity in range(2):
                for half in range(2):
                    source = 2 * parity + half
                    packed = None
                    for head in range(PACK):
                        shift = (head - source) * HALF % 128
                        moved = pltpu.roll(parts[head], shift, 1) if shift else parts[head]
                        packed = moved if head == 0 else jnp.where(chunk == head, moved, packed)
                    place = (group * 4 + kind) * 2 + half
                    wide_ref[place, pl.ds(parity, pairs, stride=2), :] = packed
    for place in range(wide_ref.shape[0]):
        out_ref[:, place * 128 : (place + 1) * 128] = wide_ref[place].astype(LOW)


def gather_columns(slots, slot_of):
    pairs = slots.shape[1]
    shape = (2 * pairs, GROUPS * 4 * GROUP)
    return pl.pallas_call(
        gather_columns_kernel,
        out_shape=jax.ShapeDtypeStruct(shape, LOW),
        in_specs=[pl.BlockSpec(memory_space=pltpu.SMEM), pl.BlockSpec(memory_space=pltpu.VMEM)],
        out_specs=pl.BlockSpec(memory_space=pltpu.VMEM),
        scratch_shapes=[pltpu.VMEM((shape[1] // 128, shape[0], 128), WIDE)],
        compiler_params=params(),
    )(slot_of, slots)


def split_columns_kernel(slot_ref, grad_ref, *refs):
    out_refs, slots_ref, wide_ref = refs[:-2], refs[-2], refs[-1]
    slots, pairs, _ = slots_ref.shape
    chunk = chunk_of((pairs, 128))
    slots_ref[...] = jnp.zeros_like(slots_ref)
    for group in range(GROUPS):
        first = group * 4 * GROUP
        for place in range(wide_ref.shape[0]):
            columns = slice(first + place * 128, first + (place + 1) * 128)
            wide_ref[place] = grad_ref[:, columns].astype(WIDE)
        for kind in range(4):
            blocks = [
                wide_ref[kind * 2 + source % 2, pl.ds(source // 2, pairs, stride=2), :]
                for source in range(4)
            ]
            for head in range(PACK):
                packed = None
                for source in range(4):
                    shift = (source - head) * HALF % 128
                    moved = pltpu.roll(blocks[source], shift, 1) if shift else blocks[source]
                    packed = moved if source == 0 else jnp.where(chunk == source, moved, packed)
                slots_ref[slot_ref[kind * HEADS + group * PACK + head]] = packed.astype(LOW)
    held = slots // len(out_refs)
    for index, out_ref in enumerate(out_refs):
        out_ref[...] = slots_ref[index * held : (index + 1) * held]


def split_columns(grad, slot_of, partners, held):
    rows = grad.shape[0]
    shape = (held, rows // 2, 128)
    return pl.pallas_call(
        split_columns_kernel,
        out_shape=[jax.ShapeDtypeStruct(shape, LOW)] * partners,
        in_specs=[pl.BlockSpec(memory_space=pltpu.SMEM), pl.BlockSpec(memory_space=pltpu.VMEM)],
        out_specs=[pl.BlockSpec(memory_space=pltpu.VMEM)] * partners,
        scratch_shapes=[
            pltpu.VMEM((partners * held, rows // 2, 128), LOW),
            pltpu.VMEM((4 * GROUP // 128, rows, 128), WIDE),
        ],
        compiler_params=params(),
    )(slot_of, grad)


def key_extent(block):
    return max((block + 1) * BLOCK, LONGEST_PREFIX)


def attend_forward_kernel(
    prefix_ref, token_ref, gain_ref, cos_ref, sin_ref, w_ref,
    query_ref, key_ref, value_ref, head_ref, total_ref, normed_ref, middle_ref, branch_ref,
    sum_ref,
):
    group = pl.program_id(0)
    length, width = token_ref.shape

    @pl.when(group == 0)
    def _():
        hidden = token_ref[...].astype(WIDE)
        scale = lax.rsqrt(jnp.mean(hidden * hidden, -1, keepdims=True) + NORM_EPSILON)
        normed_ref[...] = (hidden * scale * gain_ref[0:1, :]).astype(LOW)
        middle_ref[...] = hidden
        total_ref[...] = jnp.zeros_like(total_ref)

    projected = dot_nn(normed_ref[...], w_ref[:, : 3 * GROUP])
    cos, sin = cos_ref[...], sin_ref[...]
    for kind, ref in enumerate((query_ref, key_ref)):
        lead = projected[:, kind * GROUP : kind * GROUP + 128]
        tail = projected[:, kind * GROUP + 128 : (kind + 1) * GROUP]
        ref[:, :128] = (lead * cos - tail * sin).astype(LOW)
        ref[:, 128:] = (tail * cos + lead * sin).astype(LOW)
    value_ref[...] = projected[:, 2 * GROUP :].astype(LOW)
    prefix = prefix_ref[0]

    lane = lax.broadcasted_iota(jnp.int32, (1, GROUP), 1)
    total_lane = lax.broadcasted_iota(jnp.int32, (BLOCK, 128), 1)
    owned = [chunk_of((1, GROUP)) == head for head in range(PACK)]
    ones = [lane == (head + 1) % PACK * HALF for head in range(PACK)]
    items = [(head, block) for head in range(PACK) for block in range(length // BLOCK)]

    def score(head, block):
        rows = slice(block * BLOCK, (block + 1) * BLOCK)
        own = owned[head].astype(WIDE).astype(LOW)
        return dot_nt(
            query_ref[rows, :] * (own * HEAD_DIM ** (-0.5)), key_ref[: key_extent(block), :]
        )

    def attend(head, block, scores):
        start = block * BLOCK
        rows = slice(start, start + BLOCK)
        edge = scores[:, start:]
        key_pos = lax.broadcasted_iota(jnp.int32, edge.shape, 1)
        allowed = key_pos <= lax.broadcasted_iota(jnp.int32, edge.shape, 0)
        if start < LONGEST_PREFIX:
            allowed = allowed | (key_pos < prefix - start)
        edge = jnp.where(allowed, edge, -1e30)
        scores = jnp.concatenate([scores[:, :start], edge], 1) if start else edge
        peak = jnp.max(scores, -1, keepdims=True)
        weights = jnp.exp(scores - peak).astype(LOW)
        own = owned[head].astype(WIDE).astype(LOW)
        values = value_ref[: key_extent(block), :] * own + ones[head].astype(WIDE).astype(LOW)
        mixed = dot_nn(weights, values)
        total = jnp.sum(jnp.where(ones[head], mixed, 0.0), -1, keepdims=True)
        mixed = jnp.where(owned[head], mixed * (1.0 / total), 0.0)
        sum_ref[rows, :] = mixed if head == 0 else sum_ref[rows, :] + mixed
        total_ref[rows, :] = jnp.where(
            total_lane == group * PACK + head, peak + jnp.log(total), total_ref[rows, :]
        )

    ahead = score(*items[0])
    for index, item in enumerate(items):
        scores = ahead
        if index + 1 < len(items):
            ahead = score(*items[index + 1])
        attend(*item, scores)
    heads = sum_ref[...].astype(LOW)
    head_ref[...] = heads
    middle_ref[...] += dot_nt(heads, w_ref[:, 3 * GROUP :])

    @pl.when(group == pl.num_programs(0) - 1)
    def _():
        middle = middle_ref[...]
        scale = lax.rsqrt(jnp.mean(middle * middle, -1, keepdims=True) + NORM_EPSILON)
        branch_ref[...] = (middle * scale * gain_ref[1:2, :]).astype(LOW)


def attend_forward(prefix, tokens, gains, cos, sin, w_attn, after):
    length, width = tokens.shape
    low = lambda columns: jax.ShapeDtypeStruct((length, columns), LOW)
    grouped = pl.BlockSpec((length, GROUP), lambda group: (0, group))
    return pl.pallas_call(
        ignoring(attend_forward_kernel, 6, len(after)),
        grid=(GROUPS,),
        out_shape=[
            low(width), low(width), low(width), low(width),
            jax.ShapeDtypeStruct((length, 128), WIDE),
            low(width),
            jax.ShapeDtypeStruct((length, width), WIDE),
            low(width),
        ],
        in_specs=[
            pl.BlockSpec(memory_space=pltpu.SMEM),
            once(tokens.shape),
            once(gains.shape),
            once(cos.shape),
            once(sin.shape),
            pl.BlockSpec((width, 4 * GROUP), lambda group: (0, group)),
        ]
        + [ANYWHERE] * len(after),
        out_specs=[
            grouped, grouped, grouped, grouped,
            whole((length, 128)),
            whole((length, width)),
            whole((length, width)),
            whole((length, width)),
        ],
        scratch_shapes=[pltpu.VMEM((length, GROUP), WIDE)],
        compiler_params=params(),
        cost_estimate=pl.CostEstimate(
            flops=25_000_000_000, bytes_accessed=20_000_000, transcendentals=9_000_000
        ),
    )(prefix, tokens, gains, cos, sin, w_attn, *after)


def attend_backward_kernel(
    prefix_ref, query_ref, key_ref, value_ref, head_ref, total_ref, cos_ref, sin_ref,
    normed_t_ref, grad_ref, grad_t_ref, w_ref, grad_w_ref, grad_normed_ref,
    total_t_ref, scaled_ref, key_t_ref, grad_head_ref, center_ref,
    probs_ref, grad_scores_ref, grad_query_t_ref, grad_key_ref, grad_value_ref,
):
    step = pl.program_id(0)
    length = query_ref.shape[0]

    @pl.when(step == 0)
    def _():
        total_t_ref[...] = total_ref[...].T
        grad_normed_ref[...] = jnp.zeros_like(grad_normed_ref)

    scaled_ref[...] = query_ref[...] * HEAD_DIM ** (-0.5)
    key_t = key_ref[...].T
    for head in range(PACK):
        for half in range(2):
            first = half * 128 + head * HALF
            key_t_ref[head, half * HALF : (half + 1) * HALF, :] = key_t[first : first + HALF]
    grad_heads = dot_nn(grad_ref[...], w_ref[:, 3 * GROUP :]).astype(LOW)
    grad_head_ref[...] = grad_heads
    product = grad_heads.astype(WIDE) * head_ref[...].astype(WIDE)
    leading = product.astype(LOW)
    rest = (product - leading.astype(WIDE)).astype(LOW)
    head_row = lax.broadcasted_iota(jnp.int32, (16, GROUP), 0)
    select = (chunk_of((16, GROUP)) == head_row).astype(WIDE).astype(LOW)
    center_ref[...] = dot_nt(select, leading) + dot_nt(select, rest)
    prefix = prefix_ref[0]
    owned = [(chunk_of((1, GROUP)) == head).astype(WIDE).astype(LOW) for head in range(PACK)]
    items = [(head, block) for head in range(PACK) for block in range(length // BLOCK)]

    def score(head, block):
        rows = slice(block * BLOCK, (block + 1) * BLOCK)
        extent = key_extent(block)
        return (
            dot_nt(key_ref[:extent, :], scaled_ref[rows, :] * owned[head]),
            dot_nt(value_ref[:extent, :], grad_head_ref[rows, :] * owned[head]),
        )

    def weigh(head, block, scores, grad_probs):
        start, extent = block * BLOCK, key_extent(block)
        rows = slice(start, start + BLOCK)
        totals = total_t_ref[pl.ds(step * PACK + head, 1), rows]
        probs = jnp.exp(scores - totals)
        edge = probs[start:, :]
        key_pos = lax.broadcasted_iota(jnp.int32, edge.shape, 0)
        allowed = key_pos <= lax.broadcasted_iota(jnp.int32, edge.shape, 1)
        if start < LONGEST_PREFIX:
            allowed = allowed | (key_pos < prefix - start)
        edge = jnp.where(allowed, edge, 0.0)
        probs = jnp.concatenate([probs[:start, :], edge], 0) if start else edge
        grad_scores = (probs * (grad_probs - center_ref[head : head + 1, rows])).astype(LOW)
        probs_ref[head % 2, :extent, rows] = probs.astype(LOW)
        grad_scores_ref[head % 2, :extent, rows] = grad_scores
        grad_query_t = dot_nn(key_t_ref[head, :, :extent], grad_scores)
        for half in range(2):
            first = half * 128 + head * HALF
            grad_query_t_ref[first : first + HALF, rows] = grad_query_t[
                half * HALF : (half + 1) * HALF
            ]

    def gather_keys(head):
        queries, grads = scaled_ref[...] * owned[head], grad_head_ref[...] * owned[head]
        first = 0
        while first < length:
            seen = 0 if first < LONGEST_PREFIX else first
            keys = slice(first, LONGEST_PREFIX if first < LONGEST_PREFIX else first + BLOCK)
            for ref, source, right in (
                (grad_value_ref, probs_ref, grads),
                (grad_key_ref, grad_scores_ref, queries),
            ):
                part = dot_nn(source[head % 2, keys, seen:], right[seen:, :])
                ref[keys, :] = part if head == 0 else ref[keys, :] + part
            first = keys.stop

    ahead = score(*items[0])
    for index, (head, block) in enumerate(items):
        scores = ahead
        if index + 1 < len(items):
            ahead = score(*items[index + 1])
        weigh(head, block, *scores)
        if (block + 1) * BLOCK == length:
            gather_keys(head)
    cos, sin = cos_ref[...], sin_ref[...]
    pieces = []
    for grad in (grad_query_t_ref[...].T * HEAD_DIM ** (-0.5), grad_key_ref[...]):
        lead, tail = grad[:, :128], grad[:, 128:]
        pieces.append((lead * cos + tail * sin).astype(LOW))
        pieces.append((tail * cos - lead * sin).astype(LOW))
    pieces.append(grad_value_ref[...].astype(LOW))
    grads = jnp.concatenate(pieces, 1)
    grad_w_ref[:, : 3 * GROUP] = dot_nn(side_by_side(normed_t_ref), grads).astype(LOW)
    grad_w_ref[:, 3 * GROUP :] = dot_nn(side_by_side(grad_t_ref), head_ref[...]).astype(LOW)
    grad_normed_ref[...] += dot_nt(grads, w_ref[:, : 3 * GROUP])


def attend_backward(
    prefix, query, key, value, heads, totals, cos, sin, normed_t, grad, grad_t, w_attn
):
    length, width = grad.shape
    grouped = pl.BlockSpec((length, GROUP), lambda step: (0, step))
    return pl.pallas_call(
        attend_backward_kernel,
        grid=(GROUPS,),
        out_shape=[
            jax.ShapeDtypeStruct((width, GROUPS * 4 * GROUP), LOW),
            jax.ShapeDtypeStruct((length, width), WIDE),
        ],
        in_specs=[
            pl.BlockSpec(memory_space=pltpu.SMEM),
            grouped, grouped, grouped, grouped,
            once(totals.shape), once(cos.shape), once(sin.shape), once(normed_t.shape),
            once(grad.shape), once(grad_t.shape),
            pl.BlockSpec((width, 4 * GROUP), lambda step: (0, step)),
        ],
        out_specs=[
            pl.BlockSpec((width, 4 * GROUP), lambda step: (0, step)),
            whole((length, width)),
        ],
        scratch_shapes=[
            pltpu.VMEM((128, length), WIDE),
            pltpu.VMEM((length, GROUP), LOW),
            pltpu.VMEM((PACK, HEAD_DIM, length), LOW),
            pltpu.VMEM((length, GROUP), LOW),
            pltpu.VMEM((16, length), WIDE),
            pltpu.VMEM((2, length, length), LOW),
            pltpu.VMEM((2, length, length), LOW),
            pltpu.VMEM((GROUP, length), WIDE),
            pltpu.VMEM((length, GROUP), WIDE),
            pltpu.VMEM((length, GROUP), WIDE),
        ],
        compiler_params=params(),
        cost_estimate=AT_ONCE,
    )(prefix, query, key, value, heads, totals, cos, sin, normed_t, grad, grad_t, w_attn)


def swiglu_blocks(blocks, rows_of, w_gu_ref, w_d_ref, act_ref, grad_act_ref, sum_ref, grad_sum_ref):
    subs = w_d_ref.shape[0] // HIDDEN_BLOCK
    items = [(block, sub) for block in range(blocks) for sub in range(subs)]

    def into(block, sub):
        _, tokens, grads_in = rows_of(block)
        units = slice(sub * HIDDEN_BLOCK, (sub + 1) * HIDDEN_BLOCK)
        both = slice(2 * sub * HIDDEN_BLOCK, 2 * (sub + 1) * HIDDEN_BLOCK)
        return dot_nn(tokens, w_gu_ref[:, both]), dot_nt(grads_in, w_d_ref[units, :])

    def middle(block, sub, gate_up, grad_hidden):
        rows, _, _ = rows_of(block)
        units = slice(sub * HIDDEN_BLOCK, (sub + 1) * HIDDEN_BLOCK)
        both = slice(2 * sub * HIDDEN_BLOCK, 2 * (sub + 1) * HIDDEN_BLOCK)
        gate, up = gate_up[:, :HIDDEN_BLOCK], gate_up[:, HIDDEN_BLOCK:]
        sig = 0.5 * jnp.tanh(0.5 * gate) + 0.5
        act = gate * sig
        act_ref[rows, units] = (act * up).astype(LOW)
        grad_act_ref[rows, both] = jnp.concatenate(
            [
                (grad_hidden * up * (sig + act * (1.0 - sig))).astype(LOW),
                (grad_hidden * act).astype(LOW),
            ],
            1,
        )

    def out(block):
        rows, _, _ = rows_of(block)
        sum_ref[rows, :] += dot_nn(act_ref[rows, :], w_d_ref[...])
        grad_sum_ref[rows, :] += dot_nt(grad_act_ref[rows, :], w_gu_ref[...])

    ahead = into(*items[0])
    for index, item in enumerate(items):
        products = ahead
        if index + 1 < len(items):
            ahead = into(*items[index + 1])
        middle(*item, *products)
        if item[1] == subs - 1:
            out(item[0])


def swiglu_kernel(parts, rows_ref, grad_ref, rows_t_ref, grad_t_ref, *refs):
    w_gu_refs, w_d_refs, refs = refs[:parts], refs[parts : 2 * parts], refs[2 * parts :]
    out_ref, grad_rows_ref, refs = refs[0], refs[1], refs[2:]
    grad_gu_refs, grad_d_refs = refs[0 : 2 * parts : 2], refs[1 : 2 * parts : 2]
    act_ref, grad_act_ref = refs[2 * parts :]
    step = pl.program_id(0)
    count = rows_ref.shape[0]
    per_part = pl.num_programs(0) // parts

    @pl.when(step == 0)
    def _():
        out_ref[...] = jnp.zeros_like(out_ref)
        grad_rows_ref[...] = jnp.zeros_like(grad_rows_ref)

    def one_part(w_gu_ref, w_d_ref, grad_gu_ref, grad_d_ref):
        def rows_of(block):
            rows = slice(block * ROW_BLOCK, (block + 1) * ROW_BLOCK)
            return rows, rows_ref[rows, :], grad_ref[rows, :]

        swiglu_blocks(
            count // ROW_BLOCK, rows_of, w_gu_ref, w_d_ref, act_ref, grad_act_ref, out_ref,
            grad_rows_ref,
        )
        grad_gu_ref[...] = dot_nn(side_by_side(rows_t_ref), grad_act_ref[...]).astype(LOW)
        grad_d_ref[...] = dot_nn(side_by_side(grad_t_ref), act_ref[...]).astype(LOW).T

    for part in range(parts):
        pl.when(step // per_part == part)(
            functools.partial(
                one_part, w_gu_refs[part], w_d_refs[part], grad_gu_refs[part], grad_d_refs[part]
            )
        )


ROW_BLOCK = 1024
HIDDEN_BLOCK = 256


def swiglu(rows, grad, rows_t, grad_t, w_gu, w_d):
    count, width = rows.shape
    parts = len(w_d)
    hidden = w_d[0].shape[0]
    chunk = EXPERT_BLOCK
    per_part = hidden // chunk

    def place(part):
        return lambda step: jnp.clip(step - part * per_part, 0, per_part - 1)

    gu_specs = [
        pl.BlockSpec((width, 2 * chunk), lambda step, at=place(part): (0, at(step)))
        for part in range(parts)
    ]
    d_specs = [
        pl.BlockSpec((chunk, width), lambda step, at=place(part): (at(step), 0))
        for part in range(parts)
    ]
    gu_shape = jax.ShapeDtypeStruct((width, 2 * hidden), LOW)
    d_shape = jax.ShapeDtypeStruct((hidden, width), LOW)
    total = parts * hidden
    return pl.pallas_call(
        functools.partial(swiglu_kernel, parts),
        grid=(parts * per_part,),
        out_shape=[jax.ShapeDtypeStruct((count, width), WIDE)] * 2 + [gu_shape, d_shape] * parts,
        in_specs=[once(each.shape) for each in (rows, grad, rows_t, grad_t)] + gu_specs + d_specs,
        out_specs=[whole((count, width))] * 2
        + [spec for pair in zip(gu_specs, d_specs) for spec in pair],
        scratch_shapes=[
            pltpu.VMEM((count, chunk), LOW),
            pltpu.VMEM((count, 2 * chunk), LOW),
        ],
        compiler_params=params(),
        cost_estimate=pl.CostEstimate(
            flops=18 * count * width * total,
            bytes_accessed=12 * width * total + 12 * count * width,
            transcendentals=count * total,
        ),
    )(rows, grad, rows_t, grad_t, *w_gu, *w_d)


def wait_all(values, *others):
    count = len(values)
    anywhere = pl.BlockSpec(memory_space=pl.ANY)
    return pl.pallas_call(
        lambda *refs: None,
        out_shape=[jax.ShapeDtypeStruct(value.shape, value.dtype) for value in values],
        in_specs=[anywhere] * (count + len(others)),
        out_specs=[anywhere] * count,
        input_output_aliases={index: index for index in range(count)},
        cost_estimate=AT_ONCE,
    )(*values, *others)


def wait_for(value, *others):
    return wait_all([value], *others)[0]


def pair_gates(chosen):
    peak = functools.reduce(jnp.maximum, chosen)
    weights = [jnp.exp(each - peak) for each in chosen]
    total = sum(weights[1:], weights[0])
    return [each / total for each in weights]


def dispatch_kernel(
    here_ref, route_ref, target_ref, branch_ref, grad_ref, router_ref, *refs
):
    partner = pl.program_id(0)
    partners = (len(refs) - 3) // 2
    turned_refs, gate_ref = refs[-3:-1], refs[-1]
    top, count = route_ref.shape
    half = refs[0].shape[1]
    capacity = 2 * half

    @pl.when(partner == 0)
    def _():
        logits = dot_nt(router_ref[...], branch_ref[...])
        row = lax.broadcasted_iota(jnp.int32, logits.shape, 0)
        chosen = [
            jnp.sum(jnp.where(row == route_ref[pick : pick + 1, :], logits, 0.0), 0, keepdims=True)
            for pick in range(top)
        ]
        for pick, gate in enumerate(pair_gates(chosen)):
            gate_ref[pick : pick + 1, :] = gate

    piece = pl.ds(pl.multiple_of(jnp.minimum(partner, count // BLOCK - 1) * BLOCK, BLOCK), BLOCK)
    for source_ref, turned_ref in zip((branch_ref, grad_ref), turned_refs):
        turned_ref[0] = source_ref[piece, :].T
    expert = here_ref[0] ^ partner
    place = expert * capacity + lax.broadcasted_iota(jnp.int32, (capacity, count), 0)
    spread = jnp.zeros((capacity, count), WIDE)
    gates = jnp.zeros((capacity, count), WIDE)
    for pick in range(top):
        here = target_ref[pick : pick + 1, :] == place
        spread = jnp.where(here, 1.0, spread)
        gates = jnp.where(here, gate_ref[pick : pick + 1, :], gates)
    spread = spread.astype(LOW)
    rows = dot_nn(spread, branch_ref[...]).astype(LOW)
    grads = dot_nn(spread, grad_ref[...])
    grads = (grads * jnp.sum(gates, 1, keepdims=True)).astype(LOW)

    def store(first_ref, second_ref):
        for ref, part in ((first_ref, slice(0, half)), (second_ref, slice(half, capacity))):
            ref[0] = rows[part]
            ref[1] = grads[part]

    for index in range(partners):
        pl.when(partner == index)(
            functools.partial(store, refs[index], refs[partners + index])
        )


def dispatch(here, routes_t, target_t, branch_in, grad, router_t, partners, capacity):
    count, width = branch_in.shape
    top = routes_t.shape[0]
    shape = (2, capacity // 2, width)
    outs = pl.pallas_call(
        dispatch_kernel,
        grid=(partners,),
        out_shape=[jax.ShapeDtypeStruct(shape, LOW)] * (2 * partners)
        + [jax.ShapeDtypeStruct((count // BLOCK, width, BLOCK), LOW)] * 2
        + [jax.ShapeDtypeStruct((top, count), WIDE)],
        in_specs=[
            pl.BlockSpec(memory_space=pltpu.SMEM),
            once(routes_t.shape), once(target_t.shape), once(branch_in.shape), once(grad.shape),
            once(router_t.shape),
        ],
        out_specs=[whole(shape)] * (2 * partners)
        + [
            pl.BlockSpec(
                (1, width, BLOCK), lambda step: (jnp.minimum(step, count // BLOCK - 1), 0, 0)
            )
        ]
        * 2
        + [whole((top, count))],
        compiler_params=params(),
        cost_estimate=pl.CostEstimate(
            flops=4 * partners * capacity * count * width,
            bytes_accessed=4 * (partners * capacity + count) * width,
            transcendentals=0,
        ),
    )(here, routes_t, target_t, branch_in, grad, router_t)
    return outs[:partners], outs[partners : 2 * partners], *outs[2 * partners : -1]


def expert_kernel(sources, *refs):
    rows_refs, refs = refs[:sources], refs[sources:]
    gu_stack_ref, d_stack_ref, refs = refs[0], refs[1], refs[2:]
    out_refs, refs = refs[:sources], refs[sources:]
    act_ref, grad_act_ref, turned_ref, out_sum_ref, grad_sum_ref, w_gu_ref, w_d_ref = refs
    step = pl.program_id(0)
    _, per_source, width = rows_refs[0].shape
    block = max(1, ROW_BLOCK // per_source)
    count = block * per_source

    @pl.when(step == 0)
    def _():
        out_sum_ref[...] = jnp.zeros_like(out_sum_ref)
        grad_sum_ref[...] = jnp.zeros_like(grad_sum_ref)

    for stack_ref, w_ref in ((gu_stack_ref, w_gu_ref), (d_stack_ref, w_d_ref)):
        columns = w_ref.shape[1] // 256
        tall = stack_ref.shape[1] // columns
        for column in range(columns):
            w_ref[:, column * 256 : (column + 1) * 256] = stack_ref[
                :, column * tall : (column + 1) * tall, :
            ].reshape(w_ref.shape[0], 256)

    def gather(index, member):
        return jnp.concatenate(
            [ref[member] for ref in rows_refs[index * block : (index + 1) * block]], 0
        )

    def rows_of(index):
        return slice(index * count, (index + 1) * count), gather(index, 0), gather(index, 1)

    swiglu_blocks(
        sources // block, rows_of, w_gu_ref, w_d_ref, act_ref, grad_act_ref, out_sum_ref,
        grad_sum_ref,
    )
    for piece in range(2 * (sources // block)):

        @pl.when(step == piece)
        def _():
            turned_ref[0, 0] = gather(piece % (sources // block), piece // (sources // block)).T

    @pl.when(step == pl.num_programs(0) - 1)
    def _():
        for index, ref in enumerate(out_refs):
            rows = slice(index * per_source, (index + 1) * per_source)
            ref[0] = out_sum_ref[rows, :].astype(LOW)
            ref[1] = grad_sum_ref[rows, :].astype(LOW)


EXPERT_BLOCK = 512


def expert_pass(rows, stack, after):
    sources = len(rows)
    _, per_source, width = rows[0].shape
    count = sources * per_source
    devices = stack.shape[0]
    chunk = EXPERT_BLOCK
    hidden = FF
    steps = hidden // chunk
    gu_tall = 2 * chunk // 256 * (width // devices)
    d_tall = width // 256 * (hidden // devices)
    blocks = 2 * count // ROW_BLOCK
    assert steps >= blocks and gu_tall * steps % d_tall == 0
    outs = pl.pallas_call(
        ignoring(functools.partial(expert_kernel, sources), sources + 2, len(after)),
        grid=(steps,),
        out_shape=[jax.ShapeDtypeStruct(rows[0].shape, LOW)] * sources
        + [
            jax.ShapeDtypeStruct((count, hidden), LOW),
            jax.ShapeDtypeStruct((count, 2 * hidden), LOW),
            jax.ShapeDtypeStruct((2, blocks // 2, width, ROW_BLOCK), LOW),
        ],
        in_specs=[once(rows[0].shape)] * sources
        + [
            pl.BlockSpec((devices, gu_tall, 256), lambda step: (0, step, 0)),
            pl.BlockSpec(
                (chunk * devices // hidden, d_tall, 256),
                lambda step: (step, gu_tall * steps // d_tall, 0),
            ),
        ]
        + [ANYWHERE] * len(after),
        out_specs=[whole(rows[0].shape)] * sources
        + [
            pl.BlockSpec((count, chunk), lambda step: (0, step)),
            pl.BlockSpec((count, 2 * chunk), lambda step: (0, step)),
            pl.BlockSpec(
                (1, 1, width, ROW_BLOCK),
                lambda step: (
                    jnp.minimum(step, blocks - 1) // (blocks // 2),
                    jnp.minimum(step, blocks - 1) % (blocks // 2),
                    0,
                    0,
                ),
            ),
        ],
        scratch_shapes=[
            pltpu.VMEM((count, width), WIDE),
            pltpu.VMEM((count, width), WIDE),
            pltpu.VMEM((width, 2 * chunk), LOW),
            pltpu.VMEM((chunk, width), LOW),
        ],
        compiler_params=params(),
        cost_estimate=pl.CostEstimate(
            flops=count * width * hidden, bytes_accessed=width * hidden, transcendentals=0
        ),
    )(*rows, stack, stack, *after)
    return outs[:sources], *outs[sources:]


def weight_grad_kernel(halves, turned, *refs):
    row_refs, act_refs, out_ref = refs[:halves], refs[halves : 2 * halves], refs[-1]
    rows_t = jnp.concatenate([side_by_side(ref.at[0]) for ref in row_refs], 1)
    grad = dot_nn(rows_t, jnp.concatenate([ref[...] for ref in act_refs], 0)).astype(LOW)
    out_ref[...] = grad.T if turned else grad


def weight_grad(rows, acts, member, turned, chunk, after):
    halves = len(acts)
    _, blocks, width, _ = rows[0].shape
    count, units = acts[0].shape
    member_spec = pl.BlockSpec(
        (1, blocks, width, ROW_BLOCK),
        lambda step: (member, 0, 0, 0),
        pipeline_mode=pl.Buffered(1),
    )
    return pl.pallas_call(
        ignoring(
            functools.partial(weight_grad_kernel, halves, turned), 2 * halves, len(after)
        ),
        grid=(units // chunk,),
        out_shape=jax.ShapeDtypeStruct((units, width) if turned else (width, units), LOW),
        in_specs=[member_spec] * halves
        + [pl.BlockSpec((count, chunk), lambda step: (0, step))] * halves
        + [ANYWHERE] * len(after),
        out_specs=pl.BlockSpec((chunk, width), lambda step: (step, 0))
        if turned
        else pl.BlockSpec((width, chunk), lambda step: (0, step)),
        compiler_params=params(),
        cost_estimate=pl.CostEstimate(
            flops=count * width * units // 8, bytes_accessed=width * units // 2, transcendentals=0
        ),
    )(*rows, *acts, *after)


def combine_kernel(
    partners, here_ref, route_ref, target_ref, middle_ref, shared_ref, grad_shared_ref,
    cotangent_ref, branch_ref, normed_ref, gain_ref, router_ref, *refs
):
    halves, refs = (refs[:partners], refs[partners : 2 * partners]), refs[2 * partners :]
    out_ref, grad_ref, grad_low_ref, grad_t_ref, normed_t_ref, grad_router_ref, grad_gain_ref = refs
    normed_t_ref[0] = normed_ref[...].T
    block, top = target_ref.shape
    _, half, width = halves[0][0].shape

    @pl.when(pl.program_id(0) == 0)
    def _():
        grad_router_ref[...] = jnp.zeros_like(grad_router_ref)
        grad_gain_ref[...] = jnp.zeros_like(grad_gain_ref)

    branch = branch_ref[...]
    logits = dot_nt(branch, router_ref[...])
    lane = lax.broadcasted_iota(jnp.int32, logits.shape, 1)
    picked_lane = [lane == route_ref[:, pick : pick + 1] for pick in range(top)]
    gates = pair_gates(
        [jnp.sum(jnp.where(here, logits, 0.0), 1, keepdims=True) for here in picked_lane]
    )
    slot = lax.broadcasted_iota(jnp.int32, (1, partners * half), 1)
    slot = ((slot // half) ^ here_ref[0]) * (2 * half) + slot % half
    picked, grad_rows = 0.0, 0.0
    for index, part in enumerate(halves):
        spread = [
            (target_ref[:, pick : pick + 1] == slot + index * half).astype(WIDE)
            for pick in range(top)
        ]
        stacked = jnp.concatenate(spread, 0).astype(LOW)
        outs, grads = (jnp.concatenate([ref[member] for ref in part], 0) for member in range(2))
        picked = picked + dot_nn(stacked, outs)
        grad_rows = grad_rows + dot_nn(sum(spread[1:], spread[0]).astype(LOW), grads)
    picked = [picked[pick * block : (pick + 1) * block] for pick in range(top)]
    middle = middle_ref[...]
    mixed = sum(gate * rows for gate, rows in zip(gates, picked))
    out_ref[...] = (middle + shared_ref[...] + mixed).astype(LOW)
    cotangent = cotangent_ref[...].astype(WIDE)
    grad_gates = [jnp.sum(cotangent * rows, 1, keepdims=True) for rows in picked]
    mean = sum(gate * grad for gate, grad in zip(gates, grad_gates))
    grad_logits = sum(
        jnp.where(here, gate * (grad - mean), 0.0)
        for here, gate, grad in zip(picked_lane, gates, grad_gates)
    ).astype(LOW)
    grad_router_ref[...] += lax.dot_general(
        grad_logits, branch, (((0,), (0,)), ((), ())), preferred_element_type=WIDE
    )
    grad_branch = grad_shared_ref[...] + dot_nn(grad_logits, router_ref[...]) + grad_rows
    scale = lax.rsqrt(jnp.mean(middle * middle, -1, keepdims=True) + NORM_EPSILON)
    hat = middle * scale
    grad_gain_ref[...] += jnp.sum((grad_branch * hat).reshape(block // 8, 8, width), 0)
    grad_hat = grad_branch * gain_ref[1:2, :]
    grad = cotangent + scale * (grad_hat - hat * jnp.mean(grad_hat * hat, -1, keepdims=True))
    grad_ref[...] = grad
    grad_low_ref[...] = grad.astype(LOW)
    grad_t_ref[0] = grad.astype(LOW).T


def combine(
    here, routes, target, first, second, middle, shared_out, grad_shared, cotangent, branch_in,
    normed, gains, router_t, after
):
    count, width = middle.shape
    top = routes.shape[1]
    lanes = router_t.shape[0]
    partners = len(first)
    rows = pl.BlockSpec((BLOCK, width), lambda step: (step, 0))
    pairs = pl.BlockSpec((BLOCK, top), lambda step: (step, 0))
    return pl.pallas_call(
        ignoring(
            functools.partial(combine_kernel, partners), 11 + 2 * partners, len(after)
        ),
        grid=(count // BLOCK,),
        out_shape=[
            jax.ShapeDtypeStruct((count, width), LOW),
            jax.ShapeDtypeStruct((count, width), WIDE),
            jax.ShapeDtypeStruct((count, width), LOW),
            jax.ShapeDtypeStruct((count // BLOCK, width, BLOCK), LOW),
            jax.ShapeDtypeStruct((count // BLOCK, width, BLOCK), LOW),
            jax.ShapeDtypeStruct((lanes, width), WIDE),
            jax.ShapeDtypeStruct((8, width), WIDE),
        ],
        in_specs=[
            pl.BlockSpec(memory_space=pltpu.SMEM),
            pairs, pairs, rows, rows, rows, rows, rows, rows,
            once(gains.shape), once(router_t.shape),
        ]
        + [once(first[0].shape)] * (2 * partners)
        + [ANYWHERE] * len(after),
        out_specs=[
            rows, rows, rows,
            pl.BlockSpec((1, width, BLOCK), lambda step: (step, 0, 0)),
            pl.BlockSpec((1, width, BLOCK), lambda step: (step, 0, 0)),
            whole((lanes, width)), whole((8, width)),
        ],
        compiler_params=params(),
        cost_estimate=pl.CostEstimate(
            flops=400_000_000_000, bytes_accessed=25_000_000, transcendentals=0
        ),
    )(
        here, routes, target, middle, shared_out, grad_shared, cotangent, branch_in, normed,
        gains, router_t, *first, *second, *after
    )


def swiglu_stacks_kernel(
    partners, rings, col_rows, piece, here_ref, rows_ref, grad_ref, rows_t_ref, grad_t_ref, *refs
):
    stacks, refs = refs[: 4 * partners], refs[4 * partners :]
    out_ref, grad_rows_ref, refs = refs[0], refs[1], refs[2:]
    grad_gu_refs, grad_d_refs, refs = refs[0:4:2], refs[1:4:2], refs[4:]
    w_gu_ref, w_d_ref, act_ref, grad_act_ref = refs
    step = pl.program_id(0)
    count = rows_ref.shape[0]
    per_part = pl.num_programs(0) // 2
    device_cols, device_rows = rings * col_rows, rings * piece
    together = w_d_ref.shape[0] // device_rows

    @pl.when(step == 0)
    def _():
        out_ref[...] = jnp.zeros_like(out_ref)
        grad_rows_ref[...] = jnp.zeros_like(grad_rows_ref)

    def place(gu_ref, d_ref, device):
        for ring in range(rings):
            first = pl.multiple_of(device * device_cols + ring * col_rows, 16)
            for column in range(w_gu_ref.shape[1] // 256):
                w_gu_ref[pl.ds(first, col_rows), column * 256 : (column + 1) * 256] = gu_ref[
                    ring, column * col_rows : (column + 1) * col_rows, :
                ]

        @pl.when(device // together == step % per_part)
        def _():
            for ring in range(rings):
                first = pl.multiple_of(device % together * device_rows + ring * piece, 16)
                for column in range(w_d_ref.shape[1] // 256):
                    w_d_ref[pl.ds(first, piece), column * 256 : (column + 1) * 256] = d_ref[
                        ring, column * piece : (column + 1) * piece, :
                    ]

    for part in range(2):

        @pl.when(step // per_part == part)
        def _():
            for index in range(partners):
                at = 2 * (part * partners + index)
                place(stacks[at], stacks[at + 1], here_ref[0] ^ index)

    def rows_of(block):
        rows = slice(block * ROW_BLOCK, (block + 1) * ROW_BLOCK)
        return rows, rows_ref[rows, :], grad_ref[rows, :]

    swiglu_blocks(
        count // ROW_BLOCK, rows_of, w_gu_ref, w_d_ref, act_ref, grad_act_ref, out_ref,
        grad_rows_ref,
    )
    grad_gu = dot_nn(side_by_side(rows_t_ref), grad_act_ref[...]).astype(LOW)
    grad_d = dot_nn(side_by_side(grad_t_ref), act_ref[...]).astype(LOW).T
    for part in range(2):

        @pl.when(step // per_part == part)
        def _():
            grad_gu_refs[part][...] = grad_gu
            grad_d_refs[part][...] = grad_d


def swiglu_stacks(
    here, rows, grad, rows_t, grad_t, near, far, rings, col_rows, piece, after
):
    count, width = rows.shape
    partners = len(near)
    chunk = EXPERT_BLOCK
    hidden = partners * rings * piece
    per_part = hidden // chunk
    gu_tall, d_tall = 2 * chunk // 256 * col_rows, width // 256 * piece
    assert gu_tall * per_part % d_tall == 0

    def place(part):
        return lambda step: jnp.clip(step - part * per_part, 0, per_part - 1)

    operands, stack_specs, out_specs = [], [], []
    for part, stacks in enumerate((near, far)):
        for stack in stacks:
            operands += [stack.reshape(rings, -1, 256)] * 2
            stack_specs += [
                pl.BlockSpec(
                    (rings, gu_tall, 256), lambda step, at=place(part): (0, at(step), 0)
                ),
                pl.BlockSpec(
                    (rings, d_tall, 256),
                    lambda step: (0, gu_tall * per_part // d_tall, 0),
                    pipeline_mode=pl.Buffered(1),
                ),
            ]
        out_specs += [
            pl.BlockSpec((width, 2 * chunk), lambda step, at=place(part): (0, at(step))),
            pl.BlockSpec((chunk, width), lambda step, at=place(part): (at(step), 0)),
        ]
    kernel = functools.partial(swiglu_stacks_kernel, partners, rings, col_rows, piece)
    return pl.pallas_call(
        ignoring(kernel, 5 + 4 * partners, len(after)),
        grid=(2 * per_part,),
        out_shape=[jax.ShapeDtypeStruct((count, width), WIDE)] * 2
        + [
            jax.ShapeDtypeStruct((width, 2 * hidden), LOW),
            jax.ShapeDtypeStruct((hidden, width), LOW),
        ]
        * 2,
        in_specs=[pl.BlockSpec(memory_space=pltpu.SMEM)]
        + [once(each.shape) for each in (rows, grad, rows_t, grad_t)]
        + stack_specs
        + [ANYWHERE] * len(after),
        out_specs=[whole((count, width))] * 2 + out_specs,
        scratch_shapes=[
            pltpu.VMEM((width, 2 * chunk), LOW),
            pltpu.VMEM((chunk, width), LOW),
            pltpu.VMEM((count, chunk), LOW),
            pltpu.VMEM((count, 2 * chunk), LOW),
        ],
        compiler_params=params(),
        cost_estimate=pl.CostEstimate(
            flops=36 * count * width * hidden,
            bytes_accessed=24 * width * hidden + 12 * count * width,
            transcendentals=2 * count * hidden,
        ),
    )(here, rows, grad, rows_t, grad_t, *operands, *after)


def pack_grads_kernel(rings, col_rows, piece, here_ref, *refs):
    grad_refs, out_refs = refs[:4], refs[4:]

    def place(out_ref):
        for ring in range(rings):
            first = 0
            for near, far, rows in ((*grad_refs[:2], col_rows), (*grad_refs[2:], piece)):
                for column in range(near.shape[1] // 256):
                    part = (
                        slice(ring * rows, (ring + 1) * rows),
                        slice(column * 256, (column + 1) * 256),
                    )
                    out_ref[ring, first : first + rows, :] = (
                        near[part].astype(WIDE) + far[part].astype(WIDE)
                    ).astype(LOW)
                    first += rows

    for index, out_ref in enumerate(out_refs):
        pl.when(pl.program_id(0) == index)(functools.partial(place, out_ref))


def pack_grads(here, partners, near, far, rings, col_rows, piece):
    grads = [near[0], far[0], near[1], far[1]]
    specs = [
        pl.BlockSpec(
            (grad.shape[0] // partners, grad.shape[1]), lambda step, here: (here[0] ^ step, 0)
        )
        for grad in grads
    ]
    rows = sum(grad.shape[0] // partners * grad.shape[1] for grad in grads[::2]) // (256 * rings)
    shape = (rings, rows, 256)
    outs = pl.pallas_call(
        functools.partial(pack_grads_kernel, rings, col_rows, piece),
        grid_spec=pltpu.PrefetchScalarGridSpec(
            num_scalar_prefetch=1,
            grid=(partners,),
            in_specs=specs,
            out_specs=[whole(shape)] * partners,
        ),
        out_shape=[jax.ShapeDtypeStruct(shape, LOW)] * partners,
        compiler_params=params(),
        cost_estimate=pl.CostEstimate(flops=0, bytes_accessed=20_000_000, transcendentals=0),
    )(here, *grads)
    return [out.reshape(rings * rows, 256) for out in outs]


def adam_update(weight, first_state, second_state, gradient, step_rate, decay_rate):
    first_new = FIRST_BETA * first_state + (1.0 - FIRST_BETA) * gradient
    second_new = SECOND_BETA * second_state + (1.0 - SECOND_BETA) * gradient * gradient
    first_hat = first_new / (1.0 - FIRST_BETA**STEP)
    second_hat = second_new / (1.0 - SECOND_BETA**STEP)
    weight_new = weight - step_rate * (
        first_hat / (jnp.sqrt(second_hat) + ADAM_EPSILON) + decay_rate * weight
    )
    return (weight_new, first_new, second_new)


def update_kind(state_refs, new_refs, gradient):
    updated = adam_update(*(ref[0] for ref in state_refs), gradient, RATE_MATRIX, WEIGHT_DECAY)
    for ref, value in zip(new_refs, updated):
        ref[0] = value


def expert_update_kernel(gu_ref, down_ref, *refs):
    state_refs, new_refs, rows_ref = refs[:3], refs[3:6], refs[6]

    def one_kind(kind):
        grad_ref = gu_ref if kind < 2 else down_ref
        columns = state_refs[0].shape[1] // grad_ref.shape[0]
        for column in range(columns):
            left = column * 128
            if kind < 2:
                left = (column // 2 * 2 + kind) * 256 + column % 2 * 128
            rows_ref[pl.ds(column, grad_ref.shape[0], stride=columns), :] = grad_ref[
                :, left : left + 128
            ].astype(WIDE)
        update_kind(state_refs, new_refs, rows_ref[...])

    for kind in range(3):
        pl.when(pl.program_id(0) == kind)(functools.partial(one_kind, kind))


def shared_update_kernel(own_rows, piece, grad_ref, *refs):
    state_refs, new_refs, wide_ref, rows_ref = refs[:3], refs[3:6], refs[6], refs[7]
    blocks = FFS // 256

    def gate_or_up(kind):
        columns = FFS // 128
        lane = lax.broadcasted_iota(jnp.int32, (own_rows, 128), 1)
        for column in range(columns):
            unit = column * piece
            left = unit % 256 // 128 * 128
            low, high = (
                wide_ref[pl.ds((half * blocks + unit // 256 * 2 + kind) * own_rows, own_rows),
                         left : left + 128]
                for half in range(2)
            )
            if unit % 128:
                low = pltpu.roll(low, 64, 1)
            else:
                high = pltpu.roll(high, 64, 1)
            rows_ref[pl.ds(column, own_rows, stride=columns), :] = jnp.where(
                lane < piece, low, high
            )

    def down():
        columns = HEADS * HEAD_DIM // 128
        for column in range(columns):
            first = 2 * blocks * own_rows + column // 2 * piece
            left = column % 2 * 128
            rows_ref[pl.ds(column, piece, stride=columns), :] = wide_ref[
                first : first + piece, left : left + 128
            ]

    @pl.when(pl.program_id(0) == 0)
    def _():
        wide_ref[...] = grad_ref[...].astype(WIDE)

    for kind, place in enumerate(
        (functools.partial(gate_or_up, 0), functools.partial(gate_or_up, 1), down)
    ):

        @pl.when(pl.program_id(0) == kind)
        def _():
            place()
            update_kind(state_refs, new_refs, rows_ref[...])


def update(kernel, grads, states, scratch):
    kinds, rows, _ = states[0].shape
    block = pl.BlockSpec((1, rows, 128), lambda kind: (kind, 0, 0))
    return pl.pallas_call(
        kernel,
        grid=(kinds,),
        out_shape=[jax.ShapeDtypeStruct(states[0].shape, WIDE)] * 3,
        in_specs=[once(grad.shape) for grad in grads] + [block] * 3,
        out_specs=[block] * 3,
        scratch_shapes=scratch + [pltpu.VMEM((rows, 128), WIDE)],
        compiler_params=params(),
        cost_estimate=AT_ONCE,
    )(*grads, *states)


def expert_update(gu, down, states):
    return update(expert_update_kernel, [gu, down], states, [])


def shared_update(grad, own_rows, piece, states):
    kernel = functools.partial(shared_update_kernel, own_rows, piece)
    return update(kernel, [grad], states, [pltpu.VMEM(grad.shape, WIDE)])


def slot_place(owners, own_count, owner_count):
    onehot = (owners[:, None] == jnp.arange(owner_count, dtype=jnp.int32)[None, :]).astype(
        jnp.int32
    )
    prior_count = jnp.sum((jnp.cumsum(onehot, 0) - onehot) * onehot, 1)
    return owners * own_count + prior_count


def rope_tables(length):
    inv_freq = ROPE_BASE ** (-(jnp.arange(HALF, dtype=WIDE) * 2.0 / HEAD_DIM))
    phase_angle = jnp.arange(length, dtype=WIDE)[:, None] * inv_freq[None, :]
    return (jnp.tile(jnp.cos(phase_angle), (1, PACK)), jnp.tile(jnp.sin(phase_angle), (1, PACK)))


def rms_scale(values):
    return lax.rsqrt(jnp.mean(values * values, -1, keepdims=True) + NORM_EPSILON)


def norm_back(grad_normed, hat_values, rms_values, gain):
    grad_hat = grad_normed * gain
    return rms_values * (grad_hat - hat_values * jnp.mean(grad_hat * hat_values, -1, keepdims=True))


SHARD = ("ring", "core")
EVERY = ("expert", "ring", "core")


def to_partner(value, axis, distance):
    size = lax.axis_size(axis)
    return lax.ppermute(value, axis, [(index, index ^ distance) for index in range(size)])


def exchange(values, axis):
    return [values[0]] + [
        to_partner(value, axis, distance) for distance, value in enumerate(values) if distance
    ]


def collect(value, axis):
    return exchange([value] * lax.axis_size(axis), axis)


def add_up(value, axes):
    for axis in axes:
        distance = 1
        while distance < lax.axis_size(axis):
            value = value + to_partner(value, axis, distance)
            distance *= 2
    return value


def gather_rows(part, axes):
    return lax.all_gather(part, axes, axis=0, tiled=True)


def scatter_rows(grad, axes):
    return lax.psum_scatter(grad, axes, scatter_dimension=0, tiled=True)


def to_sibling(value):
    return to_partner(value, "core", 1)


def sum_low(parts):
    return sum((part.astype(WIDE) for part in parts[1:]), parts[0].astype(WIDE)).astype(LOW)


def interleave(gate, up):
    rows, hidden = gate.shape
    blocks = (rows, hidden // HIDDEN_BLOCK, HIDDEN_BLOCK)
    return jnp.concatenate([gate.reshape(blocks), up.reshape(blocks)], 2).reshape(rows, 2 * hidden)


def deinterleave(both):
    rows, columns = both.shape
    blocks = both.reshape(rows, columns // (2 * HIDDEN_BLOCK), 2 * HIDDEN_BLOCK)
    return (
        blocks[:, :, :HIDDEN_BLOCK].reshape(rows, columns // 2),
        blocks[:, :, HIDDEN_BLOCK:].reshape(rows, columns // 2),
    )


def by_core(columns, piece):
    rows, hidden = columns.shape
    return (
        columns.reshape(rows, hidden // (2 * piece), 2, piece)
        .transpose(0, 2, 1, 3)
        .reshape(rows, 2, hidden // 2)
    )


def from_core(columns, piece):
    rows, _, half = columns.shape
    return (
        columns.reshape(rows, 2, half // piece, piece).transpose(0, 2, 1, 3).reshape(rows, 2 * half)
    )


def pack(columns, rows):
    return jnp.concatenate(
        [
            part.reshape(part.shape[0], -1, 256).transpose(1, 0, 2).reshape(-1, 256)
            for part in (columns, rows)
        ],
        0,
    )


def unpack(stack, col_rows, piece):
    per_device = FFS // 256 * col_rows
    stack = stack.reshape(-1, per_device + piece * HEADS * HEAD_DIM // 256, 256)
    devices = stack.shape[0]
    return [
        part.reshape(devices, -1, rows, 256)
        .transpose(0, 2, 1, 3)
        .reshape(devices * rows, -1)
        for part, rows in ((stack[:, :per_device], col_rows), (stack[:, per_device:], piece))
    ]


def body(
    tokens_in,
    cotangent,
    routes,
    prefix,
    owners,
    attn_master,
    attn_first,
    attn_second,
    expert_master,
    expert_first,
    expert_second,
    shared_master,
    shared_first,
    shared_second,
    norm_gains,
    gains_first,
    gains_second,
    router,
    router_first,
    router_second,
):
    tok_count, model_width = tokens_in.shape
    owner_count = lax.axis_size("expert")
    own_count = attn_master.shape[0]
    experts_all = router.shape[1]
    top_count = routes.shape[1]
    capacity = tok_count * top_count // experts_all

    here = lax.axis_index("expert")
    here_ref = here.astype(jnp.int32)[None]
    core = lax.axis_index("core")
    rings = lax.axis_size("ring")
    slot_of = slot_place(owners, own_count, owner_count)
    slot_of = (slot_of // own_count ^ here) * own_count + slot_of % own_count
    attn_cols = gather_columns(
        jnp.concatenate(collect(attn_master.astype(LOW), "expert"), 0), slot_of
    )
    w_attn = gather_rows(attn_cols, SHARD)
    expert_columns = interleave(
        expert_master[0, 0].reshape(-1, FF).astype(LOW),
        expert_master[0, 1].reshape(-1, FF).astype(LOW),
    )
    expert_rows = expert_master[0, 2].reshape(-1, model_width).astype(LOW)
    expert_stack = gather_rows(pack(expert_columns, expert_rows)[None], SHARD)
    shared_down = shared_master[2].reshape(-1, model_width).astype(LOW)
    piece = shared_down.shape[0]
    gate_cols = by_core(shared_master[0].reshape(-1, FFS).astype(LOW), piece)
    up_cols = by_core(shared_master[1].reshape(-1, FFS).astype(LOW), piece)
    halves = [interleave(gate_cols[:, half], up_cols[:, half]) for half in range(2)]
    shared_rows = 2 * halves[0].shape[0]
    own_half = jnp.where(core == 0, halves[0], halves[1])
    far_half = to_sibling(jnp.where(core == 0, halves[1], halves[0]))
    near_gu = jnp.where(
        core == 0,
        jnp.concatenate([own_half, far_half], 0),
        jnp.concatenate([far_half, own_half], 0),
    )
    shared_packs = collect(gather_rows(pack(near_gu, shared_down), "ring"), "expert")
    whole_tiles = shared_rows % 16 == 0 and piece % 16 == 0

    router_low = router.astype(LOW)
    flat_ids = routes.reshape(-1)
    onehot = (flat_ids[:, None] == jnp.arange(experts_all, dtype=jnp.int32)[None, :]).astype(
        jnp.int32
    )
    slot_rank = jnp.sum((jnp.cumsum(onehot, 0) - onehot) * onehot, 1)
    target_row = jnp.where(
        slot_rank < capacity, flat_ids * capacity + slot_rank, experts_all * capacity
    ).reshape(tok_count, top_count)
    router_rows = jnp.zeros((128, model_width), LOW).at[:experts_all].set(router_low.T)

    cos, sin = rope_tables(tok_count)
    target_t = target_row.T
    query, key, value, heads, totals, normed, middle, branch_in = attend_forward(
        prefix, tokens_in, norm_gains, cos, sin, w_attn, [target_t, router_rows]
    )

    first_send, second_send, branch_t, cotangent_t = dispatch(
        here_ref, routes.T, target_t, branch_in, cotangent, router_rows[:16], owner_count,
        capacity,
    )
    first_rows = exchange(first_send, "expert")
    second_rows = exchange(second_send, "expert")
    turned_pair = [branch_in, cotangent, branch_t, cotangent_t]
    if whole_tiles:
        near_packs = wait_all(shared_packs, totals)
        far_packs = [to_sibling(stack) for stack in near_packs]
        shared_outs = swiglu_stacks(
            here_ref, *turned_pair, near_packs, far_packs, rings, shared_rows, piece, []
        )
    else:
        order = jnp.arange(owner_count) ^ here
        w_sgu, w_sd = unpack(
            jnp.take(jnp.stack(shared_packs), order, axis=0), shared_rows, piece
        )
        shared_outs = swiglu(
            *turned_pair, [w_sgu, to_sibling(w_sgu)], [w_sd, to_sibling(w_sd)]
        )
    shared_out, grad_branch_shared, grad_sgu, grad_sd, grad_sgu_far, grad_sd_far = shared_outs
    first_out, first_act, first_grad_act, first_turned = expert_pass(
        first_rows, expert_stack, [grad_branch_shared]
    )
    first_back = exchange(first_out, "expert")
    second_out, second_act, second_grad_act, second_turned = expert_pass(
        second_rows, expert_stack, [first_act]
    )
    second_back = exchange(second_out, "expert")
    far = [to_sibling(grad_sgu_far), to_sibling(grad_sd_far)]
    if whole_tiles:
        packs = pack_grads(
            here_ref, owner_count, [grad_sgu, grad_sd], far, rings, shared_rows, piece
        )
    else:
        pair_gu, pair_down = sum_low([grad_sgu, far[0]]), sum_low([grad_sd, far[1]])
        stacks = jnp.concatenate(
            [
                pack(
                    pair_gu[device * shared_rows : (device + 1) * shared_rows],
                    pair_down[device * piece : (device + 1) * piece],
                )
                for device in range(owner_count * rings)
            ],
            0,
        ).reshape(owner_count, -1, 256)
        stacks = jnp.take(stacks, order, axis=0)
        packs = [stacks[index] for index in range(owner_count)]
    turned = [first_turned, second_turned]
    grad_ed = weight_grad(turned, [first_act, second_act], 1, True, 512, first_back[1:])
    expert_down_low = scatter_rows(grad_ed, SHARD)
    grad_egu = weight_grad(
        turned, [first_grad_act, second_grad_act], 0, False, 1024, [grad_ed]
    )
    expert_gu_low = scatter_rows(grad_egu, SHARD)

    packs = wait_all(packs, grad_egu, *second_back[1:])
    (
        block_out, grad_middle, grad_attn_low, grad_attn_t, normed_t, grad_router_rows,
        grad_gain_rows,
    ) = combine(
        here_ref, routes, target_row, first_back, second_back, middle, shared_out,
        grad_branch_shared, cotangent, branch_in, normed, norm_gains, router_rows,
        [grad_egu, packs[0]],
    )

    grad_w, grad_normed = attend_backward(
        prefix, query, key, value, heads, totals, cos, sin, normed_t, grad_attn_low, grad_attn_t,
        w_attn,
    )
    quarters = exchange(packs, "expert")
    attn_sum = scatter_rows(
        wait_for(grad_w, expert_gu_low, expert_down_low, *quarters[1:]), SHARD
    )
    quarter = sum_low(quarters).reshape(rings, -1, 256)
    blocks = FFS // 256
    columns = quarter[:, : blocks * shared_rows].reshape(
        rings, blocks, 2, shared_rows // 2, 256
    )
    mine = jnp.where(core == 0, columns[:, :, 0], columns[:, :, 1])
    other = to_sibling(jnp.where(core == 0, columns[:, :, 1], columns[:, :, 0]))
    by_half = [jnp.where(core == half, mine, other) for half in range(2)]
    quarter = jnp.concatenate(
        [half.reshape(rings, -1, 256) for half in by_half]
        + [quarter[:, blocks * shared_rows :]],
        1,
    ).reshape(-1, 256)
    hidden_in = tokens_in.astype(WIDE)
    first_rms = rms_scale(hidden_in)
    first_hat = hidden_in * first_rms
    grad_first_gain = jnp.sum(grad_normed * first_hat, 0)
    tokens_grad = grad_middle + norm_back(grad_normed, first_hat, first_rms, norm_gains[0])

    small = jnp.concatenate(
        [
            grad_first_gain[None],
            jnp.sum(grad_gain_rows, 0, keepdims=True),
            grad_router_rows[:experts_all],
        ],
        0,
    )
    small_sum = add_up(small, EVERY)
    gain_grad = small_sum[:2]
    router_grad = small_sum[2:].T

    expert_new, expert_first_new, expert_second_new = (
        state[None]
        for state in expert_update(
            expert_gu_low,
            expert_down_low,
            [state[0] for state in (expert_master, expert_first, expert_second)],
        )
    )
    gains_new, gains_first_new, gains_second_new = adam_update(
        norm_gains, gains_first, gains_second, gain_grad, RATE_GAIN, 0.0
    )
    router_new, router_first_new, router_second_new = adam_update(
        router, router_first, router_second, router_grad, RATE_ROUTER, WEIGHT_DECAY
    )
    quarter, attn_sum = wait_all([quarter, attn_sum], gains_new, tokens_grad, expert_new)
    shared_low = scatter_rows(quarter, "ring")
    slot_grads = split_columns(attn_sum, slot_of, owner_count, own_count)
    owned_grad = sum(part.astype(WIDE) for part in exchange(slot_grads, "expert"))

    owned_count = jnp.sum((owners == lax.axis_index("expert")).astype(jnp.int32))
    slot_used = (jnp.arange(own_count, dtype=jnp.int32) < owned_count)[:, None, None]
    attn_w, attn_m, attn_n = adam_update(
        attn_master, attn_first, attn_second, owned_grad, RATE_ATTENTION, WEIGHT_DECAY
    )
    attn_new = jnp.where(slot_used, attn_w, 0.0)
    attn_first_new = jnp.where(slot_used, attn_m, 0.0)
    attn_second_new = jnp.where(slot_used, attn_n, 0.0)
    own_rows = shared_rows // 2
    shared_states = [shared_master, shared_first, shared_second]
    if whole_tiles and piece == 64 and own_rows % 8 == 0:
        shared_new, shared_first_new, shared_second_new = shared_update(
            shared_low, own_rows, piece, shared_states
        )
    else:
        top = 2 * blocks * own_rows
        by_half = (
            shared_low[:top]
            .reshape(2, blocks, own_rows, 256)
            .transpose(0, 2, 1, 3)
            .reshape(2, own_rows, FFS)
            .astype(WIDE)
        )
        parts = [deinterleave(by_half[half]) for half in range(2)]
        down = shared_low[top:].reshape(-1, piece, 256).transpose(1, 0, 2).astype(WIDE)
        shared_summed = jnp.stack(
            [
                from_core(jnp.stack([parts[0][kind], parts[1][kind]], 1), piece).reshape(-1, 128)
                for kind in range(2)
            ]
            + [down.reshape(-1, 128)]
        )
        shared_new, shared_first_new, shared_second_new = adam_update(
            *shared_states, shared_summed, RATE_MATRIX, WEIGHT_DECAY
        )
    copies = jnp.concatenate(collect(attn_new.astype(LOW), "expert"), 0)
    attn_copy = jnp.take(wait_for(copies, shared_new), slot_of, axis=0)
    return (
        block_out,
        tokens_grad,
        attn_new,
        attn_first_new,
        attn_second_new,
        attn_copy,
        expert_new,
        expert_first_new,
        expert_second_new,
        shared_new,
        shared_first_new,
        shared_second_new,
        gains_new,
        gains_first_new,
        gains_second_new,
        router_new,
        router_first_new,
        router_second_new,
    )


def solution(mesh):
    owner_count, shard_count = mesh.devices.shape
    fine = Mesh(mesh.devices.reshape(owner_count, shard_count // 2, 2), EVERY)
    tokens = P(EVERY, None)
    slots = P("expert", SHARD, None)
    experts = P("expert", None, SHARD, None)
    shared = P(None, EVERY, None)
    return jax.shard_map(
        body,
        mesh=fine,
        in_specs=(tokens,) * 3
        + (P(EVERY), P())
        + (slots,) * 3
        + (experts,) * 3
        + (shared,) * 3
        + (P(),) * 6,
        out_specs=(tokens,) * 2
        + (slots,) * 3
        + (P(None, SHARD, None),)
        + (experts,) * 3
        + (shared,) * 3
        + (P(),) * 6,
        check_vma=False,
    )
```

time: 1410 us -> 493 us (0.35)
  matrix products: 362 us -> 0 us
  waiting for transfers between devices: 467 us -> 128 us
  local copies, waits for them, and re-layouts: 298 us -> 20.5 us
  Pallas kernels: 0 us -> 260 us
  other arithmetic: 194 us -> 24.8 us
  blocking collectives: 41.5 us -> 0 us
  starting transfers between devices: 19 us -> 38.3 us
    dot_general x35 -> x0, matrix products: 362 us -> none  [the longest x2 39.1 us: attend_backward(): jnp.einsum('qhd,khd->hqk', grad_block, value_rows, preferred_element_type...]
    reduce_scatter x4, waiting for transfers between devices: 330 us -> 20.1 us  [scatter_rows(): return lax.psum_scatter(grad, axes, scatter_dimension=0, tiled=True)]
    pallas_call x0 -> x19, Pallas kernels: none -> 260 us  [the longest x2 57.4 us: expert_pass(): pl.pallas_call(ignoring(functools.partial(expert_kernel, sources), source...]
    another operation x14 -> x11, local copies, waits for them, and re-layouts: 76.8 us -> 2.9 us  [the longest x2 1.04 us: rope_tables(): jnp.tile(jnp.sin(phase_angle), (1, PACK))]
    slice x17 -> x9, local copies, waits for them, and re-layouts: 67.8 us -> 1.57 us  [the longest x1 0.74 us: body(): grad_router_rows[:experts_all]]
    convert_element_type x8 -> x3, other arithmetic: 65.8 us -> 5.52 us  [the longest x1 2.75 us: sum_low(): sum((part.astype(WIDE) for part in parts[1:]), parts[0].astype(WIDE))]
    ppermute x0 -> x40, waiting for transfers between devices: none -> 59 us  [to_partner(): lax.ppermute(value, axis, [(index, index ^ distance) for index in range(s...]
    all_to_all x4 -> x0, waiting for transfers between devices: 48.7 us -> none  [the longest x1 20.7 us: body(): lax.all_to_all(expert_out.reshape(1, owner_count, count_rows, model_width...]
  transfers between devices with their start and end apart: 13 -> 47, of which waited for: 9 -> 17; matrix products, arithmetic and copies ran while one was open for 38% -> 6% of each run, Pallas kernels for 0% -> 50%
where the time goes in v1:
time: 493 us; the launch traced here: 488 us
  Pallas kernels  260 us (53%)
  waiting for transfers between devices  128 us (26%)
  starting transfers between devices  38.3 us (8%)
  other arithmetic  24.8 us (5%)
  local copies, waits for them, and re-layouts  20.5 us (4%)
  between operations  16.1 us (3%)
    ppermute x40, waiting for transfers between devices, to_partner(): lax.ppermute(value, axis, [(index, index ^ distance) for index in range(s...  59 us
    pallas_call x2, Pallas kernels, expert_pass(): pl.pallas_call(ignoring(functools.partial(expert_kernel, sources), source...  57.4 us
    all_gather x3, waiting for transfers between devices, gather_rows(): return lax.all_gather(part, axes, axis=0, tiled=True)  49.3 us
    pallas_call x1, Pallas kernels, swiglu_stacks(): pl.pallas_call(ignoring(kernel, 5 + 4 * partners, len(after)), grid=(2 *...  42.5 us
    pallas_call x1, Pallas kernels, attend_backward(): pl.pallas_call(attend_backward_kernel, grid=(GROUPS,), out_shape=[jax.Sha...  42.3 us
    ppermute x40, starting transfers between devices, to_partner(): lax.ppermute(value, axis, [(index, index ^ distance) for index in range(s...  37.7 us
    pallas_call x2, Pallas kernels, weight_grad(): pl.pallas_call(ignoring(functools.partial(weight_grad_kernel, halves, tur...  29.3 us
    pallas_call x1, Pallas kernels, attend_forward(): pl.pallas_call(ignoring(attend_forward_kernel, 6, len(after)), grid=(GROU...  26.7 us
  transfers between devices with their start and end apart: 47, of which 17 were waited for; matrix products, arithmetic and copies ran while one was open for 6% of the time, Pallas kernels for 50%

profile of v1, /device:TPU:9, one launch (start us, length us, event | category | flops | bytes accessed | tf_op | source)
XLA Modules:
  0.0 488.3 jit_solution(9052997419692582491)
XLA Ops:
  12.1 2.2 collective-permute-start.2
  15.7 5.6 %collective-permute-done.2 = bf16[24,48,128]{2,1,0:T(8,128)(2,1)S(1)} collective-permute-done((bf16[24,48,128]{2,1,0:T(8,128)(2,1)S(1)}, bf16[24,48,128]{2,1,0:T(8,128)(2,1)S(1)}, u32[]{:S(2)}, u32[]{:S(2)}) %collective-permute-start.2) | collective-permute-done | bytes 294944 | tf_op jit(solution)/shard_map/ppermute | solution.py:1190
  21.3 7.1 %collective-permute-done.1 = bf16[24,48,128]{2,1,0:T(8,128)(2,1)S(1)} collective-permute-done((bf16[24,48,128]{2,1,0:T(8,128)(2,1)S(1)}, bf16[24,48,128]{2,1,0:T(8,128)(2,1)S(1)}, u32[]{:S(2)}, u32[]{:S(2)}) %collective-permute-start.1) | collective-permute-done | bytes 294944 | tf_op jit(solution)/shard_map/ppermute | solution.py:1190
  29.5 2.9 shard_map.331
  38.4 1.3 reduce-window.6
  43.4 1.4 collective-permute-start.6
  46.1 49.3 %all-gather.5.cloned.1.call-done.refs_5_.w_ref = bf16[768,3072]{1,0:T(8,128)(2,1)} async-done(((bf16[96,3072]{1,0:T(8,128)(2,1)}), bf16[768,3072]{1,0:T(8,128)(2,1)}) %all-gather.5.cloned.1.call-update) | async-done | bytes 4718608 | tf_op jit(solution)/shard_map/all_gather | solution.py:1213
  95.4 26.7 %shard_map.332 = (bf16[1024,768]{1,0:T(8,128)(2,1)}, bf16[1024,768]{1,0:T(8,128)(2,1)}, bf16[1024,768]{1,0:T(8,128)(2,1)}, bf16[1024,768]{1,0:T(8,128)(2,1)}, f3...) custom-call(s32[1]{0:T(128)S(6)} %copy.126.refs_0_.prefix_ref, ...), custom_call_target="tpu_custom_call" | custom-call | flops 24999999488 | bytes 20000000 | tf_op jit(solution)/shard_map/pallas_call | solution.py:239
  125.1 14.2 %shard_map.333 = (bf16[2,256,768]{2,1,0:T(8,128)(2,1)}, bf16[2,256,768]{2,1,0:T(8,128)(2,1)}, bf16[2,256,768]{2,1,0:T(8,128)(2,1)}, bf16[2,256,768]{2,1,0:T(8,12...) custom-call(s32[1]{0:T(128)} %bitcast.here_ref.refs_0_, ...), custom_call_target="tpu_custom_call" | custom-call | flops 6442450944 | bytes 9437184 | tf_op jit(solution)/shard_map/pallas_call | solution.py:606
  139.3 1.2 collective-permute-start.11
  140.5 1.2 collective-permute-start.12
  143.2 1.2 collective-permute-start.18
  144.4 42.5 %shard_map.335 = (f32[1024,768]{1,0:T(8,128)}, f32[1024,768]{1,0:T(8,128)}, bf16[768,2048]{1,0:T(8,128)(2,1)}, bf16[1024,768]{1,0:T(8,128)(2,1)}, bf16[768,2048]{1,0:T(8,128)(2,1)}, /*index=5*/bf16[1024,768]{1,0:T(8,128)(2,1)}) custom-call(s32[1]{0:T(128)} %bitcast.here_ref.refs_0_, bf16[1024,768]{1,0:T(8,128)(2,1)} %get-tuple-element.102.branch_ref.refs_1_.refs_7_, ...), custom_call_target="tpu_custom_call" | custom-call | flops 28991029248 | bytes 28311552 | tf_op jit(solution)/shard_map/pallas_call | solution.py:980
  188.1 28.9 %shard_map.336 = (bf16[2,256,768]{2,1,0:T(8,128)(2,1)}, bf16[2,256,768]{2,1,0:T(8,128)(2,1)}, bf16[2,256,768]{2,1,0:T(8,128)(2,1)}, bf16[2,256,768]{2,1,0:T(8,12...) custom-call(bf16[2,256,768]{2,1,0:T(8,128)(2,1)} %get-tuple-element.113.refs_0_, ...), custom_call_target="tpu_custom_call" | custom-call | flops 1610612736 | bytes 1572864 | tf_op jit(solution)/shard_map/pallas_call | solution.py:699
  218.2 1.2 collective-permute-start.15
  220.5 28.5 %shard_map.337 = (bf16[2,256,768]{2,1,0:T(8,128)(2,1)}, bf16[2,256,768]{2,1,0:T(8,128)(2,1)}, bf16[2,256,768]{2,1,0:T(8,128)(2,1)}, bf16[2,256,768]{2,1,0:T(8,12...) custom-call(bf16[2,256,768]{2,1,0:T(8,128)(2,1)} %get-tuple-element.121.refs_0_, ...), custom_call_target="tpu_custom_call" | custom-call | flops 1610612736 | bytes 1572864 | tf_op jit(solution)/shard_map/pallas_call | solution.py:699
  249.1 3.1 collective-permute-done.16.refs_6_.refs_14_
  253.1 11.1 %shard_map.338.refs_4_ = bf16[2048,768]{1,0:T(8,128)(2,1)} custom-call(bf16[2,1,768,1024]{3,2,1,0:T(8,128)(2,1)} %get-tuple-element.130.refs_0_, bf16[2,1,768,1024]{3,2,1,0:T(8,128)(2,1)} %get-tuple-element.131.refs_1_, bf16[1024,2048]{1,0:T(8,128)(2,1)} %get-tuple-element.125.refs_6_.refs_2_, bf16[1024,2048]{1,0:T(8,128)(2,1)} %get-tuple-element.134.refs_3_, ...), custom_call_target="tpu_custom_call" | custom-call | flops 201326592 | bytes 786432 | tf_op jit(solution)/shard_map/pallas_call | solution.py:761
  264.3 3.4 collective-permute-start.23
  270.4 5.3 %collective-permute-done.24.refs_3_ = bf16[1024,768]{1,0:T(8,128)(2,1)S(1)} collective-permute-done((bf16[1024,768]{1,0:T(8,128)(2,1)}, bf16[1024,768]{1,0:T(8,128)(2,1)S(1)}, u32[]{:S(2)}, u32[]{:S(2)}) %collective-permute-start.24) | collective-permute-done | bytes 1572896 | tf_op jit(solution)/shard_map/ppermute | solution.py:1190
  276.9 1.6 copy-done.6
  278.5 6.9 %shard_map.340 = (bf16[4,576,256]{2,1,0:T(8,128)(2,1)}, bf16[4,576,256]{2,1,0:T(8,128)(2,1)}, bf16[4,576,256]{2,1,0:T(8,128)(2,1)}, bf16[4,576,256]{2,1,0:T(8,128)(2,1)}) custom-call(s32[1]{0:T(128)} %bitcast.here_ref.refs_0_, bf16[768,2048]{1,0:T(8,128)(2,1)} %get-tuple-element.135.refs_0_, bf16[768,2048]{1,0:T(8,128)(2,1)} %copy-done.6, ...), custom_call_target="tpu_custom_call" | custom-call | bytes 20000000 | tf_op jit(solution)/shard_map/pallas_call | solution.py:1040
  285.4 18.2 %shard_map.339.refs_4_.refs_19_ = bf16[768,4096]{1,0:T(8,128)(2,1)} custom-call(bf16[2,1,768,1024]{3,2,1,0:T(8,128)(2,1)} %get-tuple-element.130.refs_0_, bf16[2,1,768,1024]{3,2,1,0:T(8,128)(2,1)} %get-tuple-element.131.refs_1_, bf16[1024,4096]{1,0:T(8,128)(2,1)} %get-tuple-element.132.refs_2_, bf16[1024,4096]{1,0:T(8,128)(2,1)} %get-tuple-element.133.refs_3_, ...), custom_call_target="tpu_custom_call" | custom-call | flops 402653184 | bytes 1572864 | tf_op jit(solution)/shard_map/pallas_call | solution.py:761
  305.8 1.4 collective-permute-start.27
  307.3 21.8 %shard_map.342 = (bf16[1024,768]{1,0:T(8,128)(2,1)}, f32[1024,768]{1,0:T(8,128)}, bf16[1024,768]{1,0:T(8,128)(2,1)}, bf16[4,768,256]{2,1,0:T(8,128)(2,1)}, bf16[...) custom-call(s32[1]{0:T(128)} %bitcast.here_ref.refs_0_, s32[1024,2]{1,0:T(8,128)} %copy-done.4, ...), custom_call_target="tpu_custom_call" | custom-call | flops 399999991808 | bytes 25000000 | tf_op jit(solution)/shard_map/pallas_call | solution.py:849
  329.1 42.3 %shard_map.343 = (bf16[768,3072]{1,0:T(8,128)(2,1)}, f32[1024,768]{1,0:T(8,128)}) custom-call(s32[1]{0:T(128)S(6)} %copy.126.refs_0_.prefix_ref, bf16[1024,768]{1,0:T(8,128)(2,1)} %get-tuple-element.146.query_ref, bf16[1024,768]{1,0:T(8,128)(2,1)} %get-tuple-element.147.key_ref, bf16[1024,768]{1,0:T(8,128)(2,1)} %get-tuple-element.148.value_ref, ...), custom_call_target="tpu_custom_call" | custom-call | tf_op jit(solution)/shard_map/pallas_call | solution.py:375
  371.4 4.9 reduce-scatter.5.cloned.1.call-done.refs_1_.gu_ref
  378.2 2.9 fusion.7
  381.8 1.3 collective-permute-start.29
  383.1 1.6 collective-permute-done.29
  384.7 1.4 collective-permute-start.30
  386.1 1.8 collective-permute-done.30
  387.9 3.6 collective-permute-done.31
  391.5 1.3 collective-permute-start.32
  392.7 3.0 collective-permute-done.32
  395.7 4.5 collective-permute-start.33
  400.2 2.8 add_convert_fusion
  404.2 2.5 fusion.6.refs_3_
  408.6 9.1 %shard_map.345 = (f32[3,1536,128]{2,1,0:T(8,128)}, f32[3,1536,128]{2,1,0:T(8,128)}, f32[3,1536,128]{2,1,0:T(8,128)}) custom-call(bf16[96,4096]{1,0:T(8,128)(2,1)} %reduce-scatter.5.cloned.1.call-done.refs_1_.gu_ref, bf16[256,768]{1,0:T(8,128)(2,1)} %reduce-scatter.7.cloned.1.call-done.refs_2_.down_ref, f32[3,1536,128]{2,1,0:T(8,128)} %bitcast.137, ...), custom_call_target="tpu_custom_call" | custom-call | tf_op jit(solution)/shard_map/pallas_call | solution.py:1140
  417.7 15.2 %reduce-scatter.9.cloned.1.call-done.refs_1_ = bf16[96,3072]{1,0:T(8,128)(2,1)} async-done(((bf16[768,3072]{1,0:T(8,128)(2,1)}), bf16[96,3072]{1,0:T(8,128)(2,1)}) %reduce-scatter.9.cloned.1.call-update) | async-done | bytes 589840 | tf_op jit(solution)/shard_map/reduce_scatter | solution.py:1217
  434.2 2.8 shard_map.347
  440.3 6.0 %collective-permute-done.34 = bf16[24,48,128]{2,1,0:T(8,128)(2,1)S(1)} collective-permute-done((bf16[24,48,128]{2,1,0:T(8,128)(2,1)}, bf16[24,48,128]{2,1,0:T(8,128)(2,1)S(1)}, u32[]{:S(2)}, u32[]{:S(2)}) %collective-permute-start.34) | collective-permute-done | bytes 294944 | tf_op jit(solution)/shard_map/ppermute | solution.py:1190
  446.2 7.4 %collective-permute-done.35 = bf16[24,48,128]{2,1,0:T(8,128)(2,1)S(1)} collective-permute-done((bf16[24,48,128]{2,1,0:T(8,128)(2,1)}, bf16[24,48,128]{2,1,0:T(8,128)(2,1)S(1)}, u32[]{:S(2)}, u32[]{:S(2)}) %collective-permute-start.35) | collective-permute-done | bytes 294944 | tf_op jit(solution)/shard_map/ppermute | solution.py:1190
  453.7 2.7 fusion.27
  459.8 5.8 %collective-permute-done.39 = bf16[24,48,128]{2,1,0:T(8,128)(2,1)S(1)} collective-permute-done((bf16[24,48,128]{2,1,0:T(8,128)(2,1)S(1)}, bf16[24,48,128]{2,1,0:T(8,128)(2,1)S(1)}, u32[]{:S(2)}, u32[]{:S(2)}) %collective-permute-start.39) | collective-permute-done | bytes 294944 | tf_op jit(solution)/shard_map/ppermute | solution.py:1190
  465.6 7.0 %collective-permute-done.38 = bf16[24,48,128]{2,1,0:T(8,128)(2,1)S(1)} collective-permute-done((bf16[24,48,128]{2,1,0:T(8,128)(2,1)S(1)}, bf16[24,48,128]{2,1,0:T(8,128)(2,1)S(1)}, u32[]{:S(2)}, u32[]{:S(2)}) %collective-permute-start.38) | collective-permute-done | bytes 294944 | tf_op jit(solution)/shard_map/ppermute | solution.py:1190
  473.8 4.4 shard_map.348
  478.2 1.9 gather_fusion
  (243 shorter events, 48.0 us)
Async XLA Ops:
  7.2 36.2 %all-gather.7.cloned.1.call-start = ((), (), s32[]{:S(2)}) async-start(), calls=%async_computation.5 | async-start | bytes 1474560 | tf_op jit(solution)/shard_map/all_gather | solution.py:1213
  9.4 1.7 collective-permute-start.3
  11.9 83.4 %all-gather.5.cloned.1.call-start = ((), (), s32[]{:S(2)}) async-start(), calls=%async_computation.4 | async-start | bytes 5308416 | tf_op jit(solution)/shard_map/all_gather | solution.py:1213
  12.1 9.2 %collective-permute-start.2 = (bf16[24,48,128]{2,1,0:T(8,128)(2,1)S(1)}, bf16[24,48,128]{2,1,0:T(8,128)(2,1)S(1)}, u32[]{:S(2)}, u32[]{:S(2)}) collective-permute-start(bf16[24,48,128]{2,1,0:T(8,128)(2,1)S(1)} %convert_element_type.85), channel_id=1, source_target_pairs={{0,24},{8,16},{16,8},{24,0},{1,25},{9,17},{17,9},{25,1},{2,26},{10... | collective-permute-start | bytes 884744 | tf_op jit(solution)/shard_map/ppermute | solution.py:1190
  14.3 14.1 %collective-permute-start.1 = (bf16[24,48,128]{2,1,0:T(8,128)(2,1)S(1)}, bf16[24,48,128]{2,1,0:T(8,128)(2,1)S(1)}, u32[]{:S(2)}, u32[]{:S(2)}) collective-permute-start(bf16[24,48,128]{2,1,0:T(8,128)(2,1)S(1)} %convert_element_type.85), channel_id=1, source_target_pairs={{0,16},{8,24},{16,0},{24,8},{1,17},{9,25},{17,1},{25,9},{2,18},{10... | collective-permute-start | bytes 884744 | tf_op jit(solution)/shard_map/ppermute | solution.py:1190
  14.5 13.9 %collective-permute-start = (bf16[24,48,128]{2,1,0:T(8,128)(2,1)S(1)}, bf16[24,48,128]{2,1,0:T(8,128)(2,1)S(1)}, u32[]{:S(2)}, u32[]{:S(2)}) collective-permute-start(bf16[24,48,128]{2,1,0:T(8,128)(2,1)S(1)} %convert_element_type.85), channel_id=1, source_target_pairs={{0,8},{8,0},{16,24},{24,16},{1,9},{9,1},{17,25},{25,17},{2,10},{10... | collective-permute-start | bytes 884744 | tf_op jit(solution)/shard_map/ppermute | solution.py:1190
  32.4 154.8 %all-gather.9.cloned.1.call-start = ((), (), s32[]{:S(2)}) async-start(), calls=%async_computation.10 | async-start | bytes 10616832 | tf_op jit(solution)/shard_map/all_gather | solution.py:1213
  35.1 336.4 %reduce-scatter.7.cloned.1.call-start = ((), (), s32[]{:S(2)}) async-start(), calls=%async_computation.7 | async-start | bytes 3538944 | tf_op jit(solution)/shard_map/reduce_scatter | solution.py:1217
  40.8 81.2 %copy-start.9 = (s32[1024,2]{1,0:T(8,128)}, s32[1024,2]{1,0:T(8,128)S(1)}, u32[]{:S(2)}) copy-start(s32[1024,2]{1,0:T(8,128)S(1)} %add_select_fusion.refs_2_) | copy-start | bytes 24580
  43.4 78.7 %collective-permute-start.6 = (bf16[2304,256]{1,0:T(8,128)(2,1)}, bf16[2304,256]{1,0:T(8,128)(2,1)S(1)}, u32[]{:S(2)}, u32[]{:S(2)}) collective-permute-start(bf16[2304,256]{1,0:T(8,128)(2,1)} %all-gather.7.cloned.1.call-done.refs_0_), channel_id=1, source_target_pairs={{0,24},{8,16},{16,8},{24,0},{1,25},{9,17},{17,9},{25,1},{2,26},{10... | collective-permute-start | bytes 3538952 | tf_op jit(solution)/shard_map/ppermute | solution.py:1190
  44.8 77.3 %collective-permute-start.5 = (bf16[2304,256]{1,0:T(8,128)(2,1)}, bf16[2304,256]{1,0:T(8,128)(2,1)S(1)}, u32[]{:S(2)}, u32[]{:S(2)}) collective-permute-start(bf16[2304,256]{1,0:T(8,128)(2,1)} %all-gather.7.cloned.1.call-done.refs_0_), channel_id=1, source_target_pairs={{0,16},{8,24},{16,0},{24,8},{1,17},{9,25},{17,1},{25,9},{2,18},{10... | collective-permute-start | bytes 3538952 | tf_op jit(solution)/shard_map/ppermute | solution.py:1190
  45.8 76.3 %collective-permute-start.4 = (bf16[2304,256]{1,0:T(8,128)(2,1)}, bf16[2304,256]{1,0:T(8,128)(2,1)}, u32[]{:S(2)}, u32[]{:S(2)}) collective-permute-start(bf16[2304,256]{1,0:T(8,128)(2,1)} %all-gather.7.cloned.1.call-done.refs_0_), channel_id=1, source_target_pairs={{0,8},{8,0},{16,24},{24,16},{1,9},{9,1},{17,25},{25,17},{2,10},{10... | collective-permute-start | bytes 3538952 | tf_op jit(solution)/shard_map/ppermute | solution.py:1190
  123.5 17.1 %collective-permute-start.7 = (bf16[2304,256]{1,0:T(8,128)(2,1)}, bf16[2304,256]{1,0:T(8,128)(2,1)S(1)}, u32[]{:S(2)}, u32[]{:S(2)}) collective-permute-start(bf16[2304,256]{1,0:T(8,128)(2,1)} %get-tuple-element.106), channel_id=1, source_target_pairs={{0,1},{1,0},{2,3},{3,2},{4,5},{5,4},{6,7},{7,6},{8,9},{9,8},{10,11... | collective-permute-start | bytes 3538952 | tf_op jit(solution)/shard_map/ppermute | solution.py:1190
  123.7 18.0 %collective-permute-start.8 = (bf16[2304,256]{1,0:T(8,128)(2,1)}, bf16[2304,256]{1,0:T(8,128)(2,1)}, u32[]{:S(2)}, u32[]{:S(2)}) collective-permute-start(bf16[2304,256]{1,0:T(8,128)(2,1)} %get-tuple-element.107), channel_id=1, source_target_pairs={{0,1},{1,0},{2,3},{3,2},{4,5},{5,4},{6,7},{7,6},{8,9},{9,8},{10,11... | collective-permute-start | bytes 3538952 | tf_op jit(solution)/shard_map/ppermute | solution.py:1190
  124.0 18.0 %collective-permute-start.9 = (bf16[2304,256]{1,0:T(8,128)(2,1)}, bf16[2304,256]{1,0:T(8,128)(2,1)}, u32[]{:S(2)}, u32[]{:S(2)}) collective-permute-start(bf16[2304,256]{1,0:T(8,128)(2,1)} %get-tuple-element.108), channel_id=1, source_target_pairs={{0,1},{1,0},{2,3},{3,2},{4,5},{5,4},{6,7},{7,6},{8,9},{9,8},{10,11... | collective-permute-start | bytes 3538952 | tf_op jit(solution)/shard_map/ppermute | solution.py:1190
  124.2 19.0 %collective-permute-start.10 = (bf16[2304,256]{1,0:T(8,128)(2,1)}, bf16[2304,256]{1,0:T(8,128)(2,1)}, u32[]{:S(2)}, u32[]{:S(2)}) collective-permute-start(bf16[2304,256]{1,0:T(8,128)(2,1)} %get-tuple-element.109), channel_id=1, source_target_pairs={{0,1},{1,0},{2,3},{3,2},{4,5},{5,4},{6,7},{7,6},{8,9},{9,8},{10,11... | collective-permute-start | bytes 3538952 | tf_op jit(solution)/shard_map/ppermute | solution.py:1190
  139.3 47.6 %collective-permute-start.11 = (bf16[2,256,768]{2,1,0:T(8,128)(2,1)}, bf16[2,256,768]{2,1,0:T(8,128)(2,1)S(1)}, u32[]{:S(2)}, u32[]{:S(2)}) collective-permute-start(bf16[2,256,768]{2,1,0:T(8,128)(2,1)} %get-tuple-element.114), channel_id=1, source_target_pairs={{0,8},{8,0},{16,24},{24,16},{1,9},{9,1},{17,25},{25,17},{2,10},{10... | collective-permute-start | bytes 2359304 | tf_op jit(solution)/shard_map/ppermute | solution.py:1190
  140.5 46.7 %collective-permute-start.12 = (bf16[2,256,768]{2,1,0:T(8,128)(2,1)}, bf16[2,256,768]{2,1,0:T(8,128)(2,1)S(1)}, u32[]{:S(2)}, u32[]{:S(2)}) collective-permute-start(bf16[2,256,768]{2,1,0:T(8,128)(2,1)} %get-tuple-element.115), channel_id=1, source_target_pairs={{0,16},{8,24},{16,0},{24,8},{1,17},{9,25},{17,1},{25,9},{2,18},{10... | collective-permute-start | bytes 2359304 | tf_op jit(solution)/shard_map/ppermute | solution.py:1190
  141.8 45.5 %collective-permute-start.13 = (bf16[2,256,768]{2,1,0:T(8,128)(2,1)}, bf16[2,256,768]{2,1,0:T(8,128)(2,1)}, u32[]{:S(2)}, u32[]{:S(2)}) collective-permute-start(bf16[2,256,768]{2,1,0:T(8,128)(2,1)} %get-tuple-element.116), channel_id=1, source_target_pairs={{0,24},{8,16},{16,8},{24,0},{1,25},{9,17},{17,9},{25,1},{2,26},{10... | collective-permute-start | bytes 2359304 | tf_op jit(solution)/shard_map/ppermute | solution.py:1190
  142.0 77.4 %collective-permute-start.17 = (bf16[2,256,768]{2,1,0:T(8,128)(2,1)}, bf16[2,256,768]{2,1,0:T(8,128)(2,1)S(1)}, u32[]{:S(2)}, u32[]{:S(2)}) collective-permute-start(bf16[2,256,768]{2,1,0:T(8,128)(2,1)} %get-tuple-element.122), channel_id=1, source_target_pairs={{0,8},{8,0},{16,24},{24,16},{1,9},{9,1},{17,25},{25,17},{2,10},{10... | collective-permute-start | bytes 2359304 | tf_op jit(solution)/shard_map/ppermute | solution.py:1190
  143.2 76.4 %collective-permute-start.18 = (bf16[2,256,768]{2,1,0:T(8,128)(2,1)}, bf16[2,256,768]{2,1,0:T(8,128)(2,1)S(1)}, u32[]{:S(2)}, u32[]{:S(2)}) collective-permute-start(bf16[2,256,768]{2,1,0:T(8,128)(2,1)} %get-tuple-element.123), channel_id=1, source_target_pairs={{0,16},{8,24},{16,0},{24,8},{1,17},{9,25},{17,1},{25,9},{2,18},{10... | collective-permute-start | bytes 2359304 | tf_op jit(solution)/shard_map/ppermute | solution.py:1190
  186.9 32.7 %collective-permute-start.19 = (bf16[2,256,768]{2,1,0:T(8,128)(2,1)}, bf16[2,256,768]{2,1,0:T(8,128)(2,1)}, u32[]{:S(2)}, u32[]{:S(2)}) collective-permute-start(bf16[2,256,768]{2,1,0:T(8,128)(2,1)} %get-tuple-element.124), channel_id=1, source_target_pairs={{0,24},{8,16},{16,8},{24,0},{1,25},{9,17},{17,9},{25,1},{2,26},{10... | collective-permute-start | bytes 2359304 | tf_op jit(solution)/shard_map/ppermute | solution.py:1190
  217.0 32.1 %collective-permute-start.14 = (bf16[2,256,768]{2,1,0:T(8,128)(2,1)}, bf16[2,256,768]{2,1,0:T(8,128)(2,1)S(1)}, u32[]{:S(2)}, u32[]{:S(2)}) collective-permute-start(bf16[2,256,768]{2,1,0:T(8,128)(2,1)} %get-tuple-element.118), channel_id=1, source_target_pairs={{0,8},{8,0},{16,24},{24,16},{1,9},{9,1},{17,25},{25,17},{2,10},{10... | collective-permute-start | bytes 2359304 | tf_op jit(solution)/shard_map/ppermute | solution.py:1190
  218.2 30.9 %collective-permute-start.15 = (bf16[2,256,768]{2,1,0:T(8,128)(2,1)}, bf16[2,256,768]{2,1,0:T(8,128)(2,1)S(1)}, u32[]{:S(2)}, u32[]{:S(2)}) collective-permute-start(bf16[2,256,768]{2,1,0:T(8,128)(2,1)} %get-tuple-element.119), channel_id=1, source_target_pairs={{0,16},{8,24},{16,0},{24,8},{1,17},{9,25},{17,1},{25,9},{2,18},{10... | collective-permute-start | bytes 2359304 | tf_op jit(solution)/shard_map/ppermute | solution.py:1190
  219.4 32.8 %collective-permute-start.16 = (bf16[2,256,768]{2,1,0:T(8,128)(2,1)}, bf16[2,256,768]{2,1,0:T(8,128)(2,1)S(1)}, u32[]{:S(2)}, u32[]{:S(2)}) collective-permute-start(bf16[2,256,768]{2,1,0:T(8,128)(2,1)} %get-tuple-element.120), channel_id=1, source_target_pairs={{0,24},{8,16},{16,8},{24,0},{1,25},{9,17},{17,9},{25,1},{2,26},{10... | collective-permute-start | bytes 2359304 | tf_op jit(solution)/shard_map/ppermute | solution.py:1190
  264.2 112.1 %reduce-scatter.5.cloned.1.call-start = ((), (), s32[]{:S(2)}) async-start(), calls=%async_computation.6 | async-start | bytes 7077888 | tf_op jit(solution)/shard_map/reduce_scatter | solution.py:1217
  264.3 11.5 %collective-permute-start.23 = (bf16[768,2048]{1,0:T(8,128)(2,1)}, bf16[768,2048]{1,0:T(8,128)(2,1)S(1)}, u32[]{:S(2)}, u32[]{:S(2)}) collective-permute-start(bf16[768,2048]{1,0:T(8,128)(2,1)} %get-tuple-element.136), channel_id=1, source_target_pairs={{0,1},{1,0},{2,3},{3,2},{4,5},{5,4},{6,7},{7,6},{8,9},{9,8},{10,11... | collective-permute-start | bytes 9437192 | tf_op jit(solution)/shard_map/ppermute | solution.py:1190
  267.7 8.0 %collective-permute-start.24 = (bf16[1024,768]{1,0:T(8,128)(2,1)}, bf16[1024,768]{1,0:T(8,128)(2,1)S(1)}, u32[]{:S(2)}, u32[]{:S(2)}) collective-permute-start(bf16[1024,768]{1,0:T(8,128)(2,1)} %get-tuple-element.138), channel_id=1, source_target_pairs={{0,1},{1,0},{2,3},{3,2},{4,5},{5,4},{6,7},{7,6},{8,9},{9,8},{10,11... | collective-permute-start | bytes 4718600 | tf_op jit(solution)/shard_map/ppermute | solution.py:1190
  267.8 35.9 %collective-permute-start.20 = (bf16[2,256,768]{2,1,0:T(8,128)(2,1)}, bf16[2,256,768]{2,1,0:T(8,128)(2,1)S(1)}, u32[]{:S(2)}, u32[]{:S(2)}) collective-permute-start(bf16[2,256,768]{2,1,0:T(8,128)(2,1)} %get-tuple-element.127), channel_id=1, source_target_pairs={{0,8},{8,0},{16,24},{24,16},{1,9},{9,1},{17,25},{25,17},{2,10},{10... | collective-permute-start | bytes 2359304 | tf_op jit(solution)/shard_map/ppermute | solution.py:1190
  268.4 35.3 %collective-permute-start.21 = (bf16[2,256,768]{2,1,0:T(8,128)(2,1)}, bf16[2,256,768]{2,1,0:T(8,128)(2,1)}, u32[]{:S(2)}, u32[]{:S(2)}) collective-permute-start(bf16[2,256,768]{2,1,0:T(8,128)(2,1)} %get-tuple-element.128), channel_id=1, source_target_pairs={{0,16},{8,24},{16,0},{24,8},{1,17},{9,25},{17,1},{25,9},{2,18},{10... | collective-permute-start | bytes 2359304 | tf_op jit(solution)/shard_map/ppermute | solution.py:1190
  269.3 35.3 %collective-permute-start.22 = (bf16[2,256,768]{2,1,0:T(8,128)(2,1)}, bf16[2,256,768]{2,1,0:T(8,128)(2,1)}, u32[]{:S(2)}, u32[]{:S(2)}) collective-permute-start(bf16[2,256,768]{2,1,0:T(8,128)(2,1)} %get-tuple-element.129), channel_id=1, source_target_pairs={{0,24},{8,16},{16,8},{24,0},{1,25},{9,17},{17,9},{25,1},{2,26},{10... | collective-permute-start | bytes 2359304 | tf_op jit(solution)/shard_map/ppermute | solution.py:1190
  303.6 129.2 %reduce-scatter.9.cloned.1.call-start = ((), (), s32[]{:S(2)}) async-start(), calls=%async_computation.8 | async-start | bytes 5308416 | tf_op jit(solution)/shard_map/reduce_scatter | solution.py:1217
  304.6 66.8 %collective-permute-start.25 = (bf16[2304,256]{1,0:T(8,128)(2,1)}, bf16[2304,256]{1,0:T(8,128)(2,1)}, u32[]{:S(2)}, u32[]{:S(2)}) collective-permute-start(bf16[2304,256]{1,0:T(8,128)(2,1)} %get-tuple-element.154), channel_id=1, source_target_pairs={{0,8},{8,0},{16,24},{24,16},{1,9},{9,1},{17,25},{25,17},{2,10},{10... | collective-permute-start | bytes 3538952 | tf_op jit(solution)/shard_map/ppermute | solution.py:1190
  304.9 66.5 %collective-permute-start.26 = (bf16[2304,256]{1,0:T(8,128)(2,1)}, bf16[2304,256]{1,0:T(8,128)(2,1)}, u32[]{:S(2)}, u32[]{:S(2)}) collective-permute-start(bf16[2304,256]{1,0:T(8,128)(2,1)} %get-tuple-element.155), channel_id=1, source_target_pairs={{0,16},{8,24},{16,0},{24,8},{1,17},{9,25},{17,1},{25,9},{2,18},{10... | collective-permute-start | bytes 3538952 | tf_op jit(solution)/shard_map/ppermute | solution.py:1190
  305.8 65.6 %collective-permute-start.27 = (bf16[2304,256]{1,0:T(8,128)(2,1)}, bf16[2304,256]{1,0:T(8,128)(2,1)}, u32[]{:S(2)}, u32[]{:S(2)}) collective-permute-start(bf16[2304,256]{1,0:T(8,128)(2,1)} %get-tuple-element.156), channel_id=1, source_target_pairs={{0,24},{8,16},{16,8},{24,0},{1,25},{9,17},{17,9},{25,1},{2,26},{10... | collective-permute-start | bytes 3538952 | tf_op jit(solution)/shard_map/ppermute | solution.py:1190
  376.3 97.5 %reduce-scatter.11.cloned.1.call-start = ((), (), s32[]{:S(2)}) async-start(), calls=%async_computation.9 | async-start | bytes 1474560 | tf_op jit(solution)/shard_map/reduce_scatter | solution.py:1217
  381.8 2.9 collective-permute-start.29
  384.7 3.1 collective-permute-start.30
  387.9 3.6 collective-permute-start.31
  391.5 4.3 collective-permute-start.32
  395.7 11.0 %collective-permute-start.33 = (f32[6,768]{1,0:T(8,128)S(1)}, f32[6,768]{1,0:T(8,128)S(1)}, u32[]{:S(2)}, u32[]{:S(2)}) collective-permute-start(f32[6,768]{1,0:T(8,128)S(1)} %add.142), channel_id=1, source_target_pairs={{0,1},{1,0},{2,3},{3,2},{4,5},{5,4},{6,7},{7,6},{8,9},{9,8},{10,11... | collective-permute-start | bytes 55304 | tf_op jit(solution)/shard_map/ppermute | solution.py:1190
  403.1 4.4 collective-permute-start.28
  437.0 9.3 %collective-permute-start.34 = (bf16[24,48,128]{2,1,0:T(8,128)(2,1)}, bf16[24,48,128]{2,1,0:T(8,128)(2,1)S(1)}, u32[]{:S(2)}, u32[]{:S(2)}) collective-permute-start(bf16[24,48,128]{2,1,0:T(8,128)(2,1)} %get-tuple-element.163), channel_id=1, source_target_pairs={{0,8},{8,0},{16,24},{24,16},{1,9},{9,1},{17,25},{25,17},{2,10},{10... | collective-permute-start | bytes 884744 | tf_op jit(solution)/shard_map/ppermute | solution.py:1190
  438.2 15.5 %collective-permute-start.35 = (bf16[24,48,128]{2,1,0:T(8,128)(2,1)}, bf16[24,48,128]{2,1,0:T(8,128)(2,1)S(1)}, u32[]{:S(2)}, u32[]{:S(2)}) collective-permute-start(bf16[24,48,128]{2,1,0:T(8,128)(2,1)} %get-tuple-element.164), channel_id=1, source_target_pairs={{0,16},{8,24},{16,0},{24,8},{1,17},{9,25},{17,1},{25,9},{2,18},{10... | collective-permute-start | bytes 884744 | tf_op jit(solution)/shard_map/ppermute | solution.py:1190
  439.3 14.3 %collective-permute-start.36 = (bf16[24,48,128]{2,1,0:T(8,128)(2,1)}, bf16[24,48,128]{2,1,0:T(8,128)(2,1)S(1)}, u32[]{:S(2)}, u32[]{:S(2)}) collective-permute-start(bf16[24,48,128]{2,1,0:T(8,128)(2,1)} %get-tuple-element.165), channel_id=1, source_target_pairs={{0,24},{8,16},{16,8},{24,0},{1,25},{9,17},{17,9},{25,1},{2,26},{10... | collective-permute-start | bytes 884744 | tf_op jit(solution)/shard_map/ppermute | solution.py:1190
  456.5 9.1 %collective-permute-start.39 = (bf16[24,48,128]{2,1,0:T(8,128)(2,1)S(1)}, bf16[24,48,128]{2,1,0:T(8,128)(2,1)S(1)}, u32[]{:S(2)}, u32[]{:S(2)}) collective-permute-start(bf16[24,48,128]{2,1,0:T(8,128)(2,1)S(1)} %get-tuple-element.179), channel_id=1, source_target_pairs={{0,24},{8,16},{16,8},{24,0},{1,25},{9,17},{17,9},{25,1},{2,26},{10... | collective-permute-start | bytes 884744 | tf_op jit(solution)/shard_map/ppermute | solution.py:1190
  457.7 15.0 %collective-permute-start.38 = (bf16[24,48,128]{2,1,0:T(8,128)(2,1)S(1)}, bf16[24,48,128]{2,1,0:T(8,128)(2,1)S(1)}, u32[]{:S(2)}, u32[]{:S(2)}) collective-permute-start(bf16[24,48,128]{2,1,0:T(8,128)(2,1)S(1)} %get-tuple-element.179), channel_id=1, source_target_pairs={{0,16},{8,24},{16,0},{24,8},{1,17},{9,25},{17,1},{25,9},{2,18},{10... | collective-permute-start | bytes 884744 | tf_op jit(solution)/shard_map/ppermute | solution.py:1190
  458.3 14.3 %collective-permute-start.37 = (bf16[24,48,128]{2,1,0:T(8,128)(2,1)S(1)}, bf16[24,48,128]{2,1,0:T(8,128)(2,1)S(1)}, u32[]{:S(2)}, u32[]{:S(2)}) collective-permute-start(bf16[24,48,128]{2,1,0:T(8,128)(2,1)S(1)} %get-tuple-element.179), channel_id=1, source_target_pairs={{0,8},{8,0},{16,24},{24,16},{1,9},{9,1},{17,25},{25,17},{2,10},{10... | collective-permute-start | bytes 884744 | tf_op jit(solution)/shard_map/ppermute | solution.py:1190
  (36 other events, 161.4 us)
Sparse Core Ops, SparseCore 0:
  12.1 30.5 all-gather.6
  44.9 50.4 all-gather.4
  97.0 88.2 all-gather.8
  264.4 40.4 reduce-scatter.6
  307.0 69.2 reduce-scatter.4
  378.4 54.3 reduce-scatter.8
  435.2 27.0 reduce-scatter.10

commit v2 on v1

--- a/solution.py
+++ b/solution.py
@@ -156,8 +156,8 @@
 
 def attend_forward_kernel(
     prefix_ref, token_ref, gain_ref, cos_ref, sin_ref, w_ref,
-    query_ref, key_ref, value_ref, head_ref, total_ref, normed_ref, middle_ref, branch_ref,
-    sum_ref,
+    query_ref, key_ref, value_ref, head_ref, rest_ref, total_ref, normed_ref, middle_ref,
+    branch_ref, sum_ref,
 ):
     group = pl.program_id(0)
     length, width = token_ref.shape
@@ -223,6 +223,7 @@
         attend(*item, scores)
     heads = sum_ref[...].astype(LOW)
     head_ref[...] = heads
+    rest_ref[...] = (sum_ref[...] - heads.astype(WIDE)).astype(LOW)
     middle_ref[...] += dot_nt(heads, w_ref[:, 3 * GROUP :])
 
     @pl.when(group == pl.num_programs(0) - 1)
@@ -240,7 +241,7 @@
         ignoring(attend_forward_kernel, 6, len(after)),
         grid=(GROUPS,),
         out_shape=[
-            low(width), low(width), low(width), low(width),
+            low(width), low(width), low(width), low(width), low(width),
             jax.ShapeDtypeStruct((length, 128), WIDE),
             low(width),
             jax.ShapeDtypeStruct((length, width), WIDE),
@@ -256,7 +257,7 @@
         ]
         + [ANYWHERE] * len(after),
         out_specs=[
-            grouped, grouped, grouped, grouped,
+            grouped, grouped, grouped, grouped, grouped,
             whole((length, 128)),
             whole((length, width)),
             whole((length, width)),
@@ -271,7 +272,7 @@
 
 
 def attend_backward_kernel(
-    prefix_ref, query_ref, key_ref, value_ref, head_ref, total_ref, cos_ref, sin_ref,
+    prefix_ref, query_ref, key_ref, value_ref, head_ref, rest_ref, total_ref, cos_ref, sin_ref,
     normed_t_ref, grad_ref, grad_t_ref, w_ref, grad_w_ref, grad_normed_ref,
     total_t_ref, scaled_ref, key_t_ref, grad_head_ref, center_ref,
     probs_ref, grad_scores_ref, grad_query_t_ref, grad_key_ref, grad_value_ref,
@@ -292,7 +293,7 @@
             key_t_ref[head, half * HALF : (half + 1) * HALF, :] = key_t[first : first + HALF]
     grad_heads = dot_nn(grad_ref[...], w_ref[:, 3 * GROUP :]).astype(LOW)
     grad_head_ref[...] = grad_heads
-    product = grad_heads.astype(WIDE) * head_ref[...].astype(WIDE)
+    product = grad_heads.astype(WIDE) * (head_ref[...].astype(WIDE) + rest_ref[...].astype(WIDE))
     leading = product.astype(LOW)
     rest = (product - leading.astype(WIDE)).astype(LOW)
     head_row = lax.broadcasted_iota(jnp.int32, (16, GROUP), 0)
@@ -368,7 +369,7 @@
 
 
 def attend_backward(
-    prefix, query, key, value, heads, totals, cos, sin, normed_t, grad, grad_t, w_attn
+    prefix, query, key, value, heads, rest, totals, cos, sin, normed_t, grad, grad_t, w_attn
 ):
     length, width = grad.shape
     grouped = pl.BlockSpec((length, GROUP), lambda step: (0, step))
@@ -381,7 +382,7 @@
         ],
         in_specs=[
             pl.BlockSpec(memory_space=pltpu.SMEM),
-            grouped, grouped, grouped, grouped,
+            grouped, grouped, grouped, grouped, grouped,
             once(totals.shape), once(cos.shape), once(sin.shape), once(normed_t.shape),
             once(grad.shape), once(grad_t.shape),
             pl.BlockSpec((width, 4 * GROUP), lambda step: (0, step)),
@@ -404,7 +405,7 @@
         ],
         compiler_params=params(),
         cost_estimate=AT_ONCE,
-    )(prefix, query, key, value, heads, totals, cos, sin, normed_t, grad, grad_t, w_attn)
+    )(prefix, query, key, value, heads, rest, totals, cos, sin, normed_t, grad, grad_t, w_attn)
 
 
 def swiglu_blocks(blocks, rows_of, w_gu_ref, w_d_ref, act_ref, grad_act_ref, sum_ref, grad_sum_ref):
@@ -482,7 +483,7 @@
         )
 
 
-ROW_BLOCK = 1024
+ROW_BLOCK = 512
 HIDDEN_BLOCK = 256
 
 
@@ -1352,7 +1353,7 @@
 
     cos, sin = rope_tables(tok_count)
     target_t = target_row.T
-    query, key, value, heads, totals, normed, middle, branch_in = attend_forward(
+    query, key, value, heads, rest, totals, normed, middle, branch_in = attend_forward(
         prefix, tokens_in, norm_gains, cos, sin, w_attn, [target_t, router_rows]
     )
 
@@ -1424,8 +1425,8 @@
     )
 
     grad_w, grad_normed = attend_backward(
-        prefix, query, key, value, heads, totals, cos, sin, normed_t, grad_attn_low, grad_attn_t,
-        w_attn,
+        prefix, query, key, value, heads, rest, totals, cos, sin, normed_t, grad_attn_low,
+        grad_attn_t, w_attn,
     )
     quarters = exchange(packs, "expert")
     attn_sum = scatter_rows(
@@ -1476,13 +1477,16 @@
     router_new, router_first_new, router_second_new = adam_update(
         router, router_first, router_second, router_grad, RATE_ROUTER, WEIGHT_DECAY
     )
-    quarter, attn_sum = wait_all([quarter, attn_sum], gains_new, tokens_grad, expert_new)
+    owned_count = jnp.sum((owners == lax.axis_index("expert")).astype(jnp.int32))
+    slot_held = (jnp.arange(own_count, dtype=jnp.int32) < owned_count).astype(jnp.int32)
+    quarter, attn_sum, slot_held = wait_all(
+        [quarter, attn_sum, slot_held], gains_new, tokens_grad, expert_new
+    )
     shared_low = scatter_rows(quarter, "ring")
     slot_grads = split_columns(attn_sum, slot_of, owner_count, own_count)
     owned_grad = sum(part.astype(WIDE) for part in exchange(slot_grads, "expert"))
 
-    owned_count = jnp.sum((owners == lax.axis_index("expert")).astype(jnp.int32))
-    slot_used = (jnp.arange(own_count, dtype=jnp.int32) < owned_count)[:, None, None]
+    slot_used = (slot_held > 0)[:, None, None]
     attn_w, attn_m, attn_n = adam_update(
         attn_master, attn_first, attn_second, owned_grad, RATE_ATTENTION, WEIGHT_DECAY
     )

time: 493 us -> 492 us (level)
    unnamed x79 -> x81, local copies, waits for them, and re-layouts: 9.97 us -> 9.55 us
where the time goes in v2:
time: 492 us; the launch traced here: 487 us
  Pallas kernels  261 us (53%)
  waiting for transfers between devices  126 us (26%)
  starting transfers between devices  38.4 us (8%)
  other arithmetic  25.2 us (5%)
  local copies, waits for them, and re-layouts  20.1 us (4%)
  between operations  15.9 us (3%)
    ppermute x40, waiting for transfers between devices, to_partner(): lax.ppermute(value, axis, [(index, index ^ distance) for index in range(s...  57.5 us
    pallas_call x2, Pallas kernels, expert_pass(): pl.pallas_call(ignoring(functools.partial(expert_kernel, sources), source...  57.2 us
    all_gather x3, waiting for transfers between devices, gather_rows(): return lax.all_gather(part, axes, axis=0, tiled=True)  49.3 us
    pallas_call x1, Pallas kernels, attend_backward(): pl.pallas_call(attend_backward_kernel, grid=(GROUPS,), out_shape=[jax.Sha...  42.8 us
    pallas_call x1, Pallas kernels, swiglu_stacks(): pl.pallas_call(ignoring(kernel, 5 + 4 * partners, len(after)), grid=(2 *...  42.4 us
    ppermute x40, starting transfers between devices, to_partner(): lax.ppermute(value, axis, [(index, index ^ distance) for index in range(s...  37.9 us
    pallas_call x2, Pallas kernels, weight_grad(): pl.pallas_call(ignoring(functools.partial(weight_grad_kernel, halves, tur...  29.1 us
    pallas_call x1, Pallas kernels, attend_forward(): pl.pallas_call(ignoring(attend_forward_kernel, 6, len(after)), grid=(GROU...  27 us
  transfers between devices with their start and end apart: 47, of which 17 were waited for; matrix products, arithmetic and copies ran while one was open for 6% of the time, Pallas kernels for 50%

profile of v2, /device:TPU:9, one launch (start us, length us, event | category | flops | bytes accessed | tf_op | source)
XLA Modules:
  0.0 486.9 jit_solution(13275673255208976683)
XLA Ops:
  12.1 2.2 collective-permute-start.2
  15.7 5.6 %collective-permute-done.2 = bf16[24,48,128]{2,1,0:T(8,128)(2,1)S(1)} collective-permute-done((bf16[24,48,128]{2,1,0:T(8,128)(2,1)S(1)}, bf16[24,48,128]{2,1,0:T(8,128)(2,1)S(1)}, u32[]{:S(2)}, u32[]{:S(2)}) %collective-permute-start.2) | collective-permute-done | bytes 294944 | tf_op jit(solution)/shard_map/ppermute | solution.py:1191
  21.3 7.1 %collective-permute-done.1 = bf16[24,48,128]{2,1,0:T(8,128)(2,1)S(1)} collective-permute-done((bf16[24,48,128]{2,1,0:T(8,128)(2,1)S(1)}, bf16[24,48,128]{2,1,0:T(8,128)(2,1)S(1)}, u32[]{:S(2)}, u32[]{:S(2)}) %collective-permute-start.1) | collective-permute-done | bytes 294944 | tf_op jit(solution)/shard_map/ppermute | solution.py:1191
  29.5 2.9 shard_map.331
  38.4 1.3 reduce-window.6
  43.4 1.3 collective-permute-start.6
  46.1 49.3 %all-gather.5.cloned.1.call-done.refs_5_.w_ref = bf16[768,3072]{1,0:T(8,128)(2,1)} async-done(((bf16[96,3072]{1,0:T(8,128)(2,1)}), bf16[768,3072]{1,0:T(8,128)(2,1)}) %all-gather.5.cloned.1.call-update) | async-done | bytes 4718608 | tf_op jit(solution)/shard_map/all_gather | solution.py:1214
  95.4 27.0 %shard_map.332 = (bf16[1024,768]{1,0:T(8,128)(2,1)}, bf16[1024,768]{1,0:T(8,128)(2,1)}, bf16[1024,768]{1,0:T(8,128)(2,1)}, bf16[1024,768]{1,0:T(8,128)(2,1)}, bf...) custom-call(s32[1]{0:T(128)S(6)} %copy.128.refs_0_.prefix_ref, ...), custom_call_target="tpu_custom_call" | custom-call | flops 24999999488 | bytes 20000000 | tf_op jit(solution)/shard_map/pallas_call | solution.py:240
  125.4 14.3 %shard_map.333 = (bf16[2,256,768]{2,1,0:T(8,128)(2,1)}, bf16[2,256,768]{2,1,0:T(8,128)(2,1)}, bf16[2,256,768]{2,1,0:T(8,128)(2,1)}, bf16[2,256,768]{2,1,0:T(8,12...) custom-call(s32[1]{0:T(128)} %bitcast.here_ref.refs_0_, ...), custom_call_target="tpu_custom_call" | custom-call | flops 6442450944 | bytes 9437184 | tf_op jit(solution)/shard_map/pallas_call | solution.py:607
  139.8 1.3 collective-permute-start.11
  141.0 1.2 collective-permute-start.12
  142.5 1.2 collective-permute-start.17
  143.7 1.2 collective-permute-start.18
  144.9 42.4 %shard_map.335 = (f32[1024,768]{1,0:T(8,128)}, f32[1024,768]{1,0:T(8,128)}, bf16[768,2048]{1,0:T(8,128)(2,1)}, bf16[1024,768]{1,0:T(8,128)(2,1)}, bf16[768,2048]{1,0:T(8,128)(2,1)}, /*index=5*/bf16[1024,768]{1,0:T(8,128)(2,1)}) custom-call(s32[1]{0:T(128)} %bitcast.here_ref.refs_0_, bf16[1024,768]{1,0:T(8,128)(2,1)} %get-tuple-element.104.branch_ref.refs_1_.refs_7_, ...), custom_call_target="tpu_custom_call" | custom-call | flops 28991029248 | bytes 28311552 | tf_op jit(solution)/shard_map/pallas_call | solution.py:981
  188.7 28.5 %shard_map.336 = (bf16[2,256,768]{2,1,0:T(8,128)(2,1)}, bf16[2,256,768]{2,1,0:T(8,128)(2,1)}, bf16[2,256,768]{2,1,0:T(8,128)(2,1)}, bf16[2,256,768]{2,1,0:T(8,12...) custom-call(bf16[2,256,768]{2,1,0:T(8,128)(2,1)} %get-tuple-element.115.refs_0_, ...), custom_call_target="tpu_custom_call" | custom-call | flops 1610612736 | bytes 1572864 | tf_op jit(solution)/shard_map/pallas_call | solution.py:700
  220.7 28.8 %shard_map.337 = (bf16[2,256,768]{2,1,0:T(8,128)(2,1)}, bf16[2,256,768]{2,1,0:T(8,128)(2,1)}, bf16[2,256,768]{2,1,0:T(8,128)(2,1)}, bf16[2,256,768]{2,1,0:T(8,12...) custom-call(bf16[2,256,768]{2,1,0:T(8,128)(2,1)} %get-tuple-element.123.refs_0_, ...), custom_call_target="tpu_custom_call" | custom-call | flops 1610612736 | bytes 1572864 | tf_op jit(solution)/shard_map/pallas_call | solution.py:700
  249.5 2.8 collective-permute-done.16.refs_6_.refs_14_
  253.2 11.0 %shard_map.338.refs_4_ = bf16[2048,768]{1,0:T(8,128)(2,1)} custom-call(bf16[2,2,768,512]{3,2,1,0:T(8,128)(2,1)} %get-tuple-element.132.refs_0_, bf16[2,2,768,512]{3,2,1,0:T(8,128)(2,1)} %get-tuple-element.133.refs_1_, bf16[1024,2048]{1,0:T(8,128)(2,1)} %get-tuple-element.127.refs_6_.refs_2_, bf16[1024,2048]{1,0:T(8,128)(2,1)} %get-tuple-element.136.refs_3_, ...), custom_call_target="tpu_custom_call" | custom-call | flops 201326592 | bytes 786432 | tf_op jit(solution)/shard_map/pallas_call | solution.py:762
  264.3 3.4 collective-permute-start.23
  270.4 5.3 %collective-permute-done.24.refs_3_ = bf16[1024,768]{1,0:T(8,128)(2,1)S(1)} collective-permute-done((bf16[1024,768]{1,0:T(8,128)(2,1)}, bf16[1024,768]{1,0:T(8,128)(2,1)S(1)}, u32[]{:S(2)}, u32[]{:S(2)}) %collective-permute-start.24) | collective-permute-done | bytes 1572896 | tf_op jit(solution)/shard_map/ppermute | solution.py:1191
  276.9 1.6 copy-done.6
  278.5 6.9 %shard_map.340 = (bf16[4,576,256]{2,1,0:T(8,128)(2,1)}, bf16[4,576,256]{2,1,0:T(8,128)(2,1)}, bf16[4,576,256]{2,1,0:T(8,128)(2,1)}, bf16[4,576,256]{2,1,0:T(8,128)(2,1)}) custom-call(s32[1]{0:T(128)} %bitcast.here_ref.refs_0_, bf16[768,2048]{1,0:T(8,128)(2,1)} %get-tuple-element.137.refs_0_, bf16[768,2048]{1,0:T(8,128)(2,1)} %copy-done.6, ...), custom_call_target="tpu_custom_call" | custom-call | bytes 20000000 | tf_op jit(solution)/shard_map/pallas_call | solution.py:1041
  285.4 18.2 %shard_map.339.refs_4_.refs_19_ = bf16[768,4096]{1,0:T(8,128)(2,1)} custom-call(bf16[2,2,768,512]{3,2,1,0:T(8,128)(2,1)} %get-tuple-element.132.refs_0_, bf16[2,2,768,512]{3,2,1,0:T(8,128)(2,1)} %get-tuple-element.133.refs_1_, bf16[1024,4096]{1,0:T(8,128)(2,1)} %get-tuple-element.134.refs_2_, bf16[1024,4096]{1,0:T(8,128)(2,1)} %get-tuple-element.135.refs_3_, ...), custom_call_target="tpu_custom_call" | custom-call | flops 402653184 | bytes 1572864 | tf_op jit(solution)/shard_map/pallas_call | solution.py:762
  305.7 1.5 collective-permute-start.27
  307.2 21.8 %shard_map.342 = (bf16[1024,768]{1,0:T(8,128)(2,1)}, f32[1024,768]{1,0:T(8,128)}, bf16[1024,768]{1,0:T(8,128)(2,1)}, bf16[4,768,256]{2,1,0:T(8,128)(2,1)}, bf16[...) custom-call(s32[1]{0:T(128)} %bitcast.here_ref.refs_0_, s32[1024,2]{1,0:T(8,128)} %copy-done.4, ...), custom_call_target="tpu_custom_call" | custom-call | flops 399999991808 | bytes 25000000 | tf_op jit(solution)/shard_map/pallas_call | solution.py:850
  329.0 42.8 %shard_map.343 = (bf16[768,3072]{1,0:T(8,128)(2,1)}, f32[1024,768]{1,0:T(8,128)}) custom-call(s32[1]{0:T(128)S(6)} %copy.128.refs_0_.prefix_ref, bf16[1024,768]{1,0:T(8,128)(2,1)} %get-tuple-element.148.query_ref, bf16[1024,768]{1,0:T(8,128)(2,1)} %get-tuple-element.149.key_ref, bf16[1024,768]{1,0:T(8,128)(2,1)} %get-tuple-element.150.value_ref, ...), custom_call_target="tpu_custom_call" | custom-call | tf_op jit(solution)/shard_map/pallas_call | solution.py:376
  371.8 4.4 reduce-scatter.5.cloned.1.call-done.refs_1_.gu_ref
  378.1 2.9 fusion.7
  381.8 1.2 collective-permute-start.29
  383.0 1.6 collective-permute-done.29
  384.6 1.4 collective-permute-start.30
  388.9 2.4 collective-permute-done.31
  391.4 1.3 collective-permute-start.32
  392.6 3.0 collective-permute-done.32
  395.6 4.5 collective-permute-start.33
  400.2 2.7 add_convert_fusion
  404.2 2.5 fusion.6.refs_4_
  408.6 9.1 %shard_map.345 = (f32[3,1536,128]{2,1,0:T(8,128)}, f32[3,1536,128]{2,1,0:T(8,128)}, f32[3,1536,128]{2,1,0:T(8,128)}) custom-call(bf16[96,4096]{1,0:T(8,128)(2,1)} %reduce-scatter.5.cloned.1.call-done.refs_1_.gu_ref, bf16[256,768]{1,0:T(8,128)(2,1)} %reduce-scatter.7.cloned.1.call-done.refs_2_.down_ref, f32[3,1536,128]{2,1,0:T(8,128)} %bitcast.137, ...), custom_call_target="tpu_custom_call" | custom-call | tf_op jit(solution)/shard_map/pallas_call | solution.py:1141
  417.6 15.1 %reduce-scatter.9.cloned.1.call-done.refs_1_ = bf16[96,3072]{1,0:T(8,128)(2,1)} async-done(((bf16[768,3072]{1,0:T(8,128)(2,1)}), bf16[96,3072]{1,0:T(8,128)(2,1)}) %reduce-scatter.9.cloned.1.call-update) | async-done | bytes 589840 | tf_op jit(solution)/shard_map/reduce_scatter | solution.py:1218
  432.8 2.9 shard_map.347
  435.8 1.2 collective-permute-start.34
  438.4 6.6 %collective-permute-done.34 = bf16[24,48,128]{2,1,0:T(8,128)(2,1)S(1)} collective-permute-done((bf16[24,48,128]{2,1,0:T(8,128)(2,1)}, bf16[24,48,128]{2,1,0:T(8,128)(2,1)S(1)}, u32[]{:S(2)}, u32[]{:S(2)}) %collective-permute-start.34) | collective-permute-done | bytes 294944 | tf_op jit(solution)/shard_map/ppermute | solution.py:1191
  445.0 7.4 %collective-permute-done.35 = bf16[24,48,128]{2,1,0:T(8,128)(2,1)S(1)} collective-permute-done((bf16[24,48,128]{2,1,0:T(8,128)(2,1)}, bf16[24,48,128]{2,1,0:T(8,128)(2,1)S(1)}, u32[]{:S(2)}, u32[]{:S(2)}) %collective-permute-start.35) | collective-permute-done | bytes 294944 | tf_op jit(solution)/shard_map/ppermute | solution.py:1191
  452.5 2.7 fusion.27
  458.6 5.8 %collective-permute-done.39 = bf16[24,48,128]{2,1,0:T(8,128)(2,1)S(1)} collective-permute-done((bf16[24,48,128]{2,1,0:T(8,128)(2,1)S(1)}, bf16[24,48,128]{2,1,0:T(8,128)(2,1)S(1)}, u32[]{:S(2)}, u32[]{:S(2)}) %collective-permute-start.39) | collective-permute-done | bytes 294944 | tf_op jit(solution)/shard_map/ppermute | solution.py:1191
  464.4 7.0 %collective-permute-done.38 = bf16[24,48,128]{2,1,0:T(8,128)(2,1)S(1)} collective-permute-done((bf16[24,48,128]{2,1,0:T(8,128)(2,1)S(1)}, bf16[24,48,128]{2,1,0:T(8,128)(2,1)S(1)}, u32[]{:S(2)}, u32[]{:S(2)}) %collective-permute-start.38) | collective-permute-done | bytes 294944 | tf_op jit(solution)/shard_map/ppermute | solution.py:1191
  472.6 4.4 shard_map.348
  477.0 1.9 gather_fusion
  (246 shorter events, 48.0 us)
Async XLA Ops:
  7.2 36.2 %all-gather.7.cloned.1.call-start = ((), (), s32[]{:S(2)}) async-start(), calls=%async_computation.5 | async-start | bytes 1474560 | tf_op jit(solution)/shard_map/all_gather | solution.py:1214
  9.4 1.7 collective-permute-start.3
  11.9 83.4 %all-gather.5.cloned.1.call-start = ((), (), s32[]{:S(2)}) async-start(), calls=%async_computation.4 | async-start | bytes 5308416 | tf_op jit(solution)/shard_map/all_gather | solution.py:1214
  12.1 9.2 %collective-permute-start.2 = (bf16[24,48,128]{2,1,0:T(8,128)(2,1)S(1)}, bf16[24,48,128]{2,1,0:T(8,128)(2,1)S(1)}, u32[]{:S(2)}, u32[]{:S(2)}) collective-permute-start(bf16[24,48,128]{2,1,0:T(8,128)(2,1)S(1)} %convert_element_type.88), channel_id=1, source_target_pairs={{0,24},{8,16},{16,8},{24,0},{1,25},{9,17},{17,9},{25,1},{2,26},{10... | collective-permute-start | bytes 884744 | tf_op jit(solution)/shard_map/ppermute | solution.py:1191
  14.3 14.1 %collective-permute-start.1 = (bf16[24,48,128]{2,1,0:T(8,128)(2,1)S(1)}, bf16[24,48,128]{2,1,0:T(8,128)(2,1)S(1)}, u32[]{:S(2)}, u32[]{:S(2)}) collective-permute-start(bf16[24,48,128]{2,1,0:T(8,128)(2,1)S(1)} %convert_element_type.88), channel_id=1, source_target_pairs={{0,16},{8,24},{16,0},{24,8},{1,17},{9,25},{17,1},{25,9},{2,18},{10... | collective-permute-start | bytes 884744 | tf_op jit(solution)/shard_map/ppermute | solution.py:1191
  14.5 13.9 %collective-permute-start = (bf16[24,48,128]{2,1,0:T(8,128)(2,1)S(1)}, bf16[24,48,128]{2,1,0:T(8,128)(2,1)S(1)}, u32[]{:S(2)}, u32[]{:S(2)}) collective-permute-start(bf16[24,48,128]{2,1,0:T(8,128)(2,1)S(1)} %convert_element_type.88), channel_id=1, source_target_pairs={{0,8},{8,0},{16,24},{24,16},{1,9},{9,1},{17,25},{25,17},{2,10},{10... | collective-permute-start | bytes 884744 | tf_op jit(solution)/shard_map/ppermute | solution.py:1191
  32.4 155.3 %all-gather.9.cloned.1.call-start = ((), (), s32[]{:S(2)}) async-start(), calls=%async_computation.10 | async-start | bytes 10616832 | tf_op jit(solution)/shard_map/all_gather | solution.py:1214
  35.1 336.8 %reduce-scatter.7.cloned.1.call-start = ((), (), s32[]{:S(2)}) async-start(), calls=%async_computation.7 | async-start | bytes 3538944 | tf_op jit(solution)/shard_map/reduce_scatter | solution.py:1218
  40.9 81.5 %copy-start.9 = (s32[1024,2]{1,0:T(8,128)}, s32[1024,2]{1,0:T(8,128)S(1)}, u32[]{:S(2)}) copy-start(s32[1024,2]{1,0:T(8,128)S(1)} %add_select_fusion.refs_2_) | copy-start | bytes 24580
  43.4 78.9 %collective-permute-start.6 = (bf16[2304,256]{1,0:T(8,128)(2,1)}, bf16[2304,256]{1,0:T(8,128)(2,1)S(1)}, u32[]{:S(2)}, u32[]{:S(2)}) collective-permute-start(bf16[2304,256]{1,0:T(8,128)(2,1)} %all-gather.7.cloned.1.call-done.refs_0_), channel_id=1, source_target_pairs={{0,24},{8,16},{16,8},{24,0},{1,25},{9,17},{17,9},{25,1},{2,26},{10... | collective-permute-start | bytes 3538952 | tf_op jit(solution)/shard_map/ppermute | solution.py:1191
  44.8 77.6 %collective-permute-start.5 = (bf16[2304,256]{1,0:T(8,128)(2,1)}, bf16[2304,256]{1,0:T(8,128)(2,1)S(1)}, u32[]{:S(2)}, u32[]{:S(2)}) collective-permute-start(bf16[2304,256]{1,0:T(8,128)(2,1)} %all-gather.7.cloned.1.call-done.refs_0_), channel_id=1, source_target_pairs={{0,16},{8,24},{16,0},{24,8},{1,17},{9,25},{17,1},{25,9},{2,18},{10... | collective-permute-start | bytes 3538952 | tf_op jit(solution)/shard_map/ppermute | solution.py:1191
  45.8 76.6 %collective-permute-start.4 = (bf16[2304,256]{1,0:T(8,128)(2,1)}, bf16[2304,256]{1,0:T(8,128)(2,1)}, u32[]{:S(2)}, u32[]{:S(2)}) collective-permute-start(bf16[2304,256]{1,0:T(8,128)(2,1)} %all-gather.7.cloned.1.call-done.refs_0_), channel_id=1, source_target_pairs={{0,8},{8,0},{16,24},{24,16},{1,9},{9,1},{17,25},{25,17},{2,10},{10... | collective-permute-start | bytes 3538952 | tf_op jit(solution)/shard_map/ppermute | solution.py:1191
  123.8 17.3 %collective-permute-start.7 = (bf16[2304,256]{1,0:T(8,128)(2,1)}, bf16[2304,256]{1,0:T(8,128)(2,1)S(1)}, u32[]{:S(2)}, u32[]{:S(2)}) collective-permute-start(bf16[2304,256]{1,0:T(8,128)(2,1)} %get-tuple-element.108), channel_id=1, source_target_pairs={{0,1},{1,0},{2,3},{3,2},{4,5},{5,4},{6,7},{7,6},{8,9},{9,8},{10,11... | collective-permute-start | bytes 3538952 | tf_op jit(solution)/shard_map/ppermute | solution.py:1191
  124.0 18.2 %collective-permute-start.8 = (bf16[2304,256]{1,0:T(8,128)(2,1)}, bf16[2304,256]{1,0:T(8,128)(2,1)}, u32[]{:S(2)}, u32[]{:S(2)}) collective-permute-start(bf16[2304,256]{1,0:T(8,128)(2,1)} %get-tuple-element.109), channel_id=1, source_target_pairs={{0,1},{1,0},{2,3},{3,2},{4,5},{5,4},{6,7},{7,6},{8,9},{9,8},{10,11... | collective-permute-start | bytes 3538952 | tf_op jit(solution)/shard_map/ppermute | solution.py:1191
  124.3 18.2 %collective-permute-start.9 = (bf16[2304,256]{1,0:T(8,128)(2,1)}, bf16[2304,256]{1,0:T(8,128)(2,1)}, u32[]{:S(2)}, u32[]{:S(2)}) collective-permute-start(bf16[2304,256]{1,0:T(8,128)(2,1)} %get-tuple-element.110), channel_id=1, source_target_pairs={{0,1},{1,0},{2,3},{3,2},{4,5},{5,4},{6,7},{7,6},{8,9},{9,8},{10,11... | collective-permute-start | bytes 3538952 | tf_op jit(solution)/shard_map/ppermute | solution.py:1191
  124.5 19.1 %collective-permute-start.10 = (bf16[2304,256]{1,0:T(8,128)(2,1)}, bf16[2304,256]{1,0:T(8,128)(2,1)}, u32[]{:S(2)}, u32[]{:S(2)}) collective-permute-start(bf16[2304,256]{1,0:T(8,128)(2,1)} %get-tuple-element.111), channel_id=1, source_target_pairs={{0,1},{1,0},{2,3},{3,2},{4,5},{5,4},{6,7},{7,6},{8,9},{9,8},{10,11... | collective-permute-start | bytes 3538952 | tf_op jit(solution)/shard_map/ppermute | solution.py:1191
  139.8 47.5 %collective-permute-start.11 = (bf16[2,256,768]{2,1,0:T(8,128)(2,1)}, bf16[2,256,768]{2,1,0:T(8,128)(2,1)S(1)}, u32[]{:S(2)}, u32[]{:S(2)}) collective-permute-start(bf16[2,256,768]{2,1,0:T(8,128)(2,1)} %get-tuple-element.116), channel_id=1, source_target_pairs={{0,8},{8,0},{16,24},{24,16},{1,9},{9,1},{17,25},{25,17},{2,10},{10... | collective-permute-start | bytes 2359304 | tf_op jit(solution)/shard_map/ppermute | solution.py:1191
  141.0 46.7 %collective-permute-start.12 = (bf16[2,256,768]{2,1,0:T(8,128)(2,1)}, bf16[2,256,768]{2,1,0:T(8,128)(2,1)S(1)}, u32[]{:S(2)}, u32[]{:S(2)}) collective-permute-start(bf16[2,256,768]{2,1,0:T(8,128)(2,1)} %get-tuple-element.117), channel_id=1, source_target_pairs={{0,16},{8,24},{16,0},{24,8},{1,17},{9,25},{17,1},{25,9},{2,18},{10... | collective-permute-start | bytes 2359304 | tf_op jit(solution)/shard_map/ppermute | solution.py:1191
  142.2 45.5 %collective-permute-start.13 = (bf16[2,256,768]{2,1,0:T(8,128)(2,1)}, bf16[2,256,768]{2,1,0:T(8,128)(2,1)}, u32[]{:S(2)}, u32[]{:S(2)}) collective-permute-start(bf16[2,256,768]{2,1,0:T(8,128)(2,1)} %get-tuple-element.118), channel_id=1, source_target_pairs={{0,24},{8,16},{16,8},{24,0},{1,25},{9,17},{17,9},{25,1},{2,26},{10... | collective-permute-start | bytes 2359304 | tf_op jit(solution)/shard_map/ppermute | solution.py:1191
  142.5 77.0 %collective-permute-start.17 = (bf16[2,256,768]{2,1,0:T(8,128)(2,1)}, bf16[2,256,768]{2,1,0:T(8,128)(2,1)S(1)}, u32[]{:S(2)}, u32[]{:S(2)}) collective-permute-start(bf16[2,256,768]{2,1,0:T(8,128)(2,1)} %get-tuple-element.124), channel_id=1, source_target_pairs={{0,8},{8,0},{16,24},{24,16},{1,9},{9,1},{17,25},{25,17},{2,10},{10... | collective-permute-start | bytes 2359304 | tf_op jit(solution)/shard_map/ppermute | solution.py:1191
  143.7 76.1 %collective-permute-start.18 = (bf16[2,256,768]{2,1,0:T(8,128)(2,1)}, bf16[2,256,768]{2,1,0:T(8,128)(2,1)S(1)}, u32[]{:S(2)}, u32[]{:S(2)}) collective-permute-start(bf16[2,256,768]{2,1,0:T(8,128)(2,1)} %get-tuple-element.125), channel_id=1, source_target_pairs={{0,16},{8,24},{16,0},{24,8},{1,17},{9,25},{17,1},{25,9},{2,18},{10... | collective-permute-start | bytes 2359304 | tf_op jit(solution)/shard_map/ppermute | solution.py:1191
  187.3 32.5 %collective-permute-start.19 = (bf16[2,256,768]{2,1,0:T(8,128)(2,1)}, bf16[2,256,768]{2,1,0:T(8,128)(2,1)}, u32[]{:S(2)}, u32[]{:S(2)}) collective-permute-start(bf16[2,256,768]{2,1,0:T(8,128)(2,1)} %get-tuple-element.126), channel_id=1, source_target_pairs={{0,24},{8,16},{16,8},{24,0},{1,25},{9,17},{17,9},{25,1},{2,26},{10... | collective-permute-start | bytes 2359304 | tf_op jit(solution)/shard_map/ppermute | solution.py:1191
  217.1 32.4 %collective-permute-start.14 = (bf16[2,256,768]{2,1,0:T(8,128)(2,1)}, bf16[2,256,768]{2,1,0:T(8,128)(2,1)S(1)}, u32[]{:S(2)}, u32[]{:S(2)}) collective-permute-start(bf16[2,256,768]{2,1,0:T(8,128)(2,1)} %get-tuple-element.120), channel_id=1, source_target_pairs={{0,8},{8,0},{16,24},{24,16},{1,9},{9,1},{17,25},{25,17},{2,10},{10... | collective-permute-start | bytes 2359304 | tf_op jit(solution)/shard_map/ppermute | solution.py:1191
  218.3 31.2 %collective-permute-start.15 = (bf16[2,256,768]{2,1,0:T(8,128)(2,1)}, bf16[2,256,768]{2,1,0:T(8,128)(2,1)S(1)}, u32[]{:S(2)}, u32[]{:S(2)}) collective-permute-start(bf16[2,256,768]{2,1,0:T(8,128)(2,1)} %get-tuple-element.121), channel_id=1, source_target_pairs={{0,16},{8,24},{16,0},{24,8},{1,17},{9,25},{17,1},{25,9},{2,18},{10... | collective-permute-start | bytes 2359304 | tf_op jit(solution)/shard_map/ppermute | solution.py:1191
  219.4 32.9 %collective-permute-start.16 = (bf16[2,256,768]{2,1,0:T(8,128)(2,1)}, bf16[2,256,768]{2,1,0:T(8,128)(2,1)S(1)}, u32[]{:S(2)}, u32[]{:S(2)}) collective-permute-start(bf16[2,256,768]{2,1,0:T(8,128)(2,1)} %get-tuple-element.122), channel_id=1, source_target_pairs={{0,24},{8,16},{16,8},{24,0},{1,25},{9,17},{17,9},{25,1},{2,26},{10... | collective-permute-start | bytes 2359304 | tf_op jit(solution)/shard_map/ppermute | solution.py:1191
  264.2 112.0 %reduce-scatter.5.cloned.1.call-start = ((), (), s32[]{:S(2)}) async-start(), calls=%async_computation.6 | async-start | bytes 7077888 | tf_op jit(solution)/shard_map/reduce_scatter | solution.py:1218
  264.3 11.4 %collective-permute-start.23 = (bf16[768,2048]{1,0:T(8,128)(2,1)}, bf16[768,2048]{1,0:T(8,128)(2,1)S(1)}, u32[]{:S(2)}, u32[]{:S(2)}) collective-permute-start(bf16[768,2048]{1,0:T(8,128)(2,1)} %get-tuple-element.138), channel_id=1, source_target_pairs={{0,1},{1,0},{2,3},{3,2},{4,5},{5,4},{6,7},{7,6},{8,9},{9,8},{10,11... | collective-permute-start | bytes 9437192 | tf_op jit(solution)/shard_map/ppermute | solution.py:1191
  267.7 8.0 %collective-permute-start.24 = (bf16[1024,768]{1,0:T(8,128)(2,1)}, bf16[1024,768]{1,0:T(8,128)(2,1)S(1)}, u32[]{:S(2)}, u32[]{:S(2)}) collective-permute-start(bf16[1024,768]{1,0:T(8,128)(2,1)} %get-tuple-element.140), channel_id=1, source_target_pairs={{0,1},{1,0},{2,3},{3,2},{4,5},{5,4},{6,7},{7,6},{8,9},{9,8},{10,11... | collective-permute-start | bytes 4718600 | tf_op jit(solution)/shard_map/ppermute | solution.py:1191
  267.8 35.8 %collective-permute-start.20 = (bf16[2,256,768]{2,1,0:T(8,128)(2,1)}, bf16[2,256,768]{2,1,0:T(8,128)(2,1)S(1)}, u32[]{:S(2)}, u32[]{:S(2)}) collective-permute-start(bf16[2,256,768]{2,1,0:T(8,128)(2,1)} %get-tuple-element.129), channel_id=1, source_target_pairs={{0,8},{8,0},{16,24},{24,16},{1,9},{9,1},{17,25},{25,17},{2,10},{10... | collective-permute-start | bytes 2359304 | tf_op jit(solution)/shard_map/ppermute | solution.py:1191
  268.3 35.4 %collective-permute-start.21 = (bf16[2,256,768]{2,1,0:T(8,128)(2,1)}, bf16[2,256,768]{2,1,0:T(8,128)(2,1)}, u32[]{:S(2)}, u32[]{:S(2)}) collective-permute-start(bf16[2,256,768]{2,1,0:T(8,128)(2,1)} %get-tuple-element.130), channel_id=1, source_target_pairs={{0,16},{8,24},{16,0},{24,8},{1,17},{9,25},{17,1},{25,9},{2,18},{10... | collective-permute-start | bytes 2359304 | tf_op jit(solution)/shard_map/ppermute | solution.py:1191
  269.3 35.2 %collective-permute-start.22 = (bf16[2,256,768]{2,1,0:T(8,128)(2,1)}, bf16[2,256,768]{2,1,0:T(8,128)(2,1)}, u32[]{:S(2)}, u32[]{:S(2)}) collective-permute-start(bf16[2,256,768]{2,1,0:T(8,128)(2,1)} %get-tuple-element.131), channel_id=1, source_target_pairs={{0,24},{8,16},{16,8},{24,0},{1,25},{9,17},{17,9},{25,1},{2,26},{10... | collective-permute-start | bytes 2359304 | tf_op jit(solution)/shard_map/ppermute | solution.py:1191
  303.6 129.2 %reduce-scatter.9.cloned.1.call-start = ((), (), s32[]{:S(2)}) async-start(), calls=%async_computation.8 | async-start | bytes 5308416 | tf_op jit(solution)/shard_map/reduce_scatter | solution.py:1218
  304.5 67.3 %collective-permute-start.25 = (bf16[2304,256]{1,0:T(8,128)(2,1)}, bf16[2304,256]{1,0:T(8,128)(2,1)}, u32[]{:S(2)}, u32[]{:S(2)}) collective-permute-start(bf16[2304,256]{1,0:T(8,128)(2,1)} %get-tuple-element.157), channel_id=1, source_target_pairs={{0,8},{8,0},{16,24},{24,16},{1,9},{9,1},{17,25},{25,17},{2,10},{10... | collective-permute-start | bytes 3538952 | tf_op jit(solution)/shard_map/ppermute | solution.py:1191
  304.9 66.9 %collective-permute-start.26 = (bf16[2304,256]{1,0:T(8,128)(2,1)}, bf16[2304,256]{1,0:T(8,128)(2,1)}, u32[]{:S(2)}, u32[]{:S(2)}) collective-permute-start(bf16[2304,256]{1,0:T(8,128)(2,1)} %get-tuple-element.158), channel_id=1, source_target_pairs={{0,16},{8,24},{16,0},{24,8},{1,17},{9,25},{17,1},{25,9},{2,18},{10... | collective-permute-start | bytes 3538952 | tf_op jit(solution)/shard_map/ppermute | solution.py:1191
  305.7 66.1 %collective-permute-start.27 = (bf16[2304,256]{1,0:T(8,128)(2,1)}, bf16[2304,256]{1,0:T(8,128)(2,1)}, u32[]{:S(2)}, u32[]{:S(2)}) collective-permute-start(bf16[2304,256]{1,0:T(8,128)(2,1)} %get-tuple-element.159), channel_id=1, source_target_pairs={{0,24},{8,16},{16,8},{24,0},{1,25},{9,17},{17,9},{25,1},{2,26},{10... | collective-permute-start | bytes 3538952 | tf_op jit(solution)/shard_map/ppermute | solution.py:1191
  376.3 96.3 %reduce-scatter.11.cloned.1.call-start = ((), (), s32[]{:S(2)}) async-start(), calls=%async_computation.9 | async-start | bytes 1474560 | tf_op jit(solution)/shard_map/reduce_scatter | solution.py:1218
  381.8 2.8 collective-permute-start.29
  384.6 3.1 collective-permute-start.30
  387.8 3.6 collective-permute-start.31
  391.4 4.3 collective-permute-start.32
  395.6 11.1 %collective-permute-start.33 = (f32[6,768]{1,0:T(8,128)S(1)}, f32[6,768]{1,0:T(8,128)S(1)}, u32[]{:S(2)}, u32[]{:S(2)}) collective-permute-start(f32[6,768]{1,0:T(8,128)S(1)} %add.142), channel_id=1, source_target_pairs={{0,1},{1,0},{2,3},{3,2},{4,5},{5,4},{6,7},{7,6},{8,9},{9,8},{10,11... | collective-permute-start | bytes 55304 | tf_op jit(solution)/shard_map/ppermute | solution.py:1191
  403.0 4.3 collective-permute-start.28
  435.8 9.3 %collective-permute-start.34 = (bf16[24,48,128]{2,1,0:T(8,128)(2,1)}, bf16[24,48,128]{2,1,0:T(8,128)(2,1)S(1)}, u32[]{:S(2)}, u32[]{:S(2)}) collective-permute-start(bf16[24,48,128]{2,1,0:T(8,128)(2,1)} %get-tuple-element.167), channel_id=1, source_target_pairs={{0,8},{8,0},{16,24},{24,16},{1,9},{9,1},{17,25},{25,17},{2,10},{10... | collective-permute-start | bytes 884744 | tf_op jit(solution)/shard_map/ppermute | solution.py:1191
  437.0 15.5 %collective-permute-start.35 = (bf16[24,48,128]{2,1,0:T(8,128)(2,1)}, bf16[24,48,128]{2,1,0:T(8,128)(2,1)S(1)}, u32[]{:S(2)}, u32[]{:S(2)}) collective-permute-start(bf16[24,48,128]{2,1,0:T(8,128)(2,1)} %get-tuple-element.168), channel_id=1, source_target_pairs={{0,16},{8,24},{16,0},{24,8},{1,17},{9,25},{17,1},{25,9},{2,18},{10... | collective-permute-start | bytes 884744 | tf_op jit(solution)/shard_map/ppermute | solution.py:1191
  438.1 14.3 %collective-permute-start.36 = (bf16[24,48,128]{2,1,0:T(8,128)(2,1)}, bf16[24,48,128]{2,1,0:T(8,128)(2,1)S(1)}, u32[]{:S(2)}, u32[]{:S(2)}) collective-permute-start(bf16[24,48,128]{2,1,0:T(8,128)(2,1)} %get-tuple-element.169), channel_id=1, source_target_pairs={{0,24},{8,16},{16,8},{24,0},{1,25},{9,17},{17,9},{25,1},{2,26},{10... | collective-permute-start | bytes 884744 | tf_op jit(solution)/shard_map/ppermute | solution.py:1191
  455.3 9.1 %collective-permute-start.39 = (bf16[24,48,128]{2,1,0:T(8,128)(2,1)S(1)}, bf16[24,48,128]{2,1,0:T(8,128)(2,1)S(1)}, u32[]{:S(2)}, u32[]{:S(2)}) collective-permute-start(bf16[24,48,128]{2,1,0:T(8,128)(2,1)S(1)} %get-tuple-element.183), channel_id=1, source_target_pairs={{0,24},{8,16},{16,8},{24,0},{1,25},{9,17},{17,9},{25,1},{2,26},{10... | collective-permute-start | bytes 884744 | tf_op jit(solution)/shard_map/ppermute | solution.py:1191
  456.5 15.0 %collective-permute-start.38 = (bf16[24,48,128]{2,1,0:T(8,128)(2,1)S(1)}, bf16[24,48,128]{2,1,0:T(8,128)(2,1)S(1)}, u32[]{:S(2)}, u32[]{:S(2)}) collective-permute-start(bf16[24,48,128]{2,1,0:T(8,128)(2,1)S(1)} %get-tuple-element.183), channel_id=1, source_target_pairs={{0,16},{8,24},{16,0},{24,8},{1,17},{9,25},{17,1},{25,9},{2,18},{10... | collective-permute-start | bytes 884744 | tf_op jit(solution)/shard_map/ppermute | solution.py:1191
  457.1 14.3 %collective-permute-start.37 = (bf16[24,48,128]{2,1,0:T(8,128)(2,1)S(1)}, bf16[24,48,128]{2,1,0:T(8,128)(2,1)S(1)}, u32[]{:S(2)}, u32[]{:S(2)}) collective-permute-start(bf16[24,48,128]{2,1,0:T(8,128)(2,1)S(1)} %get-tuple-element.183), channel_id=1, source_target_pairs={{0,8},{8,0},{16,24},{24,16},{1,9},{9,1},{17,25},{25,17},{2,10},{10... | collective-permute-start | bytes 884744 | tf_op jit(solution)/shard_map/ppermute | solution.py:1191
  (37 other events, 168.8 us)
Sparse Core Ops, SparseCore 0:
  12.1 30.5 all-gather.6
  44.9 50.4 all-gather.4
  97.0 88.2 all-gather.8
  264.4 40.4 reduce-scatter.6
  307.0 69.1 reduce-scatter.4
  378.4 54.3 reduce-scatter.8
  435.1 27.0 reduce-scatter.10
